TPU v7x, 32 devices: a whole 2x2x4 slice. The times are simulated.
32 devices in a mesh: pipe: 2 (over core), seq: 16 (over z, y, x).
Axes of the slice: x: 2, y: 2, z: 4, core: 2. Of those that a mesh axis runs over, the one named last changes fastest.
Arguments:
- inputs_saved: bfloat16 [2, 16384, 768], P('pipe', 'seq'), may hold values from -6 to 6
- grad_out: bfloat16 [16384, 768], P('seq'), may hold values from -6 to 6
- value_weight: bfloat16 [2, 768, 768], P('pipe', 'seq'), may hold values from -0.21875 to 0.21875
- gate_weight: bfloat16 [2, 768, 768], P('pipe', 'seq'), may hold values from -0.21875 to 0.21875
- out_weight: bfloat16 [2, 768, 768], P('pipe', 'seq'), may hold values from -0.21875 to 0.21875
- right_factor: bfloat16 [2, 1024, 1024], P('pipe', 'seq'), may hold values from -0.1875 to 0.1875
- left_factor: bfloat16 [2, 16, 16], P('pipe', 'seq'), may hold values from -1.5 to 1.5
- twiddle: float32 [2, 16, 1024], P('pipe', 'seq'), may hold values from -1.5 to 1.5
Outputs:
- input_grads: bfloat16 [2, 16384, 768], P('pipe', 'seq')
All inputs are finite; a program needn't handle non-finite values.
Results may differ from a plain program's by a relative error of at most 0.019.
Values may be sent and summed in bfloat16 or wider, within the bound.
No kernel may reach another device: no remote copies, remote signals or barrier semaphores. Data moves between devices by JAX's collectives and lax.ppermute only.
A program may use at most 128 MiB of HBM per device.

v0:
```python
import jax
import jax.numpy as jnp
from jax import lax
from jax.sharding import PartitionSpec as P


def passed_along(value, axis, steps):
    count = lax.axis_size(axis)
    initial, last = (max(0, -steps), min(count, count - steps))
    return lax.ppermute(value, axis, [(source, source + steps) for source in range(initial, last)])


def body(
    inputs_saved,
    grad_out,
    value_weight,
    gate_weight,
    out_weight,
    right_factor,
    left_factor,
    twiddle,
):
    segment_index = lax.axis_index("pipe")
    value_full, gate_full, out_full, right_full, left_full = (
        lax.all_gather(value_weight[0], "seq", axis=0, tiled=True),
        lax.all_gather(gate_weight[0], "seq", axis=0, tiled=True),
        lax.all_gather(out_weight[0], "seq", axis=0, tiled=True),
        lax.all_gather(right_factor[0], "seq", axis=0, tiled=True),
        lax.all_gather(left_factor[0], "seq", axis=0, tiled=True),
    )
    saved = inputs_saved[0]
    tokens_dev = saved.shape[0]
    width = saved.shape[1]
    order_right = right_full.shape[0]
    blocks_dev = tokens_dev // order_right
    blocks_all = left_full.shape[0]
    twiddle_own = twiddle[0]
    twiddle_whole = lax.all_gather(twiddle_own, "seq", axis=0, tiled=True)
    values = jnp.dot(saved, value_full, preferred_element_type=jnp.float32).astype(jnp.bfloat16)
    gates = jnp.dot(saved, gate_full, preferred_element_type=jnp.float32).astype(jnp.bfloat16)
    gates_wide = gates.astype(jnp.float32)
    sigma = jax.nn.sigmoid(gates_wide)
    active = gates_wide * sigma
    slope_values = sigma * (1.0 + gates_wide * (1.0 - sigma)) * values.astype(jnp.float32)

    def branch(incoming):
        mixed = jnp.dot(incoming, out_full.T, preferred_element_type=jnp.float32).astype(
            jnp.bfloat16
        )
        mixed = mixed.reshape(blocks_dev, order_right, width)
        spread = lax.all_to_all(mixed, "seq", split_axis=2, concat_axis=0, tiled=True)
        narrow = spread.shape[2]
        left_part = jnp.dot(
            left_full.T,
            spread.reshape(blocks_all, order_right * narrow),
            preferred_element_type=jnp.float32,
        )
        left_part = left_part.astype(jnp.bfloat16).reshape(blocks_all, order_right, narrow)
        turned = (left_part.astype(jnp.float32) * twiddle_whole[:, :, None]).astype(jnp.bfloat16)
        stacked = turned.transpose(1, 0, 2).reshape(order_right, blocks_all * narrow)
        right_part = jnp.dot(right_full.T, stacked, preferred_element_type=jnp.float32).astype(
            jnp.bfloat16
        )
        right_part = right_part.reshape(order_right, blocks_all, narrow).transpose(1, 0, 2)
        right_part = lax.all_to_all(right_part, "seq", split_axis=0, concat_axis=2, tiled=True)
        right_wide = right_part.reshape(tokens_dev, width).astype(jnp.float32)
        grad_value = (right_wide * active).astype(jnp.bfloat16)
        grad_gate = (right_wide * slope_values).astype(jnp.bfloat16)
        total = incoming.astype(jnp.float32)
        total = total + jnp.dot(grad_value, value_full.T, preferred_element_type=jnp.float32)
        total = total + jnp.dot(grad_gate, gate_full.T, preferred_element_type=jnp.float32)
        return total.astype(jnp.bfloat16)

    def one_pass(incoming):
        return branch(incoming)

    first_pass = one_pass(grad_out)
    received = passed_along(first_pass, "pipe", -1)
    second_pass = one_pass(received)
    result = jnp.where(segment_index == 1, first_pass, second_pass)
    return result[None]


def solution(mesh):
    in_specs = (
        P("pipe", "seq", None),
        P("seq", None),
        P("pipe", "seq", None),
        P("pipe", "seq", None),
        P("pipe", "seq", None),
        P("pipe", "seq", None),
        P("pipe", "seq", None),
        P("pipe", "seq", None),
    )
    out_specs = P("pipe", "seq", None)
    return jax.shard_map(body, mesh=mesh, in_specs=in_specs, out_specs=out_specs, check_vma=False)
```

profile of v0, /device:TPU:12, one launch (start us, length us, event | category | flops | bytes accessed | tf_op | source)
XLA Modules:
  0.0 474.2 jit_solution(7210830404615315919)
XLA Ops:
  8.0 58.3 %all-gather.11.cloned.1.call-done = bf16[1,768,768]{2,1,0:T(8,128)(2,1)} async-done(((bf16[1,48,768]{2,1,0:T(8,128)(2,1)}), bf16[1,768,768]{2,1,0:T(8,128)(2,1)}) %all-gather.11.cloned.1.call-update) | async-done | bytes 1179664 | tf_op jit(solution)/shard_map/all_gather | solution.py:27
  69.5 5.8 %copy.22 = bf16[1,1024,768]{1,0,2:T(2,128)(2,1)} copy(bf16[1,1024,768]{2,1,0:T(8,128)(2,1)S(1)} %fusion.29) | data formatting | bytes 3145728 | tf_op jit(solution)/shard_map/reshape | solution.py:50
  75.8 11.3 %reduce = bf16[768,1024]{1,0:T(8,128)(2,1)S(1)} reduce(bf16[768,1,1024]{2,1,0:T(2,128)(2,1)} %bitcast.107, bf16[]{:T(256)} %broadcast.13), dimensions={1}, to_apply=%bitcast.96.reduce_sub_computation | reduce | bytes 3145730
  89.1 6.1 %all-to-all-start = ((bf16[16,2,24576]{2,1,0:T(2,128)(2,1)}), bf16[16,2,24576]{2,1,0:T(2,128)(2,1)S(1)}, u32[]{:S(2)}, u32[]{:S(2)}) async-start(bf16[16,2,24576]{2,1,0:T(2,128)(2,1)} %reshape.65), calls=%async_computation | async-start | bytes 3145728 | tf_op jit(solution)/shard_map/all_to_all | solution.py:51
  96.6 72.8 %all-gather.2 = f32[16,1,1024]{2,1,0:T(1,128)S(1)} all-gather(f32[1,1,1024]{2,1,0:T(1,128)S(1)} %copy-done.13), channel_id=4, replica_groups=mesh['pipe'=2,'seq'=16] {'seq'}, dimensions={0}, use_global_device_ids=true | all-gather | bytes 69632 | tf_op jit(solution)/shard_map/all_gather | solution.py:38
  169.4 29.2 %all-gather.1 = bf16[16,1,16]{2,1,0:T(2,128)(2,1)S(1)} all-gather(bf16[1,1,16]{2,1,0:T(2,128)(2,1)S(1)} %copy-done.14), channel_id=3, replica_groups=mesh['pipe'=2,'seq'=16] {'seq'}, dimensions={0}, use_global_device_ids=true | all-gather | bytes 544 | tf_op jit(solution)/shard_map/all_gather | solution.py:29
  198.6 6.3 %reshape.66 = bf16[768,1,1024]{2,1,0:T(2,128)(2,1)} reshape(bf16[16,2,24576]{2,1,0:T(2,128)(2,1)S(1)} %all-to-all-done) | data formatting | bytes 3145728
  210.5 9.8 %reshape.46 = bf16[16,49152]{1,0:T(8,128)(2,1)S(1)} reshape(bf16[16,1,1024,48]{3,2,0,1:T(8,128)(2,1)} %copy.23) | data formatting | bytes 3145728 | tf_op jit(solution)/shard_map/reshape | solution.py:55
  222.6 6.8 %reshape.53 = f32[16,1024,48]{2,1,0:T(8,128)} reshape(f32[16,49152]{1,0:T(8,128)} %fusion.3) | data formatting | bytes 6291456 | tf_op jit(solution)/shard_map/convert_element_type | solution.py:59
  229.3 7.4 %fusion.4 = bf16[1024,16,48]{2,0,1:T(8,128)(2,1)} fusion(f32[16,1024,48]{2,1,0:T(8,128)} %reshape.53, f32[16,1024]{1,0:T(8,128)S(1)} %bitcast.118), kind=kLoop, calls=%fused_computation.11 | loop fusion | flops 1572864 | bytes 4784128 | tf_op jit(solution)/shard_map/transpose | solution.py:60
  244.8 11.8 %all-to-all-start.1 = ((bf16[16,1024,48]{1,2,0:T(8,128)(2,1)}), bf16[16,1024,48]{1,2,0:T(8,128)(2,1)S(1)}, u32[]{:S(2)}, u32[]{:S(2)}) async-start(bf16[16,1024,48]{1,2,0:T(8,128)(2,1)} %bitcast.115), calls=%async_computation.1 | async-start | bytes 3145728 | tf_op jit(solution)/shard_map/all_to_all | solution.py:65
  260.6 5.1 %all-gather.17.cloned.1.call-done = bf16[1,768,768]{2,1,0:T(8,128)(2,1)} async-done(((bf16[1,48,768]{2,1,0:T(8,128)(2,1)}), bf16[1,768,768]{2,1,0:T(8,128)(2,1)}) %all-gather.17.cloned.1.call-update) | async-done | bytes 1179664 | tf_op jit(solution)/shard_map/all_gather | solution.py:25
  265.7 5.2 %fusion.11 = f32[1024,768]{1,0:T(8,128)} fusion(bf16[1024,768]{1,0:T(8,128)(2,1)} %convolution_convert_fusion.4, bf16[1,768,768]{2,1,0:T(8,128)(2,1)} %all-gather.17.cloned.1.call-done, bf16[1,1024,768]{2,1,0:T(8,128)(2,1)S(1)} %copy-done), kind=kOutput, calls=%fused_computation.18 | convolution fusion | flops 1216610304 | bytes 7471104 | tf_op jit(solution)/shard_map/dot_general | solution.py:39
  270.9 15.4 %all-to-all-done.1 = bf16[16,1024,48]{1,2,0:T(8,128)(2,1)S(1)} async-done(((bf16[16,1024,48]{1,2,0:T(8,128)(2,1)}), bf16[16,1024,48]{1,2,0:T(8,128)(2,1)S(1)}, u32[]{:S(2)}, u32[]{:S(2)}) %all-to-all-start.1) | async-done | bytes 1572896 | tf_op jit(solution)/shard_map/all_to_all | solution.py:65
  306.1 5.9 %copy.27 = bf16[1,1024,768]{1,0,2:T(2,128)(2,1)} copy(bf16[1,1024,768]{2,1,0:T(8,128)(2,1)S(1)} %fusion.30) | data formatting | bytes 3145728 | tf_op jit(solution)/shard_map/reshape | solution.py:50
  312.0 11.2 %reduce.1 = bf16[768,1024]{1,0:T(8,128)(2,1)S(1)} reduce(bf16[768,1,1024]{2,1,0:T(2,128)(2,1)} %bitcast.108, bf16[]{:T(256)} %broadcast.13), dimensions={1}, to_apply=%bitcast.98.reduce_sub_computation | reduce | bytes 3145730
  324.4 41.0 %all_to_all.48 = bf16[16,2,24576]{2,1,0:T(2,128)(2,1)S(1)} all-to-all(bf16[16,2,24576]{2,1,0:T(2,128)(2,1)S(1)} %reshape.67), channel_id=1, replica_groups=mesh['pipe'=2,'seq'=16] {'seq'}, dimensions={0} | all-to-all | bytes 3145728 | tf_op jit(solution)/shard_map/all_to_all | solution.py:51
  365.4 6.2 %reshape.68 = bf16[768,1,1024]{2,1,0:T(2,128)(2,1)} reshape(bf16[16,2,24576]{2,1,0:T(2,128)(2,1)S(1)} %all_to_all.48) | data formatting | bytes 3145728
  377.2 9.8 %reshape.50 = bf16[16,49152]{1,0:T(8,128)(2,1)S(1)} reshape(bf16[16,1,1024,48]{3,2,0,1:T(8,128)(2,1)} %copy.28) | data formatting | bytes 3145728 | tf_op jit(solution)/shard_map/reshape | solution.py:55
  389.4 6.8 %reshape.55 = f32[16,1024,48]{2,1,0:T(8,128)} reshape(f32[16,49152]{1,0:T(8,128)} %fusion.1) | data formatting | bytes 6291456 | tf_op jit(solution)/shard_map/convert_element_type | solution.py:59
  396.2 7.4 %fusion.5 = bf16[1024,16,48]{2,0,1:T(8,128)(2,1)} fusion(f32[16,1024,48]{2,1,0:T(8,128)} %reshape.55, f32[16,1024]{1,0:T(8,128)S(1)} %bitcast.119), kind=kLoop, calls=%fused_computation.12 | loop fusion | flops 1572864 | bytes 4784128 | tf_op jit(solution)/shard_map/transpose | solution.py:60
  407.1 4.6 fusion.19
  411.7 5.4 %all-to-all-start.3 = ((bf16[16,1024,48]{1,2,0:T(8,128)(2,1)}), bf16[16,1024,48]{1,2,0:T(8,128)(2,1)S(1)}, u32[]{:S(2)}, u32[]{:S(2)}) async-start(bf16[16,1024,48]{1,2,0:T(8,128)(2,1)} %bitcast.25), calls=%async_computation.3 | async-start | bytes 3145728 | tf_op jit(solution)/shard_map/all_to_all | solution.py:65
  417.1 36.5 %all-to-all-done.3 = bf16[16,1024,48]{1,2,0:T(8,128)(2,1)S(1)} async-done(((bf16[16,1024,48]{1,2,0:T(8,128)(2,1)}), bf16[16,1024,48]{1,2,0:T(8,128)(2,1)S(1)}, u32[]{:S(2)}, u32[]{:S(2)}) %all-to-all-start.3) | async-done | bytes 1572896 | tf_op jit(solution)/shard_map/all_to_all | solution.py:65
  (77 shorter events, 74.2 us)
Async XLA Ops:
  6.5 250.1 %copy-start = (bf16[1,1024,768]{2,1,0:T(8,128)(2,1)S(1)}, bf16[1,1024,768]{2,1,0:T(8,128)(2,1)}, u32[]{:S(2)}) copy-start(bf16[1,1024,768]{2,1,0:T(8,128)(2,1)} %param.8) | copy-start | bytes 4718596
  6.5 59.8 %all-gather.11.cloned.1.call-start = ((), (), s32[]{:S(2)}) async-start(), calls=%async_computation.4 | async-start | bytes 1253376 | tf_op jit(solution)/shard_map/all_gather | solution.py:27
  7.3 233.0 %all-gather.13.cloned.1.call-start = ((), (), s32[]{:S(2)}) async-start(), calls=%async_computation.5 | async-start | bytes 2228224 | tf_op jit(solution)/shard_map/all_gather | solution.py:28
  89.1 7.4 %copy-start.13 = (f32[1,1,1024]{2,1,0:T(1,128)S(1)}, f32[1,1,1024]{2,1,0:T(1,128)}, u32[]{:S(2)}) copy-start(f32[1,1,1024]{2,1,0:T(1,128)} %param.15) | copy-start | bytes 12292
  89.1 80.3 %copy-start.14 = (bf16[1,1,16]{2,1,0:T(2,128)(2,1)S(1)}, bf16[1,1,16]{2,1,0:T(2,128)(2,1)}, u32[]{:S(2)}) copy-start(bf16[1,1,16]{2,1,0:T(2,128)(2,1)} %param.14) | copy-start | bytes 100
  89.1 109.4 %all-to-all-start = ((bf16[16,2,24576]{2,1,0:T(2,128)(2,1)}), bf16[16,2,24576]{2,1,0:T(2,128)(2,1)S(1)}, u32[]{:S(2)}, u32[]{:S(2)}) async-start(bf16[16,2,24576]{2,1,0:T(2,128)(2,1)} %reshape.65), calls=%async_computation | async-start | bytes 3145728 | tf_op jit(solution)/shard_map/all_to_all | solution.py:51
  95.3 161.4 %all-gather.15.cloned.1.call-start = ((), (), s32[]{:S(2)}) async-start(), calls=%async_computation.6 | async-start | bytes 1253376 | tf_op jit(solution)/shard_map/all_gather | solution.py:26
  96.0 169.7 %all-gather.17.cloned.1.call-start = ((), (), s32[]{:S(2)}) async-start(), calls=%async_computation.7 | async-start | bytes 1253376 | tf_op jit(solution)/shard_map/all_gather | solution.py:25
  244.8 41.5 %all-to-all-start.1 = ((bf16[16,1024,48]{1,2,0:T(8,128)(2,1)}), bf16[16,1024,48]{1,2,0:T(8,128)(2,1)S(1)}, u32[]{:S(2)}, u32[]{:S(2)}) async-start(bf16[16,1024,48]{1,2,0:T(8,128)(2,1)} %bitcast.115), calls=%async_computation.1 | async-start | bytes 3145728 | tf_op jit(solution)/shard_map/all_to_all | solution.py:65
  292.1 4.0 copy-start.3
  292.1 4.0 copy-start.4
  292.2 4.1 copy-start.8
  292.2 4.5 copy-start.12
  296.7 7.9 %copy-start.17 = (bf16[1,768,768]{2,1,0:T(8,128)(2,1)S(1)}, bf16[1,768,768]{2,1,0:T(8,128)(2,1)}, u32[]{:S(2)}) copy-start(bf16[1,768,768]{2,1,0:T(8,128)(2,1)} %all-gather.11.cloned.1.call-done) | copy-start | bytes 3538948
  298.2 7.9 %copy-start.6 = (bf16[1024,768]{1,0:T(8,128)(2,1)}, bf16[1024,768]{1,0:T(8,128)(2,1)S(1)}, u32[]{:S(2)}) copy-start(bf16[1024,768]{1,0:T(8,128)(2,1)S(1)} %add_convert_fusion.1) | copy-start | bytes 4718596
  298.2 5.3 %collective-permute-start = (bf16[1024,768]{1,0:T(8,128)(2,1)S(1)}, bf16[1024,768]{1,0:T(8,128)(2,1)S(1)}, u32[]{:S(2)}, u32[]{:S(2)}) collective-permute-start(bf16[1024,768]{1,0:T(8,128)(2,1)S(1)} %add_convert_fusion.1), channel_id=1, source_target_pairs={{16,0},{17,1},{18,2},{19,3},{20,4},{21,5},{22,6},{23,7},{24,8},{25... | collective-permute-start | bytes 4718600 | tf_op jit(solution)/shard_map/ppermute | solution.py:10
  411.7 41.9 %all-to-all-start.3 = ((bf16[16,1024,48]{1,2,0:T(8,128)(2,1)}), bf16[16,1024,48]{1,2,0:T(8,128)(2,1)S(1)}, u32[]{:S(2)}, u32[]{:S(2)}) async-start(bf16[16,1024,48]{1,2,0:T(8,128)(2,1)} %bitcast.25), calls=%async_computation.3 | async-start | bytes 3145728 | tf_op jit(solution)/shard_map/all_to_all | solution.py:65
  455.6 3.8 copy-start.16
  455.6 3.8 copy-start.19
  459.4 4.0 copy-start.2
  459.4 4.0 copy-start.5
  459.4 4.2 copy-start.7
  459.4 4.5 copy-start.9
  459.4 5.0 %copy-start.11 = (bf16[1024,768]{1,0:T(8,128)(2,1)S(1)}, bf16[1024,768]{1,0:T(8,128)(2,1)}, u32[]{:S(2)}) copy-start(bf16[1024,768]{1,0:T(8,128)(2,1)} %copy-done.10) | copy-start | bytes 4718596
  (4 other events, 11.4 us)
Sparse Core Ops, SparseCore 0:
  10.2 56.1 all-gather.10
  69.1 73.1 all-gather.12
  145.1 59.0 all-gather.14
  206.9 58.8 all-gather.16
where the time goes:
time: 483 us; the launch traced here: 474 us
  blocking collectives  143 us (30%)
  waiting for transfers between devices  122 us (25%)
  local copies, waits for them, and re-layouts  89.7 us (19%)
  other arithmetic  41.4 us (9%)
  matrix products  39.6 us (8%)
  starting transfers between devices  24.9 us (5%)
  between operations  13.8 us (3%)
    all_gather x1, blocking collectives, body(): twiddle_whole = lax.all_gather(twiddle_own, 'seq', axis=0, tiled=True)  72.8 us
    all_gather x1, waiting for transfers between devices, body(): lax.all_gather(out_weight[0], 'seq', axis=0, tiled=True)  58.3 us
    all_to_all x2, waiting for transfers between devices, branch(): lax.all_to_all(right_part, 'seq', split_axis=0, concat_axis=2, tiled=True)  51.9 us
    all_to_all x1, blocking collectives, branch(): lax.all_to_all(mixed, 'seq', split_axis=2, concat_axis=0, tiled=True)  41 us
    all_gather x1, blocking collectives, body(): lax.all_gather(left_factor[0], 'seq', axis=0, tiled=True)  29.2 us
    unnamed x48, local copies, waits for them, and re-layouts  24 us
    unnamed x2, other arithmetic  22.5 us
    reshape x2, local copies, waits for them, and re-layouts, branch(): spread.reshape(blocks_all, order_right * narrow)  19.6 us
  transfers between devices with their start and end apart: 8, of which 5 were waited for; matrix products, arithmetic and copies ran while one was open for 16% of the time, Pallas kernels for 0%

commit v1 on v0

v1 whole, which is shorter than its diff:
```python
import jax
import jax.numpy as jnp
from jax import lax
from jax.experimental import pallas as pl
from jax.experimental.pallas import tpu as pltpu
from jax.sharding import PartitionSpec as P

BF = jnp.bfloat16
F32 = jnp.float32
SHARDS = 16
ANY = pl.BlockSpec(memory_space=pl.ANY)
VMEM = pl.BlockSpec(memory_space=pltpu.VMEM)
PARAMS = pltpu.CompilerParams(vmem_limit_bytes=48 * 1024 * 1024)

RIGHT, OUT, VALUE, GATE, ROWS = 0, 256, 400, 544, 688


def dot_nn(a, b):
    return lax.dot_general(a, b, (((1,), (0,)), ((), ())), preferred_element_type=F32)


def dot_nt(a, b):
    return lax.dot_general(a, b, (((1,), (1,)), ((), ())), preferred_element_type=F32)


def dot_tn(a, b):
    return lax.dot_general(a, b, (((0,), (0,)), ((), ())), preferred_element_type=F32)


def pack_kernel(right, out, value, gate, blob):
    for g in range(4):
        blob[RIGHT + 64 * g : RIGHT + 64 * g + 64, :] = right[0, :, 256 * g : 256 * g + 256]
    for base, ref in ((OUT, out), (VALUE, value), (GATE, gate)):
        for g in range(3):
            blob[base + 48 * g : base + 48 * g + 48, :] = ref[0, :, 256 * g : 256 * g + 256]


def pack(right, out, value, gate):
    return pl.pallas_call(
        pack_kernel,
        out_shape=jax.ShapeDtypeStruct((ROWS, 256), BF),
        in_specs=[VMEM] * 4,
        out_specs=VMEM,
        name="pack",
    )(right, out, value, gate)


def mix_kernel(section, left, x, y):
    factor = left[SHARDS * section : SHARDS * (section + 1), 0, 0:16].astype(BF)
    rows = lax.broadcasted_iota(jnp.int32, (256, 16), 0)
    cols = lax.broadcasted_iota(jnp.int32, (256, 16), 1)
    spread = jnp.where(rows // 16 == cols, 1.0, 0.0).astype(BF)
    wide = dot_nt(dot_nt(spread, factor).astype(BF), spread)
    at = lax.broadcasted_iota(jnp.int32, (256, 256), 0) % 16
    to = lax.broadcasted_iota(jnp.int32, (256, 256), 1) % 16
    matrix = jnp.where(at == to, wide, 0.0).astype(BF)
    for q in range(2):
        part = x[:, 16 * q : 16 * q + 16, :].reshape(256, x.shape[2])
        y[:, 16 * q : 16 * q + 16, :] = dot_nn(matrix, part).astype(BF).reshape(16, 16, x.shape[2])


def mix(section, left, x):
    x = x.reshape(SHARDS, 32, x.shape[1])
    y = pl.pallas_call(
        lambda *refs: mix_kernel(section, *refs),
        out_shape=jax.ShapeDtypeStruct(x.shape, BF),
        in_specs=[VMEM] * 2,
        out_specs=VMEM,
        name="mix",
        cost_estimate=pl.CostEstimate(flops=2 * 256 * 256 * 768 * 2, bytes_accessed=1600000, transcendentals=0),
    )(left, x)
    return y.reshape(SHARDS * 32, x.shape[2])


def weight_copies(pieces, refs, scratch, sems, first, count):
    seq = lax.axis_index("seq")
    z, place = seq // 4, seq % 4
    copies = []
    for (at, shift, step, offset), ref in zip(pieces, refs):
        del at
        for n, k in enumerate(shift):
            shard = lax.rem(z - k + 4, 4) * 4 + jnp.bitwise_xor(place, step)
            copies.append(
                pltpu.make_async_copy(
                    ref.at[pl.ds(offset + n * ROWS + first, count), :],
                    scratch.at[shard, pl.ds(first, count), :],
                    sems.at[len(copies)],
                )
            )
    assert len(copies) == SHARDS
    return copies


def forward_kernel(pieces, n_refs, *refs):
    x, weights, active, slope, scratch, sems = refs[0], refs[1 : 1 + n_refs], *refs[1 + n_refs :]
    copies = weight_copies(pieces, weights, scratch, sems, VALUE, ROWS - VALUE)
    for c in copies:
        c.start()
    for c in copies:
        c.wait()
    for t in range(2):
        rows = slice(512 * t, 512 * t + 512)
        for e in range(3):
            lanes = slice(256 * e, 256 * e + 256)
            value = scratch[:, VALUE + 48 * e : VALUE + 48 * e + 48, :].reshape(768, 256)
            gate = scratch[:, GATE + 48 * e : GATE + 48 * e + 48, :].reshape(768, 256)
            values = dot_nn(x[0, rows, :], value).astype(BF).astype(F32)
            gates = dot_nn(x[0, rows, :], gate).astype(BF).astype(F32)
            sigma = 1.0 / (1.0 + jnp.exp(-gates))
            active[rows, lanes] = (gates * sigma).astype(BF)
            slope[rows, lanes] = (sigma * (1.0 + gates * (1.0 - sigma)) * values).astype(BF)


def forward(x, pieces, weights):
    shape = jax.ShapeDtypeStruct(x.shape[1:], BF)
    return pl.pallas_call(
        lambda *refs: forward_kernel(pieces, len(weights), *refs),
        out_shape=(shape, shape),
        in_specs=[VMEM] + [ANY] * len(weights),
        out_specs=(VMEM, VMEM),
        scratch_shapes=[pltpu.VMEM((SHARDS, ROWS, 256), BF), pltpu.SemaphoreType.DMA((SHARDS,))],
        compiler_params=PARAMS,
        name="forward",
        cost_estimate=pl.CostEstimate(flops=4 * 1024 * 768 * 768, bytes_accessed=8000000, transcendentals=786432),
    )(x, *weights)


def layer_kernel(pieces, n_refs, last, *refs):
    lo, hi, twiddle, active, slope = refs[:5]
    weights, refs = refs[5 : 5 + n_refs], refs[5 + n_refs :]
    if last:
        got_lo, got_hi, own_lo, own_hi, result = refs[:5]
        refs = refs[5:]
    else:
        given, result_lo, result_hi = refs[:3]
        refs = refs[3:]
    scratch, left, turned, inner, act, slo, base, total, sem_w, sem, sem_out = refs
    pipe = lax.axis_index("pipe")
    halves = (slice(0, 512), slice(512, 1024))

    loads = [pltpu.make_async_copy(r, left.at[h], sem.at[n]) for n, (r, h) in enumerate(zip((lo, hi), halves))]
    copies = weight_copies(pieces, weights, scratch, sem_w, 0, VALUE)
    copies_in = weight_copies(pieces, weights, scratch, sem_w.at[pl.ds(SHARDS, SHARDS)], VALUE, ROWS - VALUE)
    gate_loads = [
        pltpu.make_async_copy(active, act, sem.at[2]),
        pltpu.make_async_copy(slope, slo, sem.at[3]),
    ]
    for c in loads + copies + gate_loads + copies_in:
        c.start()
    if last:

        @pl.when(pipe == 0)
        def _():
            for n, (r, h) in enumerate(zip((got_lo, got_hi), halves)):
                pltpu.make_async_copy(r, base.at[h], sem.at[4 + n]).start()

        @pl.when(pipe != 0)
        def _():
            for n, (r, h) in enumerate(zip((own_lo, own_hi), halves)):
                pltpu.make_async_copy(r, base.at[h], sem.at[4 + n]).start()

        base_loads = [pltpu.make_async_copy(r, base.at[h], sem.at[4 + n]) for n, (r, h) in enumerate(zip((got_lo, got_hi), halves))]
    else:
        base_loads = [pltpu.make_async_copy(given, base, sem.at[4])]
        base_loads[0].start()

    for c in loads:
        c.wait()
    column = jnp.broadcast_to(twiddle[...], (128, 1024)).T
    for c in range(6):
        lanes = slice(128 * c, 128 * c + 128)
        turned[:, lanes] = (left[:, lanes].astype(F32) * column).astype(BF)
    for c in copies:
        c.wait()
    for g in range(4):
        right = scratch[:, RIGHT + 64 * g : RIGHT + 64 * g + 64, :].reshape(1024, 256)
        inner[256 * g : 256 * g + 256, :] = dot_tn(right, turned[...]).astype(BF)
    for c in gate_loads + copies_in + base_loads:
        c.wait()
    stores = []
    for t in range(2):
        rows = slice(512 * t, 512 * t + 512)
        right_part = jnp.zeros((512, 768), F32)
        for e in range(3):
            out = scratch[:, OUT + 48 * e : OUT + 48 * e + 48, :].reshape(768, 256)
            right_part = right_part + dot_nt(inner[rows, 256 * e : 256 * e + 256], out)
        right_part = right_part.astype(BF).astype(F32)
        grad_value = (right_part * act[rows, :].astype(F32)).astype(BF)
        grad_gate = (right_part * slo[rows, :].astype(F32)).astype(BF)
        added = jnp.zeros((512, 768), F32)
        for e in range(3):
            lanes = slice(256 * e, 256 * e + 256)
            value = scratch[:, VALUE + 48 * e : VALUE + 48 * e + 48, :].reshape(768, 256)
            gate = scratch[:, GATE + 48 * e : GATE + 48 * e + 48, :].reshape(768, 256)
            added = added + dot_nt(grad_value[:, lanes], value) + dot_nt(grad_gate[:, lanes], gate)
        if last:
            added = jnp.where(pipe == 0, added, 0.0)
        total[rows, :] = (base[rows, :].astype(F32) + added).astype(BF)
        target = result.at[rows] if last else (result_lo, result_hi)[t]
        stores.append(pltpu.make_async_copy(total.at[rows], target, sem_out.at[t]))
        stores[-1].start()
    for c in stores:
        c.wait()


def layer(lo, hi, twiddle, active, slope, pieces, weights, incoming, last):
    half = jax.ShapeDtypeStruct((512, 768), BF)
    whole = jax.ShapeDtypeStruct((1024, 768), BF)
    big = pltpu.VMEM((1024, 768), BF)
    return pl.pallas_call(
        lambda *refs: layer_kernel(pieces, len(weights), last, *refs),
        out_shape=whole if last else (half, half),
        in_specs=[ANY, ANY, VMEM] + [ANY] * (2 + len(weights) + len(incoming)),
        out_specs=ANY if last else (ANY, ANY),
        scratch_shapes=[pltpu.VMEM((SHARDS, ROWS, 256), BF)]
        + [big] * 7
        + [pltpu.SemaphoreType.DMA((2 * SHARDS,)), pltpu.SemaphoreType.DMA((6,)), pltpu.SemaphoreType.DMA((2,))],
        compiler_params=PARAMS,
        name="layer",
        cost_estimate=pl.CostEstimate(flops=2 * 1024 * 768 * (1024 + 3 * 768), bytes_accessed=14000000, transcendentals=0),
    )(lo, hi, twiddle, active, slope, *weights, *incoming)


def sent(x, section, to):
    pairs = [(section * SHARDS + s, section * SHARDS + to(s)) for s in range(SHARDS)]
    return lax.ppermute(x, ("pipe", "seq"), pairs)


def along_z(x, section, k):
    return sent(x, section, lambda s: ((s // 4 + k) % 4) * 4 + s % 4)


def in_plane(x, section, d):
    return sent(x, section, lambda s: s ^ d)


def exchanged(x):
    return lax.all_to_all(x, "seq", split_axis=0, concat_axis=0, tiled=True)


def tied(*xs):
    return lax.optimization_barrier(xs)


def fast_body(inputs_saved, grad_out, value_weight, gate_weight, out_weight, right_factor, left_factor, twiddle):
    pipe = lax.axis_index("pipe")
    blob = pack(right_factor, out_weight, value_weight, gate_weight)
    row = jnp.pad(left_factor[0].astype(F32), ((0, 7), (0, 112)))
    rows = jnp.broadcast_to(row[None], (32, 8, 128)).reshape(256, 128)
    left = lax.all_to_all(rows, ("pipe", "seq"), split_axis=0, concat_axis=0, tiled=True).reshape(32, 8, 128)

    first_z = [along_z(blob, 1, k) for k in (1, 2, 3)]
    first_own = [in_plane(blob, 1, d) for d in (1, 2, 3)]
    sent_rows = lax.dynamic_slice_in_dim(grad_out, pipe * 512, 512, 0)
    arrived = exchanged(sent_rows)
    mixed = mix(1, left, arrived)
    mixed, *tie = tied(mixed, *first_z, *first_own)
    first_z, first_own = tie[:3], tie[3:]
    rest = jnp.concatenate(first_z)
    first_rest = [in_plane(rest, 1, d) for d in (1, 2, 3)]
    blob_later, _ = tied(blob, mixed)
    second_z = [along_z(blob_later, 0, k) for k in (1, 2, 3)]
    back = exchanged(mixed)
    other = lax.ppermute(back, "pipe", [(0, 1)])
    pieces = [(0, (0,), 0, 0)] + [(0, (k,), 0, 0) for k in (1, 2, 3)]
    pieces += [(0, (0,), d, 0) for d in (1, 2, 3)] + [(0, (1, 2, 3), d, 0) for d in (1, 2, 3)]
    weights = [blob, *first_z, *first_own, *first_rest]
    other, *second_z = tied(other, *second_z)
    column = jnp.concatenate([blob, *second_z])
    second_xy = [in_plane(column, 0, d) for d in (1, 2, 3)]
    active, slope = forward(inputs_saved, pieces, weights)
    g_lo, g_hi = layer(other, back, twiddle[0], active, slope, pieces, weights, [grad_out], False)

    got_lo = lax.ppermute(g_lo, "pipe", [(1, 0)])
    got_hi = lax.ppermute(g_hi, "pipe", [(1, 0)])
    arrived = exchanged(jnp.where(pipe == 0, got_lo, g_hi))
    mixed = mix(0, left, arrived)
    back = exchanged(mixed)
    other = lax.ppermute(back, "pipe", [(1, 0)])
    pieces = [(0, (0, 1, 2, 3), 0, 0)] + [(0, (0, 1, 2, 3), d, 0) for d in (1, 2, 3)]
    weights = [column, *second_xy]
    active, slope = forward(inputs_saved, pieces, weights)
    result = layer(back, other, twiddle[0], active, slope, pieces, weights, [got_lo, got_hi, g_lo, g_hi], True)
    return result[None]


def plain_body(inputs_saved, grad_out, value_weight, gate_weight, out_weight, right_factor, left_factor, twiddle):
    value_full, gate_full, out_full, right_full, left_full = (
        lax.all_gather(w[0], "seq", axis=0, tiled=True)
        for w in (value_weight, gate_weight, out_weight, right_factor, left_factor)
    )
    twiddle_own = twiddle[0]
    saved = inputs_saved[0]
    tokens_dev, width = saved.shape
    order = right_full.shape[0]
    blocks_dev, blocks_all = tokens_dev // order, left_full.shape[0]
    values = jnp.dot(saved, value_full, preferred_element_type=F32).astype(BF)
    gates = jnp.dot(saved, gate_full, preferred_element_type=F32).astype(BF).astype(F32)
    sigma = jax.nn.sigmoid(gates)
    active = gates * sigma
    slope = sigma * (1.0 + gates * (1.0 - sigma)) * values.astype(F32)

    def branch(incoming):
        mixed = jnp.dot(incoming, out_full.T, preferred_element_type=F32).astype(BF)
        mixed = mixed.reshape(blocks_dev, order, width)
        spread = lax.all_to_all(mixed, "seq", split_axis=1, concat_axis=0, tiled=True)
        part = spread.shape[1]
        left_part = jnp.dot(left_full.T, spread.reshape(blocks_all, part * width), preferred_element_type=F32).astype(BF)
        left_part = left_part.reshape(blocks_all, part, width)
        left_part = lax.all_to_all(left_part, "seq", split_axis=0, concat_axis=1, tiled=True)
        turned = (left_part.astype(F32) * twiddle_own[:, :, None]).astype(BF)
        right_part = jnp.einsum("pb,apc->abc", right_full, turned, preferred_element_type=F32).astype(BF)
        right_wide = right_part.reshape(tokens_dev, width).astype(F32)
        grad_value = (right_wide * active).astype(BF)
        grad_gate = (right_wide * slope).astype(BF)
        total = incoming.astype(F32)
        total = total + jnp.dot(grad_value, value_full.T, preferred_element_type=F32)
        total = total + jnp.dot(grad_gate, gate_full.T, preferred_element_type=F32)
        return total.astype(BF)

    first = branch(grad_out)
    second = branch(lax.ppermute(first, "pipe", [(1, 0)]))
    return jnp.where(lax.axis_index("pipe") == 1, first, second)[None]


def solution(mesh):
    fast = mesh.shape["pipe"] == 2 and mesh.shape["seq"] == SHARDS
    whole = P("pipe", "seq", None)
    in_specs = (whole, P("seq", None)) + (whole,) * 6
    return jax.shard_map(
        fast_body if fast else plain_body, mesh=mesh, in_specs=in_specs, out_specs=whole, check_vma=False
    )
```

time: 483 us -> 226 us (0.47); the launches traced: 474 us -> 223 us
  blocking collectives: 143 us -> 25.5 us
  local copies, waits for them, and re-layouts: 89.7 us -> 10.4 us
  Pallas kernels: 0 us -> 46.6 us
  waiting for transfers between devices: 122 us -> 80.4 us
  matrix products: 39.6 us -> 0 us
  other arithmetic: 41.4 us -> 2.03 us
  starting transfers between devices: 24.9 us -> 57.8 us
  between operations: 13.8 us -> 0.53 us
    all_gather x2 -> x0, blocking collectives: 102 us -> none  [the longest x1 72.8 us: body(): twiddle_whole = lax.all_gather(twiddle_own, 'seq', axis=0, tiled=True)]
    all_gather x4 -> x0, waiting for transfers between devices: 63.5 us -> none  [the longest x1 58.3 us: body(): lax.all_gather(out_weight[0], 'seq', axis=0, tiled=True)]
    pallas_call x0 -> x7, Pallas kernels: none -> 46.6 us  [the longest x2 21.8 us: layer(): pl.pallas_call(lambda *refs: layer_kernel(pieces, len(weights), last, *re...]
    dot_general x12 -> x0, matrix products: 39.6 us -> none  [the longest x2 9.09 us: branch(): jnp.dot(right_full.T, stacked, preferred_element_type=jnp.float32)]
    ppermute x1 -> x19, starting transfers between devices: 1.46 us -> 35.4 us  [the longest x15 27.4 us: sent(): return lax.ppermute(x, ('pipe', 'seq'), pairs)]
    ppermute x1 -> x19, waiting for transfers between devices: 3.83 us -> 35.1 us  [the longest x15 25.3 us: sent(): return lax.ppermute(x, ('pipe', 'seq'), pairs)]
    reshape x4 -> x0, local copies, waits for them, and re-layouts: 31.2 us -> none  [the longest x2 19.6 us: branch(): spread.reshape(blocks_all, order_right * narrow)]
    unnamed x2 -> x0, other arithmetic: 22.5 us -> none
  transfers between devices with their start and end apart: 8 -> 23, of which waited for: 5 -> 8; matrix products, arithmetic and copies ran while one was open for 16% -> 3% of each run, Pallas kernels for 0% -> 10%
where the time goes in v1:
time: 226 us; the launch traced here: 223 us
  waiting for transfers between devices  80.4 us (36%)
  starting transfers between devices  57.8 us (26%)
  Pallas kernels  46.6 us (21%)
  blocking collectives  25.5 us (11%)
  local copies, waits for them, and re-layouts  10.4 us (5%)
    all_to_all x3, waiting for transfers between devices, exchanged(): return lax.all_to_all(x, 'seq', split_axis=0, concat_axis=0, tiled=True)  41.1 us
    ppermute x15, starting transfers between devices, sent(): return lax.ppermute(x, ('pipe', 'seq'), pairs)  27.4 us
    all_to_all x1, blocking collectives, exchanged(): return lax.all_to_all(x, 'seq', split_axis=0, concat_axis=0, tiled=True)  25.5 us
    ppermute x15, waiting for transfers between devices, sent(): return lax.ppermute(x, ('pipe', 'seq'), pairs)  25.3 us
    pallas_call x2, Pallas kernels, layer(): pl.pallas_call(lambda *refs: layer_kernel(pieces, len(weights), last, *re...  21.8 us
    pallas_call x2, Pallas kernels, forward(): pl.pallas_call(lambda *refs: forward_kernel(pieces, len(weights), *refs),...  17.7 us
    all_to_all x3, starting transfers between devices, exchanged(): return lax.all_to_all(x, 'seq', split_axis=0, concat_axis=0, tiled=True)  16.5 us
    ppermute x1, waiting for transfers between devices, fast_body(): got_lo = lax.ppermute(g_lo, 'pipe', [(1, 0)])  9.79 us
  transfers between devices with their start and end apart: 23, of which 8 were waited for; matrix products, arithmetic and copies ran while one was open for 3% of the time, Pallas kernels for 10%

profile of v1, /device:TPU:12, one launch (start us, length us, event | category | flops | bytes accessed | tf_op | source)
XLA Modules:
  0.0 223.3 jit_solution(12479248830934331192)
XLA Ops:
  1.3 6.0 %all-to-all-start = ((f32[32,8,128]{2,1,0:T(8,128)}), f32[32,8,128]{2,1,0:T(8,128)S(1)}, u32[]{:S(2)}, u32[]{:S(2)}) async-start(f32[32,8,128]{2,1,0:T(8,128)} %broadcast_in_dim.4), calls=%async_computation | async-start | bytes 262144 | tf_op jit(solution)/shard_map/all_to_all | solution.py:250
  9.4 4.2 %all-to-all-done.refs_0_ = f32[32,8,128]{2,1,0:T(8,128)S(1)} async-done(((f32[32,8,128]{2,1,0:T(8,128)}), f32[32,8,128]{2,1,0:T(8,128)S(1)}, u32[]{:S(2)}, u32[]{:S(2)}) %all-to-all-start) | async-done | bytes 131104 | tf_op jit(solution)/shard_map/all_to_all | solution.py:250
  13.6 5.3 %all-to-all-start.1 = ((bf16[16,32,768]{2,1,0:T(8,128)(2,1)}), bf16[16,32,768]{2,1,0:T(8,128)(2,1)S(1)}, u32[]{:S(2)}, u32[]{:S(2)}) async-start(bf16[16,32,768]{2,1,0:T(8,128)(2,1)} %bitcast.1), calls=%async_computation.1 | async-start | bytes 1572864 | tf_op jit(solution)/shard_map/all_to_all | solution.py:238
  24.8 22.6 %all-to-all-done.1.refs_1_ = bf16[16,32,768]{2,1,0:T(8,128)(2,1)S(1)} async-done(((bf16[16,32,768]{2,1,0:T(8,128)(2,1)}), bf16[16,32,768]{2,1,0:T(8,128)(2,1)S(1)}, u32[]{:S(2)}, u32[]{:S(2)}) %all-to-all-start.1) | async-done | bytes 786464 | tf_op jit(solution)/shard_map/all_to_all | solution.py:238
  48.3 2.7 %mix.2 = bf16[16,32,768]{2,1,0:T(8,128)(2,1)} custom-call(f32[32,8,128]{2,1,0:T(8,128)} %copy-done.9, bf16[16,32,768]{2,1,0:T(8,128)(2,1)} %copy-done.8), custom_call_target="tpu_custom_call" | custom-call | flops 201326592 | bytes 1600000 | tf_op jit(solution)/shard_map/mix/pallas_call | solution.py:64
  51.9 5.1 %all-to-all-start.2 = ((bf16[16,32,768]{2,1,0:T(8,128)(2,1)}), bf16[16,32,768]{2,1,0:T(8,128)(2,1)S(1)}, u32[]{:S(2)}, u32[]{:S(2)}) async-start(bf16[16,32,768]{2,1,0:T(8,128)(2,1)} %mix.2), calls=%async_computation.2 | async-start | bytes 1572864 | tf_op jit(solution)/shard_map/all_to_all | solution.py:238
  64.2 11.7 %all-to-all-done.2 = bf16[16,32,768]{2,1,0:T(8,128)(2,1)S(1)} async-done(((bf16[16,32,768]{2,1,0:T(8,128)(2,1)}), bf16[16,32,768]{2,1,0:T(8,128)(2,1)S(1)}, u32[]{:S(2)}, u32[]{:S(2)}) %all-to-all-start.2) | async-done | bytes 786464 | tf_op jit(solution)/shard_map/all_to_all | solution.py:238
  75.8 4.1 %collective-permute-start.6 = (bf16[512,768]{1,0:T(8,128)(2,1)S(1)}, bf16[512,768]{1,0:T(8,128)(2,1)S(1)}, u32[]{:S(2)}, u32[]{:S(2)}) collective-permute-start(bf16[512,768]{1,0:T(8,128)(2,1)S(1)} %bitcast.9), channel_id=1, source_target_pairs={{0,16},{1,17},{2,18},{3,19},{4,20},{5,21},{6,22},{7,23},{8,24},{9,... | collective-permute-start | bytes 2359304 | tf_op jit(solution)/shard_map/ppermute | solution.py:264
  81.9 4.7 %collective-permute-start.8 = (bf16[688,256]{1,0:T(8,128)(2,1)S(1)}, bf16[688,256]{1,0:T(8,128)(2,1)S(1)}, u32[]{:S(2)}, u32[]{:S(2)}) collective-permute-start(bf16[688,256]{1,0:T(8,128)(2,1)S(1)} %copy-done), channel_id=1, source_target_pairs={{0,8},{1,9},{2,10},{3,11},{4,12},{5,13},{6,14},{7,15},{8,0},{9,1},... | collective-permute-start | bytes 1056776 | tf_op jit(solution)/shard_map/ppermute | solution.py:226
  86.6 2.6 %collective-permute-start.9 = (bf16[688,256]{1,0:T(8,128)(2,1)S(1)}, bf16[688,256]{1,0:T(8,128)(2,1)S(1)}, u32[]{:S(2)}, u32[]{:S(2)}) collective-permute-start(bf16[688,256]{1,0:T(8,128)(2,1)S(1)} %copy-done), channel_id=1, source_target_pairs={{0,12},{1,13},{2,14},{3,15},{4,0},{5,1},{6,2},{7,3},{8,4},{9,5},{1... | collective-permute-start | bytes 1056776 | tf_op jit(solution)/shard_map/ppermute | solution.py:226
  90.2 9.1 %forward.2 = (bf16[1024,768]{1,0:T(8,128)(2,1)}, bf16[1024,768]{1,0:T(8,128)(2,1)}) custom-call(bf16[1,1024,768]{2,1,0:T(8,128)(2,1)} %refs_0_.3, bf16[688,256]{1,0:T(8,128)(2,1)S(1)} %copy-done, bf16[688,256]{1,0:T(8,128)(2,1)S(1)} %collective-permute-done.refs_2_.refs_6_, bf16[688,256]{1,0:T(8,128)(2,1)S(1)} %collective-permute-done.1.refs_3_.refs_7_, ...), custom_call_target="tpu_custom_call" | custom-call | flops 2415919104 | bytes 8000000 | tf_op jit(solution)/shard_map/forward/pallas_call | solution.py:116
  104.1 11.0 %layer.2 = (bf16[512,768]{1,0:T(8,128)(2,1)}, bf16[512,768]{1,0:T(8,128)(2,1)S(1)}) custom-call(bf16[512,768]{1,0:T(8,128)(2,1)S(1)} %collective-permute-done.6.refs_0_, bf16[512,768]{1,0:T(8,128)(2,1)S(1)} %bitcast.10, f32[1,1024]{1,0:T(1,128)S(1)} %bitcast.11, bf16[1024,768]{1,0:T(8,128)(2,1)} %get-tuple-element.32.refs_3_, ...), custom_call_target="tpu_custom_call" | custom-call | flops 5234491392 | bytes 14000000 | tf_op jit(solution)/shard_map/layer/pallas_call | solution.py:210
  116.4 9.8 %collective-permute-done.13.refs_9_ = bf16[512,768]{1,0:T(8,128)(2,1)S(1)} collective-permute-done((bf16[512,768]{1,0:T(8,128)(2,1)}, bf16[512,768]{1,0:T(8,128)(2,1)S(1)}, u32[]{:S(2)}, u32[]{:S(2)}) %collective-permute-start.13) | collective-permute-done | bytes 786464 | tf_op jit(solution)/shard_map/ppermute | solution.py:274
  126.3 25.5 %all_to_all.43.refs_1_ = bf16[16,32,768]{2,1,0:T(8,128)(2,1)} all-to-all(bf16[16,32,768]{2,1,0:T(8,128)(2,1)S(1)} %bitcast.13), channel_id=1, replica_groups=mesh['pipe'=2,'seq'=16] {'seq'}, dimensions={0} | all-to-all | bytes 1572864 | tf_op jit(solution)/shard_map/all_to_all | solution.py:238
  151.8 2.7 %mix.3 = bf16[16,32,768]{2,1,0:T(8,128)(2,1)} custom-call(f32[32,8,128]{2,1,0:T(8,128)} %copy-done.9, bf16[16,32,768]{2,1,0:T(8,128)(2,1)} %all_to_all.43.refs_1_), custom_call_target="tpu_custom_call" | custom-call | flops 201326592 | bytes 1600000 | tf_op jit(solution)/shard_map/mix/pallas_call | solution.py:64
  154.4 6.1 %all-to-all-start.4 = ((bf16[16,32,768]{2,1,0:T(8,128)(2,1)}), bf16[16,32,768]{2,1,0:T(8,128)(2,1)}, u32[]{:S(2)}, u32[]{:S(2)}) async-start(bf16[16,32,768]{2,1,0:T(8,128)(2,1)} %mix.3), calls=%async_computation.4 | async-start | bytes 1572864 | tf_op jit(solution)/shard_map/all_to_all | solution.py:238
  161.8 3.4 %collective-permute-start.15 = (bf16[2752,256]{1,0:T(8,128)(2,1)S(1)}, bf16[2752,256]{1,0:T(8,128)(2,1)}, u32[]{:S(2)}, u32[]{:S(2)}) collective-permute-start(bf16[2752,256]{1,0:T(8,128)(2,1)S(1)} %pad_maximum_fusion.refs_1_.refs_5_), channel_id=1, source_target_pairs={{0,1},{1,0},{2,3},{3,2},{4,5},{5,4},{6,7},{7,6},{8,9},{9,8},{10,11... | collective-permute-start | bytes 4227080 | tf_op jit(solution)/shard_map/ppermute | solution.py:226
  165.2 2.5 %collective-permute-start.16 = (bf16[2752,256]{1,0:T(8,128)(2,1)S(1)}, bf16[2752,256]{1,0:T(8,128)(2,1)}, u32[]{:S(2)}, u32[]{:S(2)}) collective-permute-start(bf16[2752,256]{1,0:T(8,128)(2,1)S(1)} %pad_maximum_fusion.refs_1_.refs_5_), channel_id=1, source_target_pairs={{0,2},{1,3},{2,0},{3,1},{4,6},{5,7},{6,4},{7,5},{8,10},{9,11},{10,... | collective-permute-start | bytes 4227080 | tf_op jit(solution)/shard_map/ppermute | solution.py:226
  167.7 3.4 %collective-permute-start.17 = (bf16[2752,256]{1,0:T(8,128)(2,1)S(1)}, bf16[2752,256]{1,0:T(8,128)(2,1)}, u32[]{:S(2)}, u32[]{:S(2)}) collective-permute-start(bf16[2752,256]{1,0:T(8,128)(2,1)S(1)} %pad_maximum_fusion.refs_1_.refs_5_), channel_id=1, source_target_pairs={{0,3},{1,2},{2,1},{3,0},{4,7},{5,6},{6,5},{7,4},{8,11},{9,10},{10,... | collective-permute-start | bytes 4227080 | tf_op jit(solution)/shard_map/ppermute | solution.py:226
  172.3 6.8 %all-to-all-done.4 = bf16[16,32,768]{2,1,0:T(8,128)(2,1)} async-done(((bf16[16,32,768]{2,1,0:T(8,128)(2,1)}), bf16[16,32,768]{2,1,0:T(8,128)(2,1)}, u32[]{:S(2)}, u32[]{:S(2)}) %all-to-all-start.4) | async-done | bytes 786464 | tf_op jit(solution)/shard_map/all_to_all | solution.py:238
  180.4 7.3 %collective-permute-done.15.refs_2_.refs_6_ = bf16[2752,256]{1,0:T(8,128)(2,1)} collective-permute-done((bf16[2752,256]{1,0:T(8,128)(2,1)S(1)}, bf16[2752,256]{1,0:T(8,128)(2,1)}, u32[]{:S(2)}, u32[]{:S(2)}) %collective-permute-start.15) | collective-permute-done | bytes 1409056 | tf_op jit(solution)/shard_map/ppermute | solution.py:226
  187.7 16.0 %collective-permute-done.16.refs_3_.refs_7_ = bf16[2752,256]{1,0:T(8,128)(2,1)} collective-permute-done((bf16[2752,256]{1,0:T(8,128)(2,1)S(1)}, bf16[2752,256]{1,0:T(8,128)(2,1)}, u32[]{:S(2)}, u32[]{:S(2)}) %collective-permute-start.16) | collective-permute-done | bytes 1409056 | tf_op jit(solution)/shard_map/ppermute | solution.py:226
  203.7 8.6 %forward.3 = (bf16[1024,768]{1,0:T(8,128)(2,1)}, bf16[1024,768]{1,0:T(8,128)(2,1)}) custom-call(bf16[1,1024,768]{2,1,0:T(8,128)(2,1)} %refs_0_.3, bf16[2752,256]{1,0:T(8,128)(2,1)S(1)} %pad_maximum_fusion.refs_1_.refs_5_, bf16[2752,256]{1,0:T(8,128)(2,1)} %collective-permute-done.15.refs_2_.refs_6_, ...), custom_call_target="tpu_custom_call" | custom-call | flops 2415919104 | bytes 8000000 | tf_op jit(solution)/shard_map/forward/pallas_call | solution.py:116
  212.3 10.8 %layer.3 = bf16[1024,768]{1,0:T(8,128)(2,1)} custom-call(bf16[512,768]{1,0:T(8,128)(2,1)} %bitcast.7.refs_0_, bf16[512,768]{1,0:T(8,128)(2,1)S(1)} %collective-permute-done.14.refs_1_, f32[1,1024]{1,0:T(1,128)S(1)} %bitcast.12, bf16[1024,768]{1,0:T(8,128)(2,1)} %get-tuple-element.39.refs_3_, bf16[1024,768]{1,0:T(8,128)(2,1)} %get-tuple-element.40.refs_4_, ...), custom_call_target="tpu_custom_call" | custom-call | flops 5234491392 | bytes 14000000 | tf_op jit(solution)/shard_map/layer/pallas_call | solution.py:210
  (64 shorter events, 31.0 us)
Async XLA Ops:
  1.3 12.3 %all-to-all-start = ((f32[32,8,128]{2,1,0:T(8,128)}), f32[32,8,128]{2,1,0:T(8,128)S(1)}, u32[]{:S(2)}, u32[]{:S(2)}) async-start(f32[32,8,128]{2,1,0:T(8,128)} %broadcast_in_dim.4), calls=%async_computation | async-start | bytes 262144 | tf_op jit(solution)/shard_map/all_to_all | solution.py:250
  13.6 33.8 %all-to-all-start.1 = ((bf16[16,32,768]{2,1,0:T(8,128)(2,1)}), bf16[16,32,768]{2,1,0:T(8,128)(2,1)S(1)}, u32[]{:S(2)}, u32[]{:S(2)}) async-start(bf16[16,32,768]{2,1,0:T(8,128)(2,1)} %bitcast.1), calls=%async_computation.1 | async-start | bytes 1572864 | tf_op jit(solution)/shard_map/all_to_all | solution.py:238
  20.7 3.4 %collective-permute-start = (bf16[688,256]{1,0:T(8,128)(2,1)}, bf16[688,256]{1,0:T(8,128)(2,1)S(1)}, u32[]{:S(2)}, u32[]{:S(2)}) collective-permute-start(bf16[688,256]{1,0:T(8,128)(2,1)} %pack.1.refs_1_.refs_5_), channel_id=1, source_target_pairs={{16,20},{17,21},{18,22},{19,23},{20,24},{21,25},{22,26},{23,27},{2... | collective-permute-start | bytes 1056776 | tf_op jit(solution)/shard_map/ppermute | solution.py:226
  21.4 29.6 %collective-permute-start.1 = (bf16[688,256]{1,0:T(8,128)(2,1)}, bf16[688,256]{1,0:T(8,128)(2,1)S(1)}, u32[]{:S(2)}, u32[]{:S(2)}) collective-permute-start(bf16[688,256]{1,0:T(8,128)(2,1)} %pack.1.refs_1_.refs_5_), channel_id=1, source_target_pairs={{16,24},{17,25},{18,26},{19,27},{20,28},{21,29},{22,30},{23,31},{2... | collective-permute-start | bytes 1056776 | tf_op jit(solution)/shard_map/ppermute | solution.py:226
  22.1 29.0 %collective-permute-start.2 = (bf16[688,256]{1,0:T(8,128)(2,1)}, bf16[688,256]{1,0:T(8,128)(2,1)S(1)}, u32[]{:S(2)}, u32[]{:S(2)}) collective-permute-start(bf16[688,256]{1,0:T(8,128)(2,1)} %pack.1.refs_1_.refs_5_), channel_id=1, source_target_pairs={{16,28},{17,29},{18,30},{19,31},{20,16},{21,17},{22,18},{23,19},{2... | collective-permute-start | bytes 1056776 | tf_op jit(solution)/shard_map/ppermute | solution.py:226
  22.8 28.3 %collective-permute-start.3 = (bf16[688,256]{1,0:T(8,128)(2,1)}, bf16[688,256]{1,0:T(8,128)(2,1)S(1)}, u32[]{:S(2)}, u32[]{:S(2)}) collective-permute-start(bf16[688,256]{1,0:T(8,128)(2,1)} %pack.1.refs_1_.refs_5_), channel_id=1, source_target_pairs={{16,17},{17,16},{18,19},{19,18},{20,21},{21,20},{22,23},{23,22},{2... | collective-permute-start | bytes 1056776 | tf_op jit(solution)/shard_map/ppermute | solution.py:226
  23.5 27.6 %collective-permute-start.4 = (bf16[688,256]{1,0:T(8,128)(2,1)}, bf16[688,256]{1,0:T(8,128)(2,1)S(1)}, u32[]{:S(2)}, u32[]{:S(2)}) collective-permute-start(bf16[688,256]{1,0:T(8,128)(2,1)} %pack.1.refs_1_.refs_5_), channel_id=1, source_target_pairs={{16,18},{17,19},{18,16},{19,17},{20,22},{21,23},{22,20},{23,21},{2... | collective-permute-start | bytes 1056776 | tf_op jit(solution)/shard_map/ppermute | solution.py:226
  24.2 26.9 %collective-permute-start.5 = (bf16[688,256]{1,0:T(8,128)(2,1)}, bf16[688,256]{1,0:T(8,128)(2,1)S(1)}, u32[]{:S(2)}, u32[]{:S(2)}) collective-permute-start(bf16[688,256]{1,0:T(8,128)(2,1)} %pack.1.refs_1_.refs_5_), channel_id=1, source_target_pairs={{16,19},{17,18},{18,17},{19,16},{20,23},{21,22},{22,21},{23,20},{2... | collective-permute-start | bytes 1056776 | tf_op jit(solution)/shard_map/ppermute | solution.py:226
  51.9 24.0 %all-to-all-start.2 = ((bf16[16,32,768]{2,1,0:T(8,128)(2,1)}), bf16[16,32,768]{2,1,0:T(8,128)(2,1)S(1)}, u32[]{:S(2)}, u32[]{:S(2)}) async-start(bf16[16,32,768]{2,1,0:T(8,128)(2,1)} %mix.2), calls=%async_computation.2 | async-start | bytes 1572864 | tf_op jit(solution)/shard_map/all_to_all | solution.py:238
  58.5 43.6 %copy-start.7 = (f32[1,1,1024]{2,1,0:T(1,128)S(1)}, f32[1,1,1024]{2,1,0:T(1,128)}, u32[]{:S(2)}) copy-start(f32[1,1,1024]{2,1,0:T(1,128)} %param.15) | copy-start | bytes 12292
  59.2 22.7 %collective-permute-start.10 = (bf16[2064,256]{1,0:T(8,128)(2,1)}, bf16[2064,256]{1,0:T(8,128)(2,1)}, u32[]{:S(2)}, u32[]{:S(2)}) collective-permute-start(bf16[2064,256]{1,0:T(8,128)(2,1)} %constant_dynamic-update-slice_fusion), channel_id=1, source_target_pairs={{16,17},{17,16},{18,19},{19,18},{20,21},{21,20},{22,23},{23,22},{2... | collective-permute-start | bytes 3170312 | tf_op jit(solution)/shard_map/ppermute | solution.py:226
  60.9 25.7 %collective-permute-start.11 = (bf16[2064,256]{1,0:T(8,128)(2,1)}, bf16[2064,256]{1,0:T(8,128)(2,1)}, u32[]{:S(2)}, u32[]{:S(2)}) collective-permute-start(bf16[2064,256]{1,0:T(8,128)(2,1)} %constant_dynamic-update-slice_fusion), channel_id=1, source_target_pairs={{16,18},{17,19},{18,16},{19,17},{20,22},{21,23},{22,20},{23,21},{2... | collective-permute-start | bytes 3170312 | tf_op jit(solution)/shard_map/ppermute | solution.py:226
  62.5 26.7 %collective-permute-start.12 = (bf16[2064,256]{1,0:T(8,128)(2,1)}, bf16[2064,256]{1,0:T(8,128)(2,1)}, u32[]{:S(2)}, u32[]{:S(2)}) collective-permute-start(bf16[2064,256]{1,0:T(8,128)(2,1)} %constant_dynamic-update-slice_fusion), channel_id=1, source_target_pairs={{16,19},{17,18},{18,17},{19,16},{20,23},{21,22},{22,21},{23,20},{2... | collective-permute-start | bytes 3170312 | tf_op jit(solution)/shard_map/ppermute | solution.py:226
  75.8 25.5 %collective-permute-start.6 = (bf16[512,768]{1,0:T(8,128)(2,1)S(1)}, bf16[512,768]{1,0:T(8,128)(2,1)S(1)}, u32[]{:S(2)}, u32[]{:S(2)}) collective-permute-start(bf16[512,768]{1,0:T(8,128)(2,1)S(1)} %bitcast.9), channel_id=1, source_target_pairs={{0,16},{1,17},{2,18},{3,19},{4,20},{5,21},{6,22},{7,23},{8,24},{9,... | collective-permute-start | bytes 2359304 | tf_op jit(solution)/shard_map/ppermute | solution.py:264
  80.0 19.3 %collective-permute-start.7 = (bf16[688,256]{1,0:T(8,128)(2,1)S(1)}, bf16[688,256]{1,0:T(8,128)(2,1)S(1)}, u32[]{:S(2)}, u32[]{:S(2)}) collective-permute-start(bf16[688,256]{1,0:T(8,128)(2,1)S(1)} %copy-done), channel_id=1, source_target_pairs={{0,4},{1,5},{2,6},{3,7},{4,8},{5,9},{6,10},{7,11},{8,12},{9,13},{1... | collective-permute-start | bytes 1056776 | tf_op jit(solution)/shard_map/ppermute | solution.py:226
  81.9 17.4 %collective-permute-start.8 = (bf16[688,256]{1,0:T(8,128)(2,1)S(1)}, bf16[688,256]{1,0:T(8,128)(2,1)S(1)}, u32[]{:S(2)}, u32[]{:S(2)}) collective-permute-start(bf16[688,256]{1,0:T(8,128)(2,1)S(1)} %copy-done), channel_id=1, source_target_pairs={{0,8},{1,9},{2,10},{3,11},{4,12},{5,13},{6,14},{7,15},{8,0},{9,1},... | collective-permute-start | bytes 1056776 | tf_op jit(solution)/shard_map/ppermute | solution.py:226
  86.6 14.7 %collective-permute-start.9 = (bf16[688,256]{1,0:T(8,128)(2,1)S(1)}, bf16[688,256]{1,0:T(8,128)(2,1)S(1)}, u32[]{:S(2)}, u32[]{:S(2)}) collective-permute-start(bf16[688,256]{1,0:T(8,128)(2,1)S(1)} %copy-done), channel_id=1, source_target_pairs={{0,12},{1,13},{2,14},{3,15},{4,0},{5,1},{6,2},{7,3},{8,4},{9,5},{1... | collective-permute-start | bytes 1056776 | tf_op jit(solution)/shard_map/ppermute | solution.py:226
  115.1 11.1 %collective-permute-start.13 = (bf16[512,768]{1,0:T(8,128)(2,1)}, bf16[512,768]{1,0:T(8,128)(2,1)S(1)}, u32[]{:S(2)}, u32[]{:S(2)}) collective-permute-start(bf16[512,768]{1,0:T(8,128)(2,1)} %get-tuple-element.34.refs_11_), channel_id=1, source_target_pairs={{16,0},{17,1},{18,2},{19,3},{20,4},{21,5},{22,6},{23,7},{24,8},{25... | collective-permute-start | bytes 2359304 | tf_op jit(solution)/shard_map/ppermute | solution.py:274
  154.4 24.7 %all-to-all-start.4 = ((bf16[16,32,768]{2,1,0:T(8,128)(2,1)}), bf16[16,32,768]{2,1,0:T(8,128)(2,1)}, u32[]{:S(2)}, u32[]{:S(2)}) async-start(bf16[16,32,768]{2,1,0:T(8,128)(2,1)} %mix.3), calls=%async_computation.4 | async-start | bytes 1572864 | tf_op jit(solution)/shard_map/all_to_all | solution.py:238
  161.8 25.9 %collective-permute-start.15 = (bf16[2752,256]{1,0:T(8,128)(2,1)S(1)}, bf16[2752,256]{1,0:T(8,128)(2,1)}, u32[]{:S(2)}, u32[]{:S(2)}) collective-permute-start(bf16[2752,256]{1,0:T(8,128)(2,1)S(1)} %pad_maximum_fusion.refs_1_.refs_5_), channel_id=1, source_target_pairs={{0,1},{1,0},{2,3},{3,2},{4,5},{5,4},{6,7},{7,6},{8,9},{9,8},{10,11... | collective-permute-start | bytes 4227080 | tf_op jit(solution)/shard_map/ppermute | solution.py:226
  165.2 38.5 %collective-permute-start.16 = (bf16[2752,256]{1,0:T(8,128)(2,1)S(1)}, bf16[2752,256]{1,0:T(8,128)(2,1)}, u32[]{:S(2)}, u32[]{:S(2)}) collective-permute-start(bf16[2752,256]{1,0:T(8,128)(2,1)S(1)} %pad_maximum_fusion.refs_1_.refs_5_), channel_id=1, source_target_pairs={{0,2},{1,3},{2,0},{3,1},{4,6},{5,7},{6,4},{7,5},{8,10},{9,11},{10,... | collective-permute-start | bytes 4227080 | tf_op jit(solution)/shard_map/ppermute | solution.py:226
  167.7 36.1 %collective-permute-start.17 = (bf16[2752,256]{1,0:T(8,128)(2,1)S(1)}, bf16[2752,256]{1,0:T(8,128)(2,1)}, u32[]{:S(2)}, u32[]{:S(2)}) collective-permute-start(bf16[2752,256]{1,0:T(8,128)(2,1)S(1)} %pad_maximum_fusion.refs_1_.refs_5_), channel_id=1, source_target_pairs={{0,3},{1,2},{2,1},{3,0},{4,7},{5,6},{6,5},{7,4},{8,11},{9,10},{10,... | collective-permute-start | bytes 4227080 | tf_op jit(solution)/shard_map/ppermute | solution.py:226
  171.0 41.3 %collective-permute-start.18 = (bf16[512,768]{1,0:T(8,128)(2,1)S(1)}, bf16[512,768]{1,0:T(8,128)(2,1)}, u32[]{:S(2)}, u32[]{:S(2)}) collective-permute-start(bf16[512,768]{1,0:T(8,128)(2,1)S(1)} %get-tuple-element.35.refs_12_), channel_id=1, source_target_pairs={{16,0},{17,1},{18,2},{19,3},{20,4},{21,5},{22,6},{23,7},{24,8},{25... | collective-permute-start | bytes 2359304 | tf_op jit(solution)/shard_map/ppermute | solution.py:275
  179.2 33.2 %collective-permute-start.14 = (bf16[512,768]{1,0:T(8,128)(2,1)}, bf16[512,768]{1,0:T(8,128)(2,1)S(1)}, u32[]{:S(2)}, u32[]{:S(2)}) collective-permute-start(bf16[512,768]{1,0:T(8,128)(2,1)} %bitcast.7.refs_0_), channel_id=1, source_target_pairs={{16,0},{17,1},{18,2},{19,3},{20,4},{21,5},{22,6},{23,7},{24,8},{25... | collective-permute-start | bytes 2359304 | tf_op jit(solution)/shard_map/ppermute | solution.py:279
  (12 other events, 170.2 us)

commit v2 on v1

--- a/solution.py
+++ b/solution.py
@@ -10,7 +10,8 @@
 SHARDS = 16
 ANY = pl.BlockSpec(memory_space=pl.ANY)
 VMEM = pl.BlockSpec(memory_space=pltpu.VMEM)
-PARAMS = pltpu.CompilerParams(vmem_limit_bytes=48 * 1024 * 1024)
+LIGHT = pl.CostEstimate(flops=1, bytes_accessed=1, transcendentals=0)
+PARAMS = pltpu.CompilerParams(vmem_limit_bytes=60 * 1024 * 1024)
 
 RIGHT, OUT, VALUE, GATE, ROWS = 0, 256, 400, 544, 688
 
@@ -42,34 +43,106 @@
         in_specs=[VMEM] * 4,
         out_specs=VMEM,
         name="pack",
+        cost_estimate=LIGHT,
     )(right, out, value, gate)
 
 
-def mix_kernel(section, left, x, y):
-    factor = left[SHARDS * section : SHARDS * (section + 1), 0, 0:16].astype(BF)
+def rows_kernel(grad, own, got, out, scratch, sem):
+    pipe = lax.axis_index("pipe")
+    copy = pltpu.make_async_copy(grad.at[pl.ds(pipe * 512, 512), :], scratch, sem)
+    copy.start()
+    ours, theirs = (jnp.broadcast_to(r[0].astype(F32), (16, 16)) for r in (own, got))
+    low = lax.broadcasted_iota(jnp.int32, (16, 16), 0) < 8
+    both = jnp.where(low == (pipe == 1), ours, theirs).astype(BF)
+    for j in range(SHARDS):
+        out[j, 192:208, :] = jnp.zeros((16, 128), BF)
+        out[j, 192:208, 0:16] = both
+    copy.wait()
+    for j in range(SHARDS):
+        for c in range(6):
+            out[j, 32 * c : 32 * c + 32, :] = scratch[32 * j : 32 * j + 32, 128 * c : 128 * c + 128]
+
+
+def rows_to_send(grad, own, got):
+    return pl.pallas_call(
+        rows_kernel,
+        out_shape=jax.ShapeDtypeStruct((SHARDS, 208, 128), BF),
+        in_specs=[ANY, VMEM, VMEM],
+        out_specs=VMEM,
+        scratch_shapes=[pltpu.VMEM((512, 768), BF), pltpu.SemaphoreType.DMA],
+        name="rows",
+        cost_estimate=LIGHT,
+    )(grad, own, got)
+
+
+def mixing_matrix(factor):
     rows = lax.broadcasted_iota(jnp.int32, (256, 16), 0)
     cols = lax.broadcasted_iota(jnp.int32, (256, 16), 1)
     spread = jnp.where(rows // 16 == cols, 1.0, 0.0).astype(BF)
     wide = dot_nt(dot_nt(spread, factor).astype(BF), spread)
     at = lax.broadcasted_iota(jnp.int32, (256, 256), 0) % 16
     to = lax.broadcasted_iota(jnp.int32, (256, 256), 1) % 16
-    matrix = jnp.where(at == to, wide, 0.0).astype(BF)
+    return jnp.where(at == to, wide, 0.0).astype(BF)
+
+
+def first_mix_kernel(x, y):
+    matrix = mixing_matrix(x[:, 192, 0:16])
     for q in range(2):
-        part = x[:, 16 * q : 16 * q + 16, :].reshape(256, x.shape[2])
-        y[:, 16 * q : 16 * q + 16, :] = dot_nn(matrix, part).astype(BF).reshape(16, 16, x.shape[2])
-
-
-def mix(section, left, x):
-    x = x.reshape(SHARDS, 32, x.shape[1])
-    y = pl.pallas_call(
-        lambda *refs: mix_kernel(section, *refs),
-        out_shape=jax.ShapeDtypeStruct(x.shape, BF),
-        in_specs=[VMEM] * 2,
+        for c in range(6):
+            part = x[:, 32 * c + 16 * q : 32 * c + 16 * q + 16, :].reshape(256, 128)
+            y[:, 16 * q : 16 * q + 16, 128 * c : 128 * c + 128] = dot_nn(matrix, part).astype(BF).reshape(16, 16, 128)
+
+
+def second_mix_kernel(left, x, y):
+    matrix = mixing_matrix(left[:, 8, 0:16])
+    for q in range(2):
+        part = x[:, 16 * q : 16 * q + 16, :].reshape(256, 768)
+        y[:, 16 * q : 16 * q + 16, :] = dot_nn(matrix, part).astype(BF).reshape(16, 16, 768)
+
+
+def first_mix(x):
+    return pl.pallas_call(
+        first_mix_kernel,
+        out_shape=jax.ShapeDtypeStruct((SHARDS, 32, 768), BF),
+        in_specs=[VMEM],
         out_specs=VMEM,
         name="mix",
-        cost_estimate=pl.CostEstimate(flops=2 * 256 * 256 * 768 * 2, bytes_accessed=1600000, transcendentals=0),
-    )(left, x)
-    return y.reshape(SHARDS * 32, x.shape[2])
+        cost_estimate=LIGHT,
+    )(x)
+
+
+def second_mix(first, x):
+    return pl.pallas_call(
+        second_mix_kernel,
+        grid=(1,),
+        out_shape=jax.ShapeDtypeStruct((SHARDS, 32, 768), BF),
+        in_specs=[pl.BlockSpec((SHARDS, 16, 128), lambda i: (0, 12, 0)), pl.BlockSpec((SHARDS, 32, 768), lambda i: (0, 0, 0))],
+        out_specs=pl.BlockSpec((SHARDS, 32, 768), lambda i: (0, 0, 0)),
+        name="mix",
+        cost_estimate=LIGHT,
+    )(first, x)
+
+
+def stack_kernel(n, *refs):
+    ins, out, sems = refs[:n], refs[n], refs[n + 1]
+    copies = [pltpu.make_async_copy(r, out.at[pl.ds(ROWS * i, ROWS), :], sems.at[i]) for i, r in enumerate(ins)]
+    for c in copies:
+        c.start()
+    for c in copies:
+        c.wait()
+
+
+def stacked(*parts):
+    n = len(parts)
+    return pl.pallas_call(
+        lambda *refs: stack_kernel(n, *refs),
+        out_shape=jax.ShapeDtypeStruct((ROWS * n, 256), BF),
+        in_specs=[ANY] * n,
+        out_specs=VMEM,
+        scratch_shapes=[pltpu.SemaphoreType.DMA((n,))],
+        name="stack",
+        cost_estimate=LIGHT,
+    )(*parts)
 
 
 def weight_copies(pieces, refs, scratch, sems, first, count):
@@ -91,7 +164,7 @@
     return copies
 
 
-def forward_kernel(pieces, n_refs, *refs):
+def forward_work(pieces, n_refs, *refs):
     x, weights, active, slope, scratch, sems = refs[0], refs[1 : 1 + n_refs], *refs[1 + n_refs :]
     copies = weight_copies(pieces, weights, scratch, sems, VALUE, ROWS - VALUE)
     for c in copies:
@@ -111,21 +184,27 @@
             slope[rows, lanes] = (sigma * (1.0 + gates * (1.0 - sigma)) * values).astype(BF)
 
 
-def forward(x, pieces, weights):
+def forward_kernel(section, pieces, n_refs, *refs):
+    @pl.when(lax.axis_index("pipe") == section)
+    def _():
+        forward_work(pieces, n_refs, *refs)
+
+
+def forward(section, x, pieces, weights):
     shape = jax.ShapeDtypeStruct(x.shape[1:], BF)
     return pl.pallas_call(
-        lambda *refs: forward_kernel(pieces, len(weights), *refs),
+        lambda *refs: forward_kernel(section, pieces, len(weights), *refs),
         out_shape=(shape, shape),
         in_specs=[VMEM] + [ANY] * len(weights),
         out_specs=(VMEM, VMEM),
         scratch_shapes=[pltpu.VMEM((SHARDS, ROWS, 256), BF), pltpu.SemaphoreType.DMA((SHARDS,))],
         compiler_params=PARAMS,
         name="forward",
-        cost_estimate=pl.CostEstimate(flops=4 * 1024 * 768 * 768, bytes_accessed=8000000, transcendentals=786432),
+        cost_estimate=LIGHT,
     )(x, *weights)
 
 
-def layer_kernel(pieces, n_refs, last, *refs):
+def layer_work(pieces, n_refs, last, *refs):
     lo, hi, twiddle, active, slope = refs[:5]
     weights, refs = refs[5 : 5 + n_refs], refs[5 + n_refs :]
     if last:
@@ -135,7 +214,6 @@
         given, result_lo, result_hi = refs[:3]
         refs = refs[3:]
     scratch, left, turned, inner, act, slo, base, total, sem_w, sem, sem_out = refs
-    pipe = lax.axis_index("pipe")
     halves = (slice(0, 512), slice(512, 1024))
 
     loads = [pltpu.make_async_copy(r, left.at[h], sem.at[n]) for n, (r, h) in enumerate(zip((lo, hi), halves))]
@@ -148,21 +226,11 @@
     for c in loads + copies + gate_loads + copies_in:
         c.start()
     if last:
-
-        @pl.when(pipe == 0)
-        def _():
-            for n, (r, h) in enumerate(zip((got_lo, got_hi), halves)):
-                pltpu.make_async_copy(r, base.at[h], sem.at[4 + n]).start()
-
-        @pl.when(pipe != 0)
-        def _():
-            for n, (r, h) in enumerate(zip((own_lo, own_hi), halves)):
-                pltpu.make_async_copy(r, base.at[h], sem.at[4 + n]).start()
-
         base_loads = [pltpu.make_async_copy(r, base.at[h], sem.at[4 + n]) for n, (r, h) in enumerate(zip((got_lo, got_hi), halves))]
     else:
         base_loads = [pltpu.make_async_copy(given, base, sem.at[4])]
-        base_loads[0].start()
+    for c in base_loads:
+        c.start()
 
     for c in loads:
         c.wait()
@@ -193,8 +261,6 @@
             value = scratch[:, VALUE + 48 * e : VALUE + 48 * e + 48, :].reshape(768, 256)
             gate = scratch[:, GATE + 48 * e : GATE + 48 * e + 48, :].reshape(768, 256)
             added = added + dot_nt(grad_value[:, lanes], value) + dot_nt(grad_gate[:, lanes], gate)
-        if last:
-            added = jnp.where(pipe == 0, added, 0.0)
         total[rows, :] = (base[rows, :].astype(F32) + added).astype(BF)
         target = result.at[rows] if last else (result_lo, result_hi)[t]
         stores.append(pltpu.make_async_copy(total.at[rows], target, sem_out.at[t]))
@@ -203,12 +269,39 @@
         c.wait()
 
 
-def layer(lo, hi, twiddle, active, slope, pieces, weights, incoming, last):
+def layer_kernel(section, pieces, n_refs, last, *refs):
+    pipe = lax.axis_index("pipe")
+
+    @pl.when(pipe == section)
+    def _():
+        layer_work(pieces, n_refs, last, *refs)
+
+    if last:
+
+        @pl.when(pipe != section)
+        def _():
+            own, result = refs[5 + n_refs + 2 : 5 + n_refs + 4], refs[5 + n_refs + 4]
+            total, sem, sem_out = refs[-4], refs[-2], refs[-1]
+            loads = [pltpu.make_async_copy(own[t], total.at[512 * t : 512 * t + 512], sem.at[t]) for t in range(2)]
+            stores = [
+                pltpu.make_async_copy(total.at[512 * t : 512 * t + 512], result.at[512 * t : 512 * t + 512], sem_out.at[t])
+                for t in range(2)
+            ]
+            for c in loads:
+                c.start()
+            for load, store in zip(loads, stores):
+                load.wait()
+                store.start()
+            for c in stores:
+                c.wait()
+
+
+def layer(section, lo, hi, twiddle, active, slope, pieces, weights, incoming, last):
     half = jax.ShapeDtypeStruct((512, 768), BF)
     whole = jax.ShapeDtypeStruct((1024, 768), BF)
     big = pltpu.VMEM((1024, 768), BF)
     return pl.pallas_call(
-        lambda *refs: layer_kernel(pieces, len(weights), last, *refs),
+        lambda *refs: layer_kernel(section, pieces, len(weights), last, *refs),
         out_shape=whole if last else (half, half),
         in_specs=[ANY, ANY, VMEM] + [ANY] * (2 + len(weights) + len(incoming)),
         out_specs=ANY if last else (ANY, ANY),
@@ -242,45 +335,61 @@
     return lax.optimization_barrier(xs)
 
 
+LATER = (
+    [(0, (0,), 0, 0)]
+    + [(0, (k,), 0, 0) for k in (1, 2, 3)]
+    + [(0, (0,), d, 0) for d in (1, 2, 3)]
+    + [(0, (1, 2, 3), d, 0) for d in (1, 2, 3)]
+)
+EARLIER = tuple((0, (0, 1, 2, 3), d, 0) for d in range(4))
+
+
+def apart(f, *args):
+    shapes = jax.eval_shape(f, *args)
+    return lax.cond(
+        lax.axis_index("seq") >= 0,
+        f,
+        lambda *_: jax.tree.map(lambda x: jnp.zeros(x.shape, x.dtype), shapes),
+        *args,
+    )
+
+
 def fast_body(inputs_saved, grad_out, value_weight, gate_weight, out_weight, right_factor, left_factor, twiddle):
     pipe = lax.axis_index("pipe")
-    blob = pack(right_factor, out_weight, value_weight, gate_weight)
-    row = jnp.pad(left_factor[0].astype(F32), ((0, 7), (0, 112)))
-    rows = jnp.broadcast_to(row[None], (32, 8, 128)).reshape(256, 128)
-    left = lax.all_to_all(rows, ("pipe", "seq"), split_axis=0, concat_axis=0, tiled=True).reshape(32, 8, 128)
-
-    first_z = [along_z(blob, 1, k) for k in (1, 2, 3)]
-    first_own = [in_plane(blob, 1, d) for d in (1, 2, 3)]
-    sent_rows = lax.dynamic_slice_in_dim(grad_out, pipe * 512, 512, 0)
-    arrived = exchanged(sent_rows)
-    mixed = mix(1, left, arrived)
-    mixed, *tie = tied(mixed, *first_z, *first_own)
-    first_z, first_own = tie[:3], tie[3:]
-    rest = jnp.concatenate(first_z)
-    first_rest = [in_plane(rest, 1, d) for d in (1, 2, 3)]
-    blob_later, _ = tied(blob, mixed)
-    second_z = [along_z(blob_later, 0, k) for k in (1, 2, 3)]
-    back = exchanged(mixed)
-    other = lax.ppermute(back, "pipe", [(0, 1)])
-    pieces = [(0, (0,), 0, 0)] + [(0, (k,), 0, 0) for k in (1, 2, 3)]
-    pieces += [(0, (0,), d, 0) for d in (1, 2, 3)] + [(0, (1, 2, 3), d, 0) for d in (1, 2, 3)]
-    weights = [blob, *first_z, *first_own, *first_rest]
-    other, *second_z = tied(other, *second_z)
-    column = jnp.concatenate([blob, *second_z])
-    second_xy = [in_plane(column, 0, d) for d in (1, 2, 3)]
-    active, slope = forward(inputs_saved, pieces, weights)
-    g_lo, g_hi = layer(other, back, twiddle[0], active, slope, pieces, weights, [grad_out], False)
-
-    got_lo = lax.ppermute(g_lo, "pipe", [(1, 0)])
+    swap = [(0, 1), (1, 0)]
+    got_left = lax.ppermute(left_factor, "pipe", swap)
+    blob, got_left = tied(pack(right_factor, out_weight, value_weight, gate_weight), got_left)
+
+    along = [along_z(blob, 1, k) for k in (1, 2, 3)]
+    own = [in_plane(blob, 1, d) for d in (1, 2, 3)]
+    rows = rows_to_send(grad_out, left_factor, got_left)
+    rows, rest, *own = tied(rows, stacked(*along), *own)
+    plane = [in_plane(rest, 1, d) for d in (1, 2, 3)]
+    first, mixed = apart(lambda r: (lambda x: (x, first_mix(x)))(exchanged(r)), rows)
+    mixed, later_blob, *plane = tied(mixed, blob, *plane)
+    weights = [blob, *along, *own, *plane]
+    active, slope = forward(1, inputs_saved, LATER, weights)
+    later_along = [along_z(later_blob, 0, k) for k in (1, 2, 3)]
+    column = stacked(later_blob, *later_along)
+    back, active, slope, column = tied(exchanged(mixed).reshape(512, 768), active, slope, column)
+    other, column = tied(lax.ppermute(back, "pipe", [(0, 1)]), column)
+    later_plane = [in_plane(column, 0, d) for d in (1, 2, 3)]
+
+    def later_layer(other, back, active, slope, *weights):
+        g_lo, g_hi = layer(1, other, back, twiddle[0], active, slope, LATER, weights, [grad_out], False)
+        got_lo = lax.ppermute(g_lo, "pipe", [(1, 0)])
+        return g_lo, g_hi, got_lo, jnp.where(pipe == 0, got_lo, g_hi).reshape(SHARDS, 32, 768)
+
+    g_lo, g_hi, got_lo, rows = apart(later_layer, other, back, active, slope, *weights)
+
+    mixed = apart(lambda r, f: second_mix(f, exchanged(r)), rows, first)
+    mixed, g_hi, *later_plane = tied(mixed, g_hi, *later_plane)
     got_hi = lax.ppermute(g_hi, "pipe", [(1, 0)])
-    arrived = exchanged(jnp.where(pipe == 0, got_lo, g_hi))
-    mixed = mix(0, left, arrived)
-    back = exchanged(mixed)
+    weights = [column, *later_plane]
+    active, slope = forward(0, inputs_saved, EARLIER, weights)
+    back, active, slope, got_hi = tied(exchanged(mixed).reshape(512, 768), active, slope, got_hi)
     other = lax.ppermute(back, "pipe", [(1, 0)])
-    pieces = [(0, (0, 1, 2, 3), 0, 0)] + [(0, (0, 1, 2, 3), d, 0) for d in (1, 2, 3)]
-    weights = [column, *second_xy]
-    active, slope = forward(inputs_saved, pieces, weights)
-    result = layer(back, other, twiddle[0], active, slope, pieces, weights, [got_lo, got_hi, g_lo, g_hi], True)
+    result = layer(0, back, other, twiddle[0], active, slope, EARLIER, weights, [got_lo, got_hi, g_lo, g_hi], True)
     return result[None]
 
 

time: 226 us -> 191 us (0.85)
  waiting for transfers between devices: 80.4 us -> 40.2 us
  blocking collectives: 25.5 us -> 47 us
  Pallas kernels: 46.6 us -> 34.8 us
  local copies, waits for them, and re-layouts: 10.4 us -> 1.66 us
  starting transfers between devices: 57.8 us -> 63 us
    all_to_all x3 -> x2, waiting for transfers between devices: 41.1 us -> 9.48 us  [exchanged(): return lax.all_to_all(x, 'seq', split_axis=0, concat_axis=0, tiled=True)]
    all_to_all x1 -> x2, blocking collectives: 25.5 us -> 47 us  [exchanged(): return lax.all_to_all(x, 'seq', split_axis=0, concat_axis=0, tiled=True)]
    ppermute x2 -> x3, starting transfers between devices: 5.42 us -> 20 us  [the longest x1 18.7 us: fast_body(): other, column = tied(lax.ppermute(back, 'pipe', [(0, 1)]), column)]
    pallas_call x6 -> x9, Pallas kernels: 44.8 us -> 33.8 us  [the longest x2 11.3 us: forward(): pl.pallas_call(lambda *refs: forward_kernel(section, pieces, len(weights)...]
    ppermute x15, waiting for transfers between devices: 25.3 us -> 17.5 us  [sent(): return lax.ppermute(x, ('pipe', 'seq'), pairs)]
    all_to_all x1 -> x0, starting transfers between devices: 5.99 us -> none  [fast_body(): lax.all_to_all(rows, ('pipe', 'seq'), split_axis=0, concat_axis=0, tiled=...]
    all_to_all x3 -> x2, starting transfers between devices: 16.5 us -> 11.1 us  [exchanged(): return lax.all_to_all(x, 'seq', split_axis=0, concat_axis=0, tiled=True)]
    unnamed x28 -> x18, local copies, waits for them, and re-layouts: 6.9 us -> 1.66 us
  transfers between devices with their start and end apart: 23 -> 22, of which waited for: 8 -> 7; matrix products, arithmetic and copies ran while one was open for 3% -> 1% of each run, Pallas kernels for 10% -> 13%
where the time goes in v2:
time: 191 us; the launch traced here: 188 us
  starting transfers between devices  63 us (33%)
  blocking collectives  47 us (25%)
  waiting for transfers between devices  40.2 us (21%)
  Pallas kernels  34.8 us (18%)
    all_to_all x2, blocking collectives, exchanged(): return lax.all_to_all(x, 'seq', split_axis=0, concat_axis=0, tiled=True)  47 us
    ppermute x15, starting transfers between devices, sent(): return lax.ppermute(x, ('pipe', 'seq'), pairs)  29.3 us
    ppermute x1, starting transfers between devices, fast_body(): other, column = tied(lax.ppermute(back, 'pipe', [(0, 1)]), column)  18.7 us
    ppermute x15, waiting for transfers between devices, sent(): return lax.ppermute(x, ('pipe', 'seq'), pairs)  17.5 us
    pallas_call x2, Pallas kernels, forward(): pl.pallas_call(lambda *refs: forward_kernel(section, pieces, len(weights)...  11.3 us
    pallas_call x2, Pallas kernels, layer(): pl.pallas_call(lambda *refs: layer_kernel(section, pieces, len(weights),...  11.2 us
    all_to_all x2, starting transfers between devices, exchanged(): return lax.all_to_all(x, 'seq', split_axis=0, concat_axis=0, tiled=True)  11.1 us
    all_to_all x2, waiting for transfers between devices, exchanged(): return lax.all_to_all(x, 'seq', split_axis=0, concat_axis=0, tiled=True)  9.48 us
  transfers between devices with their start and end apart: 22, of which 7 were waited for; matrix products, arithmetic and copies ran while one was open for 1% of the time, Pallas kernels for 13%

profile of v2, /device:TPU:12, one launch (start us, length us, event | category | flops | bytes accessed | tf_op | source)
XLA Modules:
  0.0 188.4 jit_solution(8782198345983510947)
XLA Ops:
  13.8 23.2 %conditional.3 = (bf16[16,208,128]{2,1,0:T(8,128)(2,1)}, bf16[16,32,768]{2,1,0:T(8,128)(2,1)}) conditional(s32[]{:T(128)} %convert_element_type.2, () %tuple.36, bf16[16,208,128]{2,1,0:T(8,128)(2,1)S(1)} %rows.1), branch_computations={%region_0.0_spmd, %region_1.0_spmd} | conditional | flops 1 | bytes 1703953 | solution.py:349
  13.8 20.4 %all_to_all.18.x = bf16[16,208,128]{2,1,0:T(8,128)(2,1)} all-to-all(bf16[16,208,128]{2,1,0:T(8,128)(2,1)S(1)} %param.1), channel_id=1, replica_groups=mesh['pipe'=2,'seq'=16] {'seq'}, dimensions={0} | all-to-all | bytes 1703936 | tf_op jit(solution)/shard_map/cond/branch_1_fun/all_to_all | solution.py:331
  34.2 2.8 %mix.2 = bf16[16,32,768]{2,1,0:T(8,128)(2,1)} custom-call(bf16[16,208,128]{2,1,0:T(8,128)(2,1)} %all_to_all.18.x), custom_call_target="tpu_custom_call" | custom-call | flops 1 | bytes 1 | tf_op jit(solution)/shard_map/cond/branch_1_fun/mix/pallas_call | solution.py:104
  37.1 5.8 %all-to-all-start.2 = ((bf16[16,32,768]{2,1,0:T(8,128)(2,1)}), bf16[16,32,768]{2,1,0:T(8,128)(2,1)}, u32[]{:S(2)}, u32[]{:S(2)}) async-start(bf16[16,32,768]{2,1,0:T(8,128)(2,1)} %get-tuple-element.110), calls=%async_computation.2 | async-start | bytes 1572864 | tf_op jit(solution)/shard_map/all_to_all | solution.py:331
  42.9 2.4 %collective-permute-start.13 = (bf16[688,256]{1,0:T(8,128)(2,1)S(1)}, bf16[688,256]{1,0:T(8,128)(2,1)S(1)}, u32[]{:S(2)}, u32[]{:S(2)}) collective-permute-start(bf16[688,256]{1,0:T(8,128)(2,1)S(1)} %pack.1.refs_1_.refs_0_), channel_id=1, source_target_pairs={{0,12},{1,13},{2,14},{3,15},{4,0},{5,1},{6,2},{7,3},{8,4},{9,5},{1... | collective-permute-start | bytes 1056776 | tf_op jit(solution)/shard_map/ppermute | solution.py:319
  45.3 4.3 %collective-permute-start.12 = (bf16[688,256]{1,0:T(8,128)(2,1)S(1)}, bf16[688,256]{1,0:T(8,128)(2,1)}, u32[]{:S(2)}, u32[]{:S(2)}) collective-permute-start(bf16[688,256]{1,0:T(8,128)(2,1)S(1)} %pack.1.refs_1_.refs_0_), channel_id=1, source_target_pairs={{0,8},{1,9},{2,10},{3,11},{4,12},{5,13},{6,14},{7,15},{8,0},{9,1},... | collective-permute-start | bytes 1056776 | tf_op jit(solution)/shard_map/ppermute | solution.py:319
  49.7 4.3 %collective-permute-start.11 = (bf16[688,256]{1,0:T(8,128)(2,1)S(1)}, bf16[688,256]{1,0:T(8,128)(2,1)}, u32[]{:S(2)}, u32[]{:S(2)}) collective-permute-start(bf16[688,256]{1,0:T(8,128)(2,1)S(1)} %pack.1.refs_1_.refs_0_), channel_id=1, source_target_pairs={{0,4},{1,5},{2,6},{3,7},{4,8},{5,9},{6,10},{7,11},{8,12},{9,13},{1... | collective-permute-start | bytes 1056776 | tf_op jit(solution)/shard_map/ppermute | solution.py:319
  54.0 3.2 %forward.2 = (bf16[1024,768]{1,0:T(8,128)(2,1)}, bf16[1024,768]{1,0:T(8,128)(2,1)}) custom-call(bf16[1,1024,768]{2,1,0:T(8,128)(2,1)} %refs_0_.3, bf16[688,256]{1,0:T(8,128)(2,1)S(1)} %pack.1.refs_1_.refs_0_, bf16[688,256]{1,0:T(8,128)(2,1)S(1)} %collective-permute-done.2.refs_0_.refs_2_, bf16[688,256]{1,0:T(8,128)(2,1)S(1)} %collective-permute-done.3.refs_1_.refs_3_, ...), custom_call_target="tpu_custom_call" | custom-call | flops 1 | bytes 1 | tf_op jit(solution)/shard_map/forward/pallas_call | solution.py:195
  57.3 16.4 %collective-permute-done.13.refs_3_ = bf16[688,256]{1,0:T(8,128)(2,1)S(1)} collective-permute-done((bf16[688,256]{1,0:T(8,128)(2,1)S(1)}, bf16[688,256]{1,0:T(8,128)(2,1)S(1)}, u32[]{:S(2)}, u32[]{:S(2)}) %collective-permute-start.13) | collective-permute-done | bytes 352288 | tf_op jit(solution)/shard_map/ppermute | solution.py:319
  75.5 2.5 %stack.3.refs_1_.refs_5_ = bf16[2752,256]{1,0:T(8,128)(2,1)} custom-call(bf16[688,256]{1,0:T(8,128)(2,1)S(1)} %pack.1.refs_1_.refs_0_, bf16[688,256]{1,0:T(8,128)(2,1)} %collective-permute-done.11.refs_1_, bf16[688,256]{1,0:T(8,128)(2,1)} %collective-permute-done.12.refs_2_, bf16[688,256]{1,0:T(8,128)(2,1)} %copy-done.4), custom_call_target="tpu_custom_call" | custom-call | flops 1 | bytes 1 | tf_op jit(solution)/shard_map/stack/pallas_call | solution.py:137
  78.0 18.7 %collective-permute-start.14 = (bf16[512,768]{1,0:T(8,128)(2,1)}, bf16[512,768]{1,0:T(8,128)(2,1)}, u32[]{:S(2)}, u32[]{:S(2)}) collective-permute-start(bf16[512,768]{1,0:T(8,128)(2,1)} %bitcast.2), channel_id=1, source_target_pairs={{0,16},{1,17},{2,18},{3,19},{4,20},{5,21},{6,22},{7,23},{8,24},{9,... | collective-permute-start | bytes 2359304 | tf_op jit(solution)/shard_map/ppermute | solution.py:375
  98.0 3.4 %collective-permute-start.17 = (bf16[2752,256]{1,0:T(8,128)(2,1)}, bf16[2752,256]{1,0:T(8,128)(2,1)}, u32[]{:S(2)}, u32[]{:S(2)}) collective-permute-start(bf16[2752,256]{1,0:T(8,128)(2,1)} %stack.3.refs_1_.refs_5_), channel_id=1, source_target_pairs={{0,3},{1,2},{2,1},{3,0},{4,7},{5,6},{6,5},{7,4},{8,11},{9,10},{10,... | collective-permute-start | bytes 4227080 | tf_op jit(solution)/shard_map/ppermute | solution.py:319
  101.4 3.4 %collective-permute-start.16 = (bf16[2752,256]{1,0:T(8,128)(2,1)}, bf16[2752,256]{1,0:T(8,128)(2,1)}, u32[]{:S(2)}, u32[]{:S(2)}) collective-permute-start(bf16[2752,256]{1,0:T(8,128)(2,1)} %stack.3.refs_1_.refs_5_), channel_id=1, source_target_pairs={{0,2},{1,3},{2,0},{3,1},{4,6},{5,7},{6,4},{7,5},{8,10},{9,11},{10,... | collective-permute-start | bytes 4227080 | tf_op jit(solution)/shard_map/ppermute | solution.py:319
  104.7 2.5 %collective-permute-start.15 = (bf16[2752,256]{1,0:T(8,128)(2,1)}, bf16[2752,256]{1,0:T(8,128)(2,1)}, u32[]{:S(2)}, u32[]{:S(2)}) collective-permute-start(bf16[2752,256]{1,0:T(8,128)(2,1)} %stack.3.refs_1_.refs_5_), channel_id=1, source_target_pairs={{0,1},{1,0},{2,3},{3,2},{4,5},{5,4},{6,7},{7,6},{8,9},{9,8},{10,11... | collective-permute-start | bytes 4227080 | tf_op jit(solution)/shard_map/ppermute | solution.py:319
  107.3 11.7 %conditional.4 = (bf16[512,768]{1,0:T(8,128)(2,1)}, bf16[512,768]{1,0:T(8,128)(2,1)}, bf16[512,768]{1,0:T(8,128)(2,1)}, bf16[16,32,768]{2,1,0:T(8,128)(2,1)S(1)}) conditional(s32[]{:T(128)} %convert_element_type.2, () %tuple.35, (f32[1,1,1024]{2,1,0:T(1,128)S(1)}, bf16[512,768]{1,0:T(8,128)(2,1)}, bf16[512,768]{1,0:T(8,128)(2,1)}, ...), branch_computations={%region_2.0_spmd, %region_3.4_spmd} | conditional | flops 5234884608 | bytes 19505104 | solution.py:349
  109.0 8.8 %collective-permute-done = bf16[512,768]{1,0:T(8,128)(2,1)} collective-permute-done((bf16[512,768]{1,0:T(8,128)(2,1)}, bf16[512,768]{1,0:T(8,128)(2,1)}, u32[]{:S(2)}, u32[]{:S(2)}) %collective-permute-start) | collective-permute-done | bytes 786464 | tf_op jit(solution)/shard_map/cond/branch_1_fun/ppermute | solution.py:380
  119.0 29.3 %conditional.5 = (bf16[16,32,768]{2,1,0:T(8,128)(2,1)}) conditional(s32[]{:T(128)} %convert_element_type.2, () %tuple.34, (bf16[16,32,768]{2,1,0:T(8,128)(2,1)S(1)}, bf16[16,208,128]{2,1,0:T(8,128)(2,1)}) %tuple.43), branch_computations={%region_4.5_spmd, %region_5.6_spmd} | conditional | flops 1 | bytes 1572873 | solution.py:349
  119.0 26.7 %all_to_all.19.x = bf16[16,32,768]{2,1,0:T(8,128)(2,1)} all-to-all(bf16[16,32,768]{2,1,0:T(8,128)(2,1)S(1)} %get-tuple-element.67), channel_id=1, replica_groups=mesh['pipe'=2,'seq'=16] {'seq'}, dimensions={0} | all-to-all | bytes 1572864 | tf_op jit(solution)/shard_map/cond/branch_1_fun/all_to_all | solution.py:331
  145.6 2.6 %mix.3 = bf16[16,32,768]{2,1,0:T(8,128)(2,1)} custom-call(bf16[16,208,128]{2,1,0:T(8,128)(2,1)} %get-tuple-element.66.left, bf16[16,32,768]{2,1,0:T(8,128)(2,1)} %all_to_all.19.x), custom_call_target="tpu_custom_call" | custom-call | flops 1 | bytes 1 | tf_op jit(solution)/shard_map/cond/branch_1_fun/mix/pallas_call | solution.py:115
  148.3 5.3 %all-to-all-start.3 = ((bf16[16,32,768]{2,1,0:T(8,128)(2,1)}), bf16[16,32,768]{2,1,0:T(8,128)(2,1)S(1)}, u32[]{:S(2)}, u32[]{:S(2)}) async-start(bf16[16,32,768]{2,1,0:T(8,128)(2,1)} %get-tuple-element.154), calls=%async_computation.3 | async-start | bytes 1572864 | tf_op jit(solution)/shard_map/all_to_all | solution.py:331
  154.9 8.1 %forward.3 = (bf16[1024,768]{1,0:T(8,128)(2,1)}, bf16[1024,768]{1,0:T(8,128)(2,1)}) custom-call(bf16[1,1024,768]{2,1,0:T(8,128)(2,1)} %refs_0_.3, bf16[2752,256]{1,0:T(8,128)(2,1)} %stack.3.refs_1_.refs_5_, bf16[2752,256]{1,0:T(8,128)(2,1)} %collective-permute-done.15.refs_2_.refs_6_, bf16[2752,256]{1,0:T(8,128)(2,1)} %collective-permute-done.16.refs_3_.refs_7_, ...), custom_call_target="tpu_custom_call" | custom-call | flops 1 | bytes 1 | tf_op jit(solution)/shard_map/forward/pallas_call | solution.py:195
  163.0 9.5 %all-to-all-done.3 = bf16[16,32,768]{2,1,0:T(8,128)(2,1)S(1)} async-done(((bf16[16,32,768]{2,1,0:T(8,128)(2,1)}), bf16[16,32,768]{2,1,0:T(8,128)(2,1)S(1)}, u32[]{:S(2)}, u32[]{:S(2)}) %all-to-all-start.3) | async-done | bytes 786464 | tf_op jit(solution)/shard_map/all_to_all | solution.py:331
  173.7 2.9 %collective-permute-done.19.refs_1_ = bf16[512,768]{1,0:T(8,128)(2,1)S(1)} collective-permute-done((bf16[512,768]{1,0:T(8,128)(2,1)S(1)}, bf16[512,768]{1,0:T(8,128)(2,1)S(1)}, u32[]{:S(2)}, u32[]{:S(2)}) %collective-permute-start.19) | collective-permute-done | bytes 786464 | tf_op jit(solution)/shard_map/ppermute | solution.py:391
  177.5 10.8 %layer.3 = bf16[1024,768]{1,0:T(8,128)(2,1)} custom-call(bf16[512,768]{1,0:T(8,128)(2,1)} %bitcast.8, bf16[512,768]{1,0:T(8,128)(2,1)} %copy-done.7, f32[1,1024]{1,0:T(1,128)S(1)} %bitcast.9, bf16[1024,768]{1,0:T(8,128)(2,1)} %get-tuple-element.137.refs_3_, bf16[1024,768]{1,0:T(8,128)(2,1)} %get-tuple-element.138.refs_4_, ...), custom_call_target="tpu_custom_call" | custom-call | flops 5234491392 | bytes 14000000 | tf_op jit(solution)/shard_map/layer/pallas_call | solution.py:303
  (54 shorter events, 23.2 us)
Async XLA Ops:
  0.0 1.3 collective-permute-start.1
  1.3 3.4 %collective-permute-start.4 = (bf16[688,256]{1,0:T(8,128)(2,1)S(1)}, bf16[688,256]{1,0:T(8,128)(2,1)S(1)}, u32[]{:S(2)}, u32[]{:S(2)}) collective-permute-start(bf16[688,256]{1,0:T(8,128)(2,1)S(1)} %pack.1.refs_1_.refs_0_), channel_id=1, source_target_pairs={{16,28},{17,29},{18,30},{19,31},{20,16},{21,17},{22,18},{23,19},{2... | collective-permute-start | bytes 1056776 | tf_op jit(solution)/shard_map/ppermute | solution.py:319
  1.9 5.4 %collective-permute-start.3 = (bf16[688,256]{1,0:T(8,128)(2,1)S(1)}, bf16[688,256]{1,0:T(8,128)(2,1)S(1)}, u32[]{:S(2)}, u32[]{:S(2)}) collective-permute-start(bf16[688,256]{1,0:T(8,128)(2,1)S(1)} %pack.1.refs_1_.refs_0_), channel_id=1, source_target_pairs={{16,24},{17,25},{18,26},{19,27},{20,28},{21,29},{22,30},{23,31},{2... | collective-permute-start | bytes 1056776 | tf_op jit(solution)/shard_map/ppermute | solution.py:319
  2.6 4.8 %collective-permute-start.2 = (bf16[688,256]{1,0:T(8,128)(2,1)S(1)}, bf16[688,256]{1,0:T(8,128)(2,1)S(1)}, u32[]{:S(2)}, u32[]{:S(2)}) collective-permute-start(bf16[688,256]{1,0:T(8,128)(2,1)S(1)} %pack.1.refs_1_.refs_0_), channel_id=1, source_target_pairs={{16,20},{17,21},{18,22},{19,23},{20,24},{21,25},{22,26},{23,27},{2... | collective-permute-start | bytes 1056776 | tf_op jit(solution)/shard_map/ppermute | solution.py:319
  3.3 5.5 %collective-permute-start.7 = (bf16[688,256]{1,0:T(8,128)(2,1)S(1)}, bf16[688,256]{1,0:T(8,128)(2,1)S(1)}, u32[]{:S(2)}, u32[]{:S(2)}) collective-permute-start(bf16[688,256]{1,0:T(8,128)(2,1)S(1)} %pack.1.refs_1_.refs_0_), channel_id=1, source_target_pairs={{16,19},{17,18},{18,17},{19,16},{20,23},{21,22},{22,21},{23,20},{2... | collective-permute-start | bytes 1056776 | tf_op jit(solution)/shard_map/ppermute | solution.py:319
  4.0 4.8 %collective-permute-start.6 = (bf16[688,256]{1,0:T(8,128)(2,1)S(1)}, bf16[688,256]{1,0:T(8,128)(2,1)S(1)}, u32[]{:S(2)}, u32[]{:S(2)}) collective-permute-start(bf16[688,256]{1,0:T(8,128)(2,1)S(1)} %pack.1.refs_1_.refs_0_), channel_id=1, source_target_pairs={{16,18},{17,19},{18,16},{19,17},{20,22},{21,23},{22,20},{23,21},{2... | collective-permute-start | bytes 1056776 | tf_op jit(solution)/shard_map/ppermute | solution.py:319
  4.7 4.1 %collective-permute-start.5 = (bf16[688,256]{1,0:T(8,128)(2,1)S(1)}, bf16[688,256]{1,0:T(8,128)(2,1)S(1)}, u32[]{:S(2)}, u32[]{:S(2)}) collective-permute-start(bf16[688,256]{1,0:T(8,128)(2,1)S(1)} %pack.1.refs_1_.refs_0_), channel_id=1, source_target_pairs={{16,17},{17,16},{18,19},{19,18},{20,21},{21,20},{22,23},{23,22},{2... | collective-permute-start | bytes 1056776 | tf_op jit(solution)/shard_map/ppermute | solution.py:319
  8.9 28.2 %collective-permute-start.10 = (bf16[2064,256]{1,0:T(8,128)(2,1)}, bf16[2064,256]{1,0:T(8,128)(2,1)}, u32[]{:S(2)}, u32[]{:S(2)}) collective-permute-start(bf16[2064,256]{1,0:T(8,128)(2,1)} %stack.2), channel_id=1, source_target_pairs={{16,19},{17,18},{18,17},{19,16},{20,23},{21,22},{22,21},{23,20},{2... | collective-permute-start | bytes 3170312 | tf_op jit(solution)/shard_map/ppermute | solution.py:319
  10.5 26.5 %collective-permute-start.9 = (bf16[2064,256]{1,0:T(8,128)(2,1)}, bf16[2064,256]{1,0:T(8,128)(2,1)}, u32[]{:S(2)}, u32[]{:S(2)}) collective-permute-start(bf16[2064,256]{1,0:T(8,128)(2,1)} %stack.2), channel_id=1, source_target_pairs={{16,18},{17,19},{18,16},{19,17},{20,22},{21,23},{22,20},{23,21},{2... | collective-permute-start | bytes 3170312 | tf_op jit(solution)/shard_map/ppermute | solution.py:319
  12.2 24.9 %collective-permute-start.8 = (bf16[2064,256]{1,0:T(8,128)(2,1)}, bf16[2064,256]{1,0:T(8,128)(2,1)}, u32[]{:S(2)}, u32[]{:S(2)}) collective-permute-start(bf16[2064,256]{1,0:T(8,128)(2,1)} %stack.2), channel_id=1, source_target_pairs={{16,17},{17,16},{18,19},{19,18},{20,21},{21,20},{22,23},{23,22},{2... | collective-permute-start | bytes 3170312 | tf_op jit(solution)/shard_map/ppermute | solution.py:319
  37.1 40.9 %all-to-all-start.2 = ((bf16[16,32,768]{2,1,0:T(8,128)(2,1)}), bf16[16,32,768]{2,1,0:T(8,128)(2,1)}, u32[]{:S(2)}, u32[]{:S(2)}) async-start(bf16[16,32,768]{2,1,0:T(8,128)(2,1)} %get-tuple-element.110), calls=%async_computation.2 | async-start | bytes 1572864 | tf_op jit(solution)/shard_map/all_to_all | solution.py:331
  42.9 30.8 %collective-permute-start.13 = (bf16[688,256]{1,0:T(8,128)(2,1)S(1)}, bf16[688,256]{1,0:T(8,128)(2,1)S(1)}, u32[]{:S(2)}, u32[]{:S(2)}) collective-permute-start(bf16[688,256]{1,0:T(8,128)(2,1)S(1)} %pack.1.refs_1_.refs_0_), channel_id=1, source_target_pairs={{0,12},{1,13},{2,14},{3,15},{4,0},{5,1},{6,2},{7,3},{8,4},{9,5},{1... | collective-permute-start | bytes 1056776 | tf_op jit(solution)/shard_map/ppermute | solution.py:319
  45.3 28.3 %collective-permute-start.12 = (bf16[688,256]{1,0:T(8,128)(2,1)S(1)}, bf16[688,256]{1,0:T(8,128)(2,1)}, u32[]{:S(2)}, u32[]{:S(2)}) collective-permute-start(bf16[688,256]{1,0:T(8,128)(2,1)S(1)} %pack.1.refs_1_.refs_0_), channel_id=1, source_target_pairs={{0,8},{1,9},{2,10},{3,11},{4,12},{5,13},{6,14},{7,15},{8,0},{9,1},... | collective-permute-start | bytes 1056776 | tf_op jit(solution)/shard_map/ppermute | solution.py:319
  49.7 25.8 %collective-permute-start.11 = (bf16[688,256]{1,0:T(8,128)(2,1)S(1)}, bf16[688,256]{1,0:T(8,128)(2,1)}, u32[]{:S(2)}, u32[]{:S(2)}) collective-permute-start(bf16[688,256]{1,0:T(8,128)(2,1)S(1)} %pack.1.refs_1_.refs_0_), channel_id=1, source_target_pairs={{0,4},{1,5},{2,6},{3,7},{4,8},{5,9},{6,10},{7,11},{8,12},{9,13},{1... | collective-permute-start | bytes 1056776 | tf_op jit(solution)/shard_map/ppermute | solution.py:319
  57.2 50.0 %copy-start = (bf16[1024,768]{1,0:T(8,128)(2,1)S(1)}, bf16[1024,768]{1,0:T(8,128)(2,1)}, u32[]{:S(2)}) copy-start(bf16[1024,768]{1,0:T(8,128)(2,1)} %grad.1) | copy-start | bytes 4718596
  57.2 50.0 %copy-start.8 = (f32[1,1,1024]{2,1,0:T(1,128)S(1)}, f32[1,1,1024]{2,1,0:T(1,128)}, u32[]{:S(2)}) copy-start(f32[1,1,1024]{2,1,0:T(1,128)} %param.21) | copy-start | bytes 12292
  78.0 20.0 %collective-permute-start.14 = (bf16[512,768]{1,0:T(8,128)(2,1)}, bf16[512,768]{1,0:T(8,128)(2,1)}, u32[]{:S(2)}, u32[]{:S(2)}) collective-permute-start(bf16[512,768]{1,0:T(8,128)(2,1)} %bitcast.2), channel_id=1, source_target_pairs={{0,16},{1,17},{2,18},{3,19},{4,20},{5,21},{6,22},{7,23},{8,24},{9,... | collective-permute-start | bytes 2359304 | tf_op jit(solution)/shard_map/ppermute | solution.py:375
  98.0 50.3 %collective-permute-start.17 = (bf16[2752,256]{1,0:T(8,128)(2,1)}, bf16[2752,256]{1,0:T(8,128)(2,1)}, u32[]{:S(2)}, u32[]{:S(2)}) collective-permute-start(bf16[2752,256]{1,0:T(8,128)(2,1)} %stack.3.refs_1_.refs_5_), channel_id=1, source_target_pairs={{0,3},{1,2},{2,1},{3,0},{4,7},{5,6},{6,5},{7,4},{8,11},{9,10},{10,... | collective-permute-start | bytes 4227080 | tf_op jit(solution)/shard_map/ppermute | solution.py:319
  101.4 46.9 %collective-permute-start.16 = (bf16[2752,256]{1,0:T(8,128)(2,1)}, bf16[2752,256]{1,0:T(8,128)(2,1)}, u32[]{:S(2)}, u32[]{:S(2)}) collective-permute-start(bf16[2752,256]{1,0:T(8,128)(2,1)} %stack.3.refs_1_.refs_5_), channel_id=1, source_target_pairs={{0,2},{1,3},{2,0},{3,1},{4,6},{5,7},{6,4},{7,5},{8,10},{9,11},{10,... | collective-permute-start | bytes 4227080 | tf_op jit(solution)/shard_map/ppermute | solution.py:319
  104.7 43.5 %collective-permute-start.15 = (bf16[2752,256]{1,0:T(8,128)(2,1)}, bf16[2752,256]{1,0:T(8,128)(2,1)}, u32[]{:S(2)}, u32[]{:S(2)}) collective-permute-start(bf16[2752,256]{1,0:T(8,128)(2,1)} %stack.3.refs_1_.refs_5_), channel_id=1, source_target_pairs={{0,1},{1,0},{2,3},{3,2},{4,5},{5,4},{6,7},{7,6},{8,9},{9,8},{10,11... | collective-permute-start | bytes 4227080 | tf_op jit(solution)/shard_map/ppermute | solution.py:319
  107.6 10.1 %collective-permute-start = (bf16[512,768]{1,0:T(8,128)(2,1)}, bf16[512,768]{1,0:T(8,128)(2,1)}, u32[]{:S(2)}, u32[]{:S(2)}) collective-permute-start(bf16[512,768]{1,0:T(8,128)(2,1)} %get-tuple-element.150), channel_id=1, source_target_pairs={{16,0},{17,1},{18,2},{19,3},{20,4},{21,5},{22,6},{23,7},{24,8},{25... | collective-permute-start | bytes 2359304 | tf_op jit(solution)/shard_map/cond/branch_1_fun/ppermute | solution.py:380
  148.3 24.2 %all-to-all-start.3 = ((bf16[16,32,768]{2,1,0:T(8,128)(2,1)}), bf16[16,32,768]{2,1,0:T(8,128)(2,1)S(1)}, u32[]{:S(2)}, u32[]{:S(2)}) async-start(bf16[16,32,768]{2,1,0:T(8,128)(2,1)} %get-tuple-element.154), calls=%async_computation.3 | async-start | bytes 1572864 | tf_op jit(solution)/shard_map/all_to_all | solution.py:331
  153.6 9.4 %collective-permute-start.18 = (bf16[512,768]{1,0:T(8,128)(2,1)}, bf16[512,768]{1,0:T(8,128)(2,1)S(1)}, u32[]{:S(2)}, u32[]{:S(2)}) collective-permute-start(bf16[512,768]{1,0:T(8,128)(2,1)} %get-tuple-element.135.refs_12_), channel_id=1, source_target_pairs={{16,0},{17,1},{18,2},{19,3},{20,4},{21,5},{22,6},{23,7},{24,8},{25... | collective-permute-start | bytes 2359304 | tf_op jit(solution)/shard_map/ppermute | solution.py:387
  172.5 4.2 %collective-permute-start.19 = (bf16[512,768]{1,0:T(8,128)(2,1)S(1)}, bf16[512,768]{1,0:T(8,128)(2,1)S(1)}, u32[]{:S(2)}, u32[]{:S(2)}) collective-permute-start(bf16[512,768]{1,0:T(8,128)(2,1)S(1)} %bitcast.7), channel_id=1, source_target_pairs={{16,0},{17,1},{18,2},{19,3},{20,4},{21,5},{22,6},{23,7},{24,8},{25... | collective-permute-start | bytes 2359304 | tf_op jit(solution)/shard_map/ppermute | solution.py:391
  (7 other events, 113.9 us)

commit v3 on v2

v3 whole, which is shorter than its diff:
```python
import jax
import jax.numpy as jnp
from jax import lax
from jax.experimental import pallas as pl
from jax.experimental.pallas import tpu as pltpu
from jax.sharding import PartitionSpec as P

BF = jnp.bfloat16
F32 = jnp.float32
SHARDS = 16
ANY = pl.BlockSpec(memory_space=pl.ANY)
VMEM = pl.BlockSpec(memory_space=pltpu.VMEM)
LIGHT = pl.CostEstimate(flops=1, bytes_accessed=1, transcendentals=0)
PARAMS = pltpu.CompilerParams(vmem_limit_bytes=62 * 1024 * 1024)

RIGHT, OUT, VALUE, GATE, ROWS = 0, 256, 400, 544, 688


def dot_nn(a, b):
    return lax.dot_general(a, b, (((1,), (0,)), ((), ())), preferred_element_type=F32)


def dot_nt(a, b):
    return lax.dot_general(a, b, (((1,), (1,)), ((), ())), preferred_element_type=F32)


def dot_tn(a, b):
    return lax.dot_general(a, b, (((0,), (0,)), ((), ())), preferred_element_type=F32)


def pack_kernel(right, out, value, gate, blob):
    for g in range(4):
        blob[RIGHT + 64 * g : RIGHT + 64 * g + 64, :] = right[0, :, 256 * g : 256 * g + 256]
    for base, ref in ((OUT, out), (VALUE, value), (GATE, gate)):
        for g in range(3):
            blob[base + 48 * g : base + 48 * g + 48, :] = ref[0, :, 256 * g : 256 * g + 256]


def pack(right, out, value, gate):
    return pl.pallas_call(
        pack_kernel,
        out_shape=jax.ShapeDtypeStruct((ROWS, 256), BF),
        in_specs=[VMEM] * 4,
        out_specs=VMEM,
        name="pack",
        cost_estimate=LIGHT,
    )(right, out, value, gate)


GROUPS = 25


def group_copies(block, out, sems, first, count):
    return [
        pltpu.make_async_copy(
            block.at[pl.ds(first, count), :, :, pl.ds(128 * c, 128)],
            out.at[pl.ds(first, count), pl.ds(4 * c, 4)],
            sems.at[c],
        )
        for c in range(6)
    ]


def factor_group(factor, tail, out, sem):
    tail[...] = jnp.zeros((SHARDS, 16, 128), BF)
    tail[:, :, 0:16] = jnp.broadcast_to(factor[0], (SHARDS, 16, 16))
    return pltpu.make_async_copy(tail, out.at[:, GROUPS - 1], sem)


def rows_kernel(section, source, factor, out, block, tail, sems):
    @pl.when(lax.axis_index("pipe") != section)
    def _():
        loads = [pltpu.make_async_copy(source.at[pl.ds(8 * t, 8)], block.at[pl.ds(8 * t, 8)], sems.at[t]) for t in range(2)]
        for c in loads:
            c.start()
        stores = [factor_group(factor, tail, out, sems.at[2])]
        stores[0].start()
        for t in range(2):
            loads[t].wait()
            copies = group_copies(block, out, sems.at[pl.ds(3 + 6 * t, 6)], 8 * t, 8)
            for c in copies:
                c.start()
            stores += copies
        for c in stores:
            c.wait()


def rows_to_send(section, source, factor):
    return pl.pallas_call(
        lambda *refs: rows_kernel(section, *refs),
        out_shape=jax.ShapeDtypeStruct((SHARDS, GROUPS, 16, 128), BF),
        in_specs=[ANY, VMEM],
        out_specs=ANY,
        scratch_shapes=[pltpu.VMEM((SHARDS, 4, 16, 768), BF), pltpu.VMEM((SHARDS, 16, 128), BF), pltpu.SemaphoreType.DMA((15,))],
        compiler_params=PARAMS,
        name="rows",
        cost_estimate=LIGHT,
    )(source.reshape(SHARDS, 4, 16, 768), factor)


def mix_kernel(left, x, y, matrix):
    @pl.when(pl.program_id(0) == 0)
    def _():
        rows = lax.broadcasted_iota(jnp.int32, (256, 16), 0)
        cols = lax.broadcasted_iota(jnp.int32, (256, 16), 1)
        spread = jnp.where(rows // 16 == cols, 1.0, 0.0).astype(BF)
        wide = dot_nt(dot_nt(spread, left[:, 0, 0, 0:16]).astype(BF), spread)
        at = lax.broadcasted_iota(jnp.int32, (256, 256), 0) % 16
        to = lax.broadcasted_iota(jnp.int32, (256, 256), 1) % 16
        matrix[...] = jnp.where(at == to, wide, 0.0).astype(BF)

    for q in range(4):
        part = jnp.concatenate([x[:, 4 * c + q, :, :].reshape(256, 128) for c in range(2)], axis=1)
        y[:, 16 * q : 16 * q + 16, :] = dot_nn(matrix[...], part).astype(BF).reshape(16, 16, 256)


def mix(x):
    return pl.pallas_call(
        mix_kernel,
        grid=(3,),
        out_shape=jax.ShapeDtypeStruct((SHARDS, 64, 768), BF),
        in_specs=[
            pl.BlockSpec((SHARDS, 1, 16, 128), lambda i: (0, GROUPS - 1, 0, 0)),
            pl.BlockSpec((SHARDS, 8, 16, 128), lambda i: (0, i, 0, 0)),
        ],
        out_specs=pl.BlockSpec((SHARDS, 64, 256), lambda i: (0, 0, i)),
        scratch_shapes=[pltpu.VMEM((256, 256), BF)],
        name="mix",
        cost_estimate=LIGHT,
    )(x, x)


def stack_kernel(section, n, *refs):
    ins, out, scratch, sems = refs[:n], refs[n], refs[n + 1], refs[n + 2]

    @pl.when(lax.axis_index("pipe") == section)
    def _():
        copies = [pltpu.make_async_copy(r, scratch.at[pl.ds(ROWS * i, ROWS), :], sems.at[i]) for i, r in enumerate(ins)]
        stores = [
            pltpu.make_async_copy(scratch.at[pl.ds(ROWS * i, ROWS), :], out.at[pl.ds(ROWS * i, ROWS), :], sems.at[n + i])
            for i in range(n)
        ]
        for c in copies:
            c.start()
        for c, d in zip(copies, stores):
            c.wait()
            d.start()
        for d in stores:
            d.wait()


def stacked(section, *parts):
    n = len(parts)
    return pl.pallas_call(
        lambda *refs: stack_kernel(section, n, *refs),
        out_shape=jax.ShapeDtypeStruct((ROWS * n, 256), BF),
        in_specs=[ANY] * n,
        out_specs=ANY,
        scratch_shapes=[pltpu.VMEM((ROWS * n, 256), BF), pltpu.SemaphoreType.DMA((2 * n,))],
        compiler_params=PARAMS,
        name="stack",
        cost_estimate=LIGHT,
    )(*parts)


def weight_copies(pieces, refs, scratch, sems, first, count):
    seq = lax.axis_index("seq")
    z, place = seq // 4, seq % 4
    copies = []
    for (at, shift, step, offset), ref in zip(pieces, refs):
        del at
        for n, k in enumerate(shift):
            shard = lax.rem(z - k + 4, 4) * 4 + jnp.bitwise_xor(place, step)
            copies.append(
                pltpu.make_async_copy(
                    ref.at[pl.ds(offset + n * ROWS + first, count), :],
                    scratch.at[shard, pl.ds(first, count), :],
                    sems.at[len(copies)],
                )
            )
    assert len(copies) == SHARDS
    return copies


def lanes_of(scratch, base, rows, groups):
    parts = [scratch[:, base + rows * g : base + rows * g + rows, :].reshape(SHARDS * rows, 256) for g in range(groups)]
    return jnp.concatenate(parts, axis=1)


def forward_work(pieces, n_refs, *refs):
    x, twiddle, weights, refs = refs[0], refs[1], refs[2 : 2 + n_refs], refs[2 + n_refs :]
    active, slope, turning, gathered, scratch, rows_in, act, slo, right, sem_w, sem, sem_out = refs
    loads = [pltpu.make_async_copy(x.at[0, pl.ds(512 * t, 512)], rows_in.at[pl.ds(512 * t, 512)], sem.at[t]) for t in range(2)]
    copies = weight_copies(pieces, weights, scratch, sem_w, 0, ROWS)
    for c in loads[:1] + copies + loads[1:]:
        c.start()
    for c in copies:
        c.wait()
    stores = []

    def store(source, target):
        stores.append(pltpu.make_async_copy(source, target, sem_out.at[len(stores)]))
        stores[-1].start()

    store(scratch.at[:, pl.ds(OUT, ROWS - OUT), :], gathered)
    for t in range(2):
        loads[t].wait()
        rows = slice(512 * t, 512 * t + 512)
        for e in range(3):
            lanes = slice(256 * e, 256 * e + 256)
            value = scratch[:, VALUE + 48 * e : VALUE + 48 * e + 48, :].reshape(768, 256)
            gate = scratch[:, GATE + 48 * e : GATE + 48 * e + 48, :].reshape(768, 256)
            values = dot_nn(rows_in[rows, :], value).astype(BF).astype(F32)
            gates = dot_nn(rows_in[rows, :], gate).astype(BF).astype(F32)
            sigma = 0.5 + 0.5 * jnp.tanh(0.5 * gates)
            on = gates * sigma
            act[rows, lanes] = on.astype(BF)
            slo[rows, lanes] = ((sigma + on * (1.0 - sigma)) * values).astype(BF)
            step = 3 * t + e
            if step in (0, 1, 3, 4):
                g = (0, 1, 0, 2, 3)[step]
                part = scratch[:, RIGHT + 64 * g : RIGHT + 64 * g + 64, :].reshape(1024, 256)
                right[256 * g : 256 * g + 256, :] = (part.T.astype(F32) * twiddle[...]).astype(BF)
        store(act.at[rows], active.at[rows])
        store(slo.at[rows], slope.at[rows])
        store(right.at[rows], turning.at[rows])
    for c in stores:
        c.wait()


def forward_kernel(section, pieces, n_refs, *refs):
    @pl.when(lax.axis_index("pipe") == section)
    def _():
        forward_work(pieces, n_refs, *refs)


def forward(section, x, twiddle, pieces, weights):
    shape = jax.ShapeDtypeStruct((1024, 768), BF)
    square = jax.ShapeDtypeStruct((1024, 1024), BF)
    rows = jax.ShapeDtypeStruct((SHARDS, ROWS - OUT, 256), BF)
    big = pltpu.VMEM((1024, 768), BF)
    return pl.pallas_call(
        lambda *refs: forward_kernel(section, pieces, len(weights), *refs),
        out_shape=(shape, shape, square, rows),
        in_specs=[ANY, VMEM] + [ANY] * len(weights),
        out_specs=(ANY,) * 4,
        scratch_shapes=[pltpu.VMEM((SHARDS, ROWS, 256), BF), big, big, big, pltpu.VMEM((1024, 1024), BF)]
        + [pltpu.SemaphoreType.DMA((SHARDS,)), pltpu.SemaphoreType.DMA((2,)), pltpu.SemaphoreType.DMA((7,))],
        compiler_params=PARAMS,
        name="forward",
        cost_estimate=LIGHT,
    )(x, twiddle, *weights)


def layer_work(last, *refs):
    given, active, slope, turning, gathered, incoming = refs[:6]
    if last:
        result, refs = refs[7], refs[8:]
    else:
        factor, result, out, refs = refs[6], refs[7], refs[8], refs[9:]
    weights, left, right, inner, act, slo, base, total, sem, sem_out, *tail = refs
    halves = (slice(0, 512), slice(512, 1024))
    loads = []

    def load(source, target):
        loads.append(pltpu.make_async_copy(source, target, sem.at[len(loads)]))
        loads[-1].start()
        return loads[-1]

    part = load(given, left)
    rights = [load(turning.at[h], right.at[h]) for h in halves]
    part.wait()
    rights[0].wait()
    projections = load(gathered, weights)
    inner[halves[0], :] = dot_nn(right[halves[0], :], left[...]).astype(BF)
    gates = []
    for h in halves:
        gates += [load(active.at[h], act.at[h]), load(slope.at[h], slo.at[h]), load(incoming.at[h], base.at[h])]
    rights[1].wait()
    inner[halves[1], :] = dot_nn(right[halves[1], :], left[...]).astype(BF)
    projections.wait()
    stores = [] if last else [factor_group(factor, tail[0], out, sem_out.at[4])]
    for c in stores:
        c.start()
    for t in range(4):
        rows = slice(256 * t, 256 * t + 256)
        pieces = slice(4 * t, 4 * t + 4)
        right_part = dot_nt(inner[rows, :], lanes_of(weights, 0, 48, 3)).astype(BF).astype(F32)
        if t % 2 == 0:
            for c in gates[3 * (t // 2) : 3 * (t // 2) + 3]:
                c.wait()
        grad_value = (right_part * act[rows, :].astype(F32)).astype(BF)
        grad_gate = (right_part * slo[rows, :].astype(F32)).astype(BF)
        added = dot_nt(grad_value, lanes_of(weights, VALUE - OUT, 48, 3)) + dot_nt(grad_gate, lanes_of(weights, GATE - OUT, 48, 3))
        total[pieces] = (base[rows, :].astype(F32) + added).astype(BF).reshape(4, 4, 16, 768)
        copies = [pltpu.make_async_copy(total.at[pieces], result.at[pieces], sem_out.at[t])]
        if not last:
            copies += group_copies(total, out, sem_out.at[pl.ds(5 + 6 * t, 6)], 4 * t, 4)
        for c in copies:
            c.start()
        stores += copies
    for c in stores:
        c.wait()


def layer_kernel(section, last, *refs):
    pipe = lax.axis_index("pipe")

    @pl.when(pipe == section)
    def _():
        layer_work(last, *refs)

    if last:

        @pl.when(pipe != section)
        def _():
            own, result = refs[6], refs[7]
            total, sem, sem_out = refs[-3:]
            halves = [pl.ds(8 * t, 8) for t in range(2)]
            loads = [pltpu.make_async_copy(own.at[h], total.at[h], sem.at[t]) for t, h in enumerate(halves)]
            stores = [pltpu.make_async_copy(total.at[h], result.at[h], sem_out.at[t]) for t, h in enumerate(halves)]
            for c in loads:
                c.start()
            for load, store in zip(loads, stores):
                load.wait()
                store.start()
            for c in stores:
                c.wait()


def layer(section, left, gated, incoming, other, last):
    whole = jax.ShapeDtypeStruct((SHARDS, 4, 16, 768), BF)
    groups = jax.ShapeDtypeStruct((SHARDS, GROUPS, 16, 128), BF)
    big = pltpu.VMEM((1024, 768), BF)
    return pl.pallas_call(
        lambda *refs: layer_kernel(section, last, *refs),
        out_shape=whole if last else (whole, groups),
        in_specs=[ANY] * (2 + len(gated)) + [ANY if last else VMEM],
        out_specs=ANY if last else (ANY, ANY),
        scratch_shapes=[pltpu.VMEM((SHARDS, ROWS - OUT, 256), BF), big, pltpu.VMEM((1024, 1024), BF)]
        + [big] * 4
        + [pltpu.VMEM((SHARDS, 4, 16, 768), BF), pltpu.SemaphoreType.DMA((10,)), pltpu.SemaphoreType.DMA((29,))]
        + ([] if last else [pltpu.VMEM((SHARDS, 16, 128), BF)]),
        compiler_params=PARAMS,
        name="layer",
        cost_estimate=LIGHT,
    )(left, *gated, incoming, other)


def sent(x, section, to):
    pairs = [(section * SHARDS + s, section * SHARDS + to(s)) for s in range(SHARDS)]
    return lax.ppermute(x, ("pipe", "seq"), pairs)


def along_z(x, section, k):
    return sent(x, section, lambda s: ((s // 4 + k) % 4) * 4 + s % 4)


def in_plane(x, section, d):
    return sent(x, section, lambda s: s ^ d)


def exchanged(x):
    return lax.all_to_all(x, "seq", split_axis=0, concat_axis=0, tiled=True)


def tied(*xs):
    return lax.optimization_barrier(xs)


PIECES = (
    [(0, (0,), 0, 0)]
    + [(0, (k,), 0, 0) for k in (1, 2, 3)]
    + [(0, (0,), d, 0) for d in (1, 2, 3)]
    + [(0, (1, 2, 3), d, 0) for d in (1, 2, 3)]
)


def only_on(core, f, *args):
    shapes, tree = jax.tree.flatten(jax.eval_shape(f, *args))

    def idle(*_):
        arrays = pl.pallas_call(
            lambda *refs: None, out_shape=shapes, out_specs=[ANY] * len(shapes), name="idle", cost_estimate=LIGHT
        )()
        return jax.tree.unflatten(tree, arrays)

    return lax.cond(lax.axis_index("pipe") == core, f, idle, *args)


def mixed(rows):
    return exchanged(mix(exchanged(rows))).reshape(1024, 768)


def fast_body(inputs_saved, grad_out, value_weight, gate_weight, out_weight, right_factor, left_factor, twiddle):
    got_left = lax.ppermute(left_factor, "pipe", [(0, 1), (1, 0)])
    blob, got_left = tied(pack(right_factor, out_weight, value_weight, gate_weight), got_left)

    along = [along_z(blob, 1, k) for k in (1, 2, 3)]
    own = [in_plane(blob, 1, d) for d in (1, 2, 3)]
    rest, *own = tied(stacked(1, *along), *own)
    plane = [in_plane(rest, 1, d) for d in (1, 2, 3)]
    left = only_on(0, mixed, rows_to_send(1, grad_out, got_left))
    left, *plane = tied(left, *plane)
    gated = forward(1, inputs_saved, twiddle[0], PIECES, [blob, *along, *own, *plane])
    left, later_blob, *gated = tied(left, blob, *gated)
    got = lax.ppermute(left, "pipe", [(0, 1)])
    along = [along_z(later_blob, 0, k) for k in (1, 2, 3)]
    own = [in_plane(later_blob, 0, d) for d in (1, 2, 3)]
    grad, rows = layer(1, got, gated, grad_out, got_left, False)
    grad, rows, *moved = tied(grad, rows, *along, *own)
    along, own = moved[:3], moved[3:]

    got_grad = lax.ppermute(grad.reshape(1024, 768), "pipe", [(1, 0)])
    left, later_blob, *moved = tied(only_on(1, mixed, rows), later_blob, *along, *own)
    got = lax.ppermute(left, "pipe", [(1, 0)])

    def gathered(x, twiddle, blob, *moved):
        rest = stacked(0, *moved[:3])
        plane = [in_plane(rest, 0, d) for d in (1, 2, 3)]
        return forward(0, x, twiddle, PIECES, [blob, *moved, *plane])

    gated = only_on(0, gathered, inputs_saved, twiddle[0], later_blob, *moved)
    return layer(0, got, gated, got_grad, grad, True).reshape(1, 1024, 768)


def plain_body(inputs_saved, grad_out, value_weight, gate_weight, out_weight, right_factor, left_factor, twiddle):
    value_full, gate_full, out_full, right_full, left_full = (
        lax.all_gather(w[0], "seq", axis=0, tiled=True)
        for w in (value_weight, gate_weight, out_weight, right_factor, left_factor)
    )
    twiddle_own = twiddle[0]
    saved = inputs_saved[0]
    tokens_dev, width = saved.shape
    order = right_full.shape[0]
    blocks_dev, blocks_all = tokens_dev // order, left_full.shape[0]
    values = jnp.dot(saved, value_full, preferred_element_type=F32).astype(BF)
    gates = jnp.dot(saved, gate_full, preferred_element_type=F32).astype(BF).astype(F32)
    sigma = jax.nn.sigmoid(gates)
    active = gates * sigma
    slope = sigma * (1.0 + gates * (1.0 - sigma)) * values.astype(F32)

    def branch(incoming):
        mixed = jnp.dot(incoming, out_full.T, preferred_element_type=F32).astype(BF)
        mixed = mixed.reshape(blocks_dev, order, width)
        spread = lax.all_to_all(mixed, "seq", split_axis=1, concat_axis=0, tiled=True)
        part = spread.shape[1]
        left_part = jnp.dot(left_full.T, spread.reshape(blocks_all, part * width), preferred_element_type=F32).astype(BF)
        left_part = left_part.reshape(blocks_all, part, width)
        left_part = lax.all_to_all(left_part, "seq", split_axis=0, concat_axis=1, tiled=True)
        turned = (left_part.astype(F32) * twiddle_own[:, :, None]).astype(BF)
        right_part = jnp.einsum("pb,apc->abc", right_full, turned, preferred_element_type=F32).astype(BF)
        right_wide = right_part.reshape(tokens_dev, width).astype(F32)
        grad_value = (right_wide * active).astype(BF)
        grad_gate = (right_wide * slope).astype(BF)
        total = incoming.astype(F32)
        total = total + jnp.dot(grad_value, value_full.T, preferred_element_type=F32)
        total = total + jnp.dot(grad_gate, gate_full.T, preferred_element_type=F32)
        return total.astype(BF)

    first = branch(grad_out)
    second = branch(lax.ppermute(first, "pipe", [(1, 0)]))
    return jnp.where(lax.axis_index("pipe") == 1, first, second)[None]


def solution(mesh):
    fast = mesh.shape["pipe"] == 2 and mesh.shape["seq"] == SHARDS
    whole = P("pipe", "seq", None)
    in_specs = (whole, P("seq", None)) + (whole,) * 6
    return jax.shard_map(
        fast_body if fast else plain_body, mesh=mesh, in_specs=in_specs, out_specs=whole, check_vma=False
    )
```

time: 191 us -> 173 us (0.906)
  starting transfers between devices: 63 us -> 42.2 us
  blocking collectives: 47 us -> 56.4 us
  Pallas kernels: 34.8 us -> 28.3 us
    ppermute x15 -> x18, waiting for transfers between devices: 17.5 us -> 37.6 us  [sent(): return lax.ppermute(x, ('pipe', 'seq'), pairs)]
    ppermute x5 -> x4, starting transfers between devices: 22.5 us -> 4.1 us  [the longest x1 1.42 us: fast_body(): got = lax.ppermute(left, 'pipe', [(1, 0)])]
    all_to_all x2 -> x0, starting transfers between devices: 11.1 us -> none  [exchanged(): return lax.all_to_all(x, 'seq', split_axis=0, concat_axis=0, tiled=True)]
    ppermute x5 -> x4, waiting for transfers between devices: 13.2 us -> 3.38 us  [the longest x1 2.45 us: fast_body(): got_grad = lax.ppermute(grad.reshape(1024, 768), 'pipe', [(1, 0)])]
    all_to_all x2 -> x0, waiting for transfers between devices: 9.48 us -> none  [exchanged(): return lax.all_to_all(x, 'seq', split_axis=0, concat_axis=0, tiled=True)]
    all_to_all x2, blocking collectives: 47 us -> 56.4 us  [exchanged(): return lax.all_to_all(x, 'seq', split_axis=0, concat_axis=0, tiled=True)]
    ppermute x15 -> x18, starting transfers between devices: 29.3 us -> 38.1 us  [sent(): return lax.ppermute(x, ('pipe', 'seq'), pairs)]
    pallas_call x2, Pallas kernels: 11.3 us -> 7.93 us  [forward(): pl.pallas_call(lambda *refs: forward_kernel(section, pieces, len(weights)...]
  transfers between devices with their start and end apart: 22 -> 22, of which waited for: 7 -> 7; matrix products, arithmetic and copies ran while one was open for 1% -> 0% of each run, Pallas kernels for 13% -> 11%
where the time goes in v3:
time: 173 us; the launch traced here: 170 us
  blocking collectives  56.4 us (33%)
  starting transfers between devices  42.2 us (24%)
  waiting for transfers between devices  41 us (24%)
  Pallas kernels  28.3 us (16%)
    all_to_all x2, blocking collectives, exchanged(): return lax.all_to_all(x, 'seq', split_axis=0, concat_axis=0, tiled=True)  56.4 us
    ppermute x18, starting transfers between devices, sent(): return lax.ppermute(x, ('pipe', 'seq'), pairs)  38.1 us
    ppermute x18, waiting for transfers between devices, sent(): return lax.ppermute(x, ('pipe', 'seq'), pairs)  37.6 us
    pallas_call x2, Pallas kernels, layer(): pl.pallas_call(lambda *refs: layer_kernel(section, last, *refs), out_shap...  10.9 us
    pallas_call x2, Pallas kernels, forward(): pl.pallas_call(lambda *refs: forward_kernel(section, pieces, len(weights)...  7.93 us
    pallas_call x1, Pallas kernels, mix(): pl.pallas_call(mix_kernel, grid=(3,), out_shape=jax.ShapeDtypeStruct((SHA...  4.05 us
  transfers between devices with their start and end apart: 22, of which 7 were waited for; matrix products, arithmetic and copies ran while one was open for 0% of the time, Pallas kernels for 11%

profile of v3, /device:TPU:12, one launch (start us, length us, event | category | flops | bytes accessed | tf_op | source)
XLA Modules:
  0.0 169.9 jit_solution(13590743156011543152)
XLA Ops:
  8.4 1.7 collective-permute-start.10
  13.4 2.3 %rows.1 = bf16[16,25,16,128]{3,2,1,0:T(8,128)(2,1)S(1)} custom-call(bf16[16,4,16,768]{3,2,1,0:T(8,128)(2,1)} %bitcast.6, bf16[1,1,16]{2,1,0:T(2,128)(2,1)} %copy-done.8), custom_call_target="tpu_custom_call" | custom-call | flops 1 | bytes 1 | tf_op jit(solution)/shard_map/rows/pallas_call | solution.py:89
  15.7 60.5 %conditional.3 = (bf16[1024,768]{1,0:T(8,128)(2,1)}) conditional(s32[]{:T(128)} %convert_element_type.8, () %tuple.30, bf16[16,25,16,128]{3,2,1,0:T(8,128)(2,1)S(1)} %rows.1), branch_computations={%region_0.0_spmd, %region_1.0_spmd} | conditional | flops 1 | bytes 6422537 | solution.py:388
  15.7 28.8 %all_to_all.16.left.x = bf16[16,25,16,128]{3,2,1,0:T(8,128)(2,1)} all-to-all(bf16[16,25,16,128]{3,2,1,0:T(8,128)(2,1)S(1)} %param.1), channel_id=1, replica_groups=mesh['pipe'=2,'seq'=16] {'seq'}, dimensions={0} | all-to-all | bytes 3276800 | tf_op jit(solution)/shard_map/cond/branch_1_fun/all_to_all | solution.py:364
  44.5 4.0 %mix.2 = bf16[16,64,768]{2,1,0:T(8,128)(2,1)} custom-call(bf16[16,25,16,128]{3,2,1,0:T(8,128)(2,1)} %all_to_all.16.left.x, bf16[16,25,16,128]{3,2,1,0:T(8,128)(2,1)} %all_to_all.16.left.x), custom_call_target="tpu_custom_call" | custom-call | flops 1 | bytes 1 | tf_op jit(solution)/shard_map/cond/branch_1_fun/mix/pallas_call | solution.py:118
  48.6 27.6 %all_to_all.17 = bf16[16,64,768]{2,1,0:T(8,128)(2,1)} all-to-all(bf16[16,64,768]{2,1,0:T(8,128)(2,1)} %mix.2), channel_id=1, replica_groups=mesh['pipe'=2,'seq'=16] {'seq'}, dimensions={0} | all-to-all | bytes 3145728 | tf_op jit(solution)/shard_map/cond/branch_1_fun/all_to_all | solution.py:364
  77.8 1.9 %collective-permute-start.14 = (bf16[688,256]{1,0:T(8,128)(2,1)S(1)}, bf16[688,256]{1,0:T(8,128)(2,1)S(1)}, u32[]{:S(2)}, u32[]{:S(2)}) collective-permute-start(bf16[688,256]{1,0:T(8,128)(2,1)S(1)} %pack.1.refs_2_), channel_id=1, source_target_pairs={{0,4},{1,5},{2,6},{3,7},{4,8},{5,9},{6,10},{7,11},{8,12},{9,13},{1... | collective-permute-start | bytes 1056776 | tf_op jit(solution)/shard_map/ppermute | solution.py:352
  79.8 5.0 %collective-permute-start.15 = (bf16[688,256]{1,0:T(8,128)(2,1)S(1)}, bf16[688,256]{1,0:T(8,128)(2,1)}, u32[]{:S(2)}, u32[]{:S(2)}) collective-permute-start(bf16[688,256]{1,0:T(8,128)(2,1)S(1)} %pack.1.refs_2_), channel_id=1, source_target_pairs={{0,8},{1,9},{2,10},{3,11},{4,12},{5,13},{6,14},{7,15},{8,0},{9,1},... | collective-permute-start | bytes 1056776 | tf_op jit(solution)/shard_map/ppermute | solution.py:352
  84.8 2.3 %collective-permute-start.16 = (bf16[688,256]{1,0:T(8,128)(2,1)S(1)}, bf16[688,256]{1,0:T(8,128)(2,1)}, u32[]{:S(2)}, u32[]{:S(2)}) collective-permute-start(bf16[688,256]{1,0:T(8,128)(2,1)S(1)} %pack.1.refs_2_), channel_id=1, source_target_pairs={{0,12},{1,13},{2,14},{3,15},{4,0},{5,1},{6,2},{7,3},{8,4},{9,5},{1... | collective-permute-start | bytes 1056776 | tf_op jit(solution)/shard_map/ppermute | solution.py:352
  87.1 3.5 %collective-permute-start.17 = (bf16[688,256]{1,0:T(8,128)(2,1)S(1)}, bf16[688,256]{1,0:T(8,128)(2,1)}, u32[]{:S(2)}, u32[]{:S(2)}) collective-permute-start(bf16[688,256]{1,0:T(8,128)(2,1)S(1)} %pack.1.refs_2_), channel_id=1, source_target_pairs={{0,1},{1,0},{2,3},{3,2},{4,5},{5,4},{6,7},{7,6},{8,9},{9,8},{10,11... | collective-permute-start | bytes 1056776 | tf_op jit(solution)/shard_map/ppermute | solution.py:352
  90.6 2.2 %collective-permute-start.18 = (bf16[688,256]{1,0:T(8,128)(2,1)S(1)}, bf16[688,256]{1,0:T(8,128)(2,1)}, u32[]{:S(2)}, u32[]{:S(2)}) collective-permute-start(bf16[688,256]{1,0:T(8,128)(2,1)S(1)} %pack.1.refs_2_), channel_id=1, source_target_pairs={{0,2},{1,3},{2,0},{3,1},{4,6},{5,7},{6,4},{7,5},{8,10},{9,11},{10,... | collective-permute-start | bytes 1056776 | tf_op jit(solution)/shard_map/ppermute | solution.py:352
  92.9 3.5 %collective-permute-start.19 = (bf16[688,256]{1,0:T(8,128)(2,1)S(1)}, bf16[688,256]{1,0:T(8,128)(2,1)}, u32[]{:S(2)}, u32[]{:S(2)}) collective-permute-start(bf16[688,256]{1,0:T(8,128)(2,1)S(1)} %pack.1.refs_2_), channel_id=1, source_target_pairs={{0,3},{1,2},{2,1},{3,0},{4,7},{5,6},{6,5},{7,4},{8,11},{9,10},{10,... | collective-permute-start | bytes 1056776 | tf_op jit(solution)/shard_map/ppermute | solution.py:352
  97.4 2.2 %collective-permute-done.16 = bf16[688,256]{1,0:T(8,128)(2,1)} collective-permute-done((bf16[688,256]{1,0:T(8,128)(2,1)S(1)}, bf16[688,256]{1,0:T(8,128)(2,1)}, u32[]{:S(2)}, u32[]{:S(2)}) %collective-permute-start.16) | collective-permute-done | bytes 352288 | tf_op jit(solution)/shard_map/ppermute | solution.py:352
  99.6 5.6 %collective-permute-done.18 = bf16[688,256]{1,0:T(8,128)(2,1)} collective-permute-done((bf16[688,256]{1,0:T(8,128)(2,1)S(1)}, bf16[688,256]{1,0:T(8,128)(2,1)}, u32[]{:S(2)}, u32[]{:S(2)}) %collective-permute-start.18) | collective-permute-done | bytes 352288 | tf_op jit(solution)/shard_map/ppermute | solution.py:352
  108.0 48.7 %conditional.5 = ((bf16[1024,768]{1,0:T(8,128)(2,1)}, bf16[1024,768]{1,0:T(8,128)(2,1)}, bf16[1024,1024]{1,0:T(8,128)(2,1)}, bf16[16,432,256]{2,1,0:T(8,128)(2,1)})) conditional(s32[]{:T(128)} %convert_element_type.8, () %tuple.37, (bf16[688,256]{1,0:T(8,128)(2,1)}, bf16[688,256]{1,0:T(8,128)(2,1)}, bf16[688,256]{1,0:T(8,128)(2,1)}, ...), branch_computations={%region_4.0_spmd, %region_5.0_spmd} | conditional | flops 2 | bytes 12681346 | solution.py:388
  108.0 2.0 %stack.2 = bf16[2064,256]{1,0:T(8,128)(2,1)} custom-call(bf16[688,256]{1,0:T(8,128)(2,1)} %get-tuple-element.34.refs_0_.refs_3_, bf16[688,256]{1,0:T(8,128)(2,1)} %get-tuple-element.35.refs_1_.refs_4_, bf16[688,256]{1,0:T(8,128)(2,1)} %get-tuple-element.36.refs_2_.refs_5_), custom_call_target="tpu_custom_call" | custom-call | flops 1 | bytes 1 | tf_op jit(solution)/shard_map/cond/branch_1_fun/stack/pallas_call | solution.py:154
  110.0 1.9 %collective-permute-start = (bf16[2064,256]{1,0:T(8,128)(2,1)}, bf16[2064,256]{1,0:T(8,128)(2,1)}, u32[]{:S(2)}, u32[]{:S(2)}) collective-permute-start(bf16[2064,256]{1,0:T(8,128)(2,1)} %stack.2), channel_id=1, source_target_pairs={{0,1},{1,0},{2,3},{3,2},{4,5},{5,4},{6,7},{7,6},{8,9},{9,8},{10,11... | collective-permute-start | bytes 3170312 | tf_op jit(solution)/shard_map/cond/branch_1_fun/ppermute | solution.py:352
  112.0 1.9 %collective-permute-start.1 = (bf16[2064,256]{1,0:T(8,128)(2,1)}, bf16[2064,256]{1,0:T(8,128)(2,1)}, u32[]{:S(2)}, u32[]{:S(2)}) collective-permute-start(bf16[2064,256]{1,0:T(8,128)(2,1)} %stack.2), channel_id=1, source_target_pairs={{0,2},{1,3},{2,0},{3,1},{4,6},{5,7},{6,4},{7,5},{8,10},{9,11},{10,... | collective-permute-start | bytes 3170312 | tf_op jit(solution)/shard_map/cond/branch_1_fun/ppermute | solution.py:352
  113.9 5.4 %collective-permute-start.2 = (bf16[2064,256]{1,0:T(8,128)(2,1)}, bf16[2064,256]{1,0:T(8,128)(2,1)}, u32[]{:S(2)}, u32[]{:S(2)}) collective-permute-start(bf16[2064,256]{1,0:T(8,128)(2,1)} %stack.2), channel_id=1, source_target_pairs={{0,3},{1,2},{2,1},{3,0},{4,7},{5,6},{6,5},{7,4},{8,11},{9,10},{10,... | collective-permute-start | bytes 3170312 | tf_op jit(solution)/shard_map/cond/branch_1_fun/ppermute | solution.py:352
  119.3 10.2 %collective-permute-done.refs_9_ = bf16[2064,256]{1,0:T(8,128)(2,1)} collective-permute-done((bf16[2064,256]{1,0:T(8,128)(2,1)}, bf16[2064,256]{1,0:T(8,128)(2,1)}, u32[]{:S(2)}, u32[]{:S(2)}) %collective-permute-start) | collective-permute-done | bytes 1056800 | tf_op jit(solution)/shard_map/cond/branch_1_fun/ppermute | solution.py:352
  129.5 19.5 %collective-permute-done.1.refs_10_ = bf16[2064,256]{1,0:T(8,128)(2,1)} collective-permute-done((bf16[2064,256]{1,0:T(8,128)(2,1)}, bf16[2064,256]{1,0:T(8,128)(2,1)}, u32[]{:S(2)}, u32[]{:S(2)}) %collective-permute-start.1) | collective-permute-done | bytes 1056800 | tf_op jit(solution)/shard_map/cond/branch_1_fun/ppermute | solution.py:352
  149.0 7.7 %forward.2 = (bf16[1024,768]{1,0:T(8,128)(2,1)}, bf16[1024,768]{1,0:T(8,128)(2,1)}, bf16[1024,1024]{1,0:T(8,128)(2,1)}, bf16[16,432,256]{2,1,0:T(8,128)(2,1)}) custom-call(bf16[1,1024,768]{2,1,0:T(8,128)(2,1)S(1)} %get-tuple-element.31.refs_0_, f32[1,1024]{1,0:T(1,128)S(1)} %get-tuple-element.32.refs_1_, bf16[688,256]{1,0:T(8,128)(2,1)S(1)} %get-tuple-element.33.refs_2_, ...), custom_call_target="tpu_custom_call" | custom-call | flops 1 | bytes 1 | tf_op jit(solution)/shard_map/cond/branch_1_fun/forward/pallas_call | solution.py:242
  157.4 2.5 %collective-permute-done.21.refs_5_ = bf16[1024,768]{1,0:T(8,128)(2,1)} collective-permute-done((bf16[1024,768]{1,0:T(8,128)(2,1)}, bf16[1024,768]{1,0:T(8,128)(2,1)}, u32[]{:S(2)}, u32[]{:S(2)}) %collective-permute-start.21) | collective-permute-done | bytes 1572896 | tf_op jit(solution)/shard_map/ppermute | solution.py:414
  159.9 9.9 %layer.3 = bf16[16,4,16,768]{3,2,1,0:T(8,128)(2,1)} custom-call(bf16[1024,768]{1,0:T(8,128)(2,1)} %collective-permute-done.20.refs_0_, bf16[1024,768]{1,0:T(8,128)(2,1)} %get-tuple-element.119.refs_1_, bf16[1024,768]{1,0:T(8,128)(2,1)} %get-tuple-element.120.refs_2_, bf16[1024,1024]{1,0:T(8,128)(2,1)} %get-tuple-element.121.refs_3_, ...), custom_call_target="tpu_custom_call" | custom-call | flops 1 | bytes 1 | tf_op jit(solution)/shard_map/layer/pallas_call | solution.py:335
  (53 shorter events, 17.7 us)
Async XLA Ops:
  0.0 1.3 collective-permute-start.3
  1.3 12.1 %copy-start.8 = (bf16[1,1,16]{2,1,0:T(2,128)(2,1)}, bf16[1,1,16]{2,1,0:T(2,128)(2,1)S(1)}, u32[]{:S(2)}) copy-start(bf16[1,1,16]{2,1,0:T(2,128)(2,1)S(1)} %collective-permute-done.3.refs_1_.refs_6_) | copy-start | bytes 100
  1.3 4.2 %collective-permute-start.4 = (bf16[688,256]{1,0:T(8,128)(2,1)S(1)}, bf16[688,256]{1,0:T(8,128)(2,1)S(1)}, u32[]{:S(2)}, u32[]{:S(2)}) collective-permute-start(bf16[688,256]{1,0:T(8,128)(2,1)S(1)} %pack.1.refs_2_), channel_id=1, source_target_pairs={{16,20},{17,21},{18,22},{19,23},{20,24},{21,25},{22,26},{23,27},{2... | collective-permute-start | bytes 1056776 | tf_op jit(solution)/shard_map/ppermute | solution.py:352
  1.9 4.9 %collective-permute-start.5 = (bf16[688,256]{1,0:T(8,128)(2,1)S(1)}, bf16[688,256]{1,0:T(8,128)(2,1)S(1)}, u32[]{:S(2)}, u32[]{:S(2)}) collective-permute-start(bf16[688,256]{1,0:T(8,128)(2,1)S(1)} %pack.1.refs_2_), channel_id=1, source_target_pairs={{16,24},{17,25},{18,26},{19,27},{20,28},{21,29},{22,30},{23,31},{2... | collective-permute-start | bytes 1056776 | tf_op jit(solution)/shard_map/ppermute | solution.py:352
  2.6 4.2 %collective-permute-start.6 = (bf16[688,256]{1,0:T(8,128)(2,1)S(1)}, bf16[688,256]{1,0:T(8,128)(2,1)S(1)}, u32[]{:S(2)}, u32[]{:S(2)}) collective-permute-start(bf16[688,256]{1,0:T(8,128)(2,1)S(1)} %pack.1.refs_2_), channel_id=1, source_target_pairs={{16,28},{17,29},{18,30},{19,31},{20,16},{21,17},{22,18},{23,19},{2... | collective-permute-start | bytes 1056776 | tf_op jit(solution)/shard_map/ppermute | solution.py:352
  3.3 5.0 %collective-permute-start.7 = (bf16[688,256]{1,0:T(8,128)(2,1)S(1)}, bf16[688,256]{1,0:T(8,128)(2,1)S(1)}, u32[]{:S(2)}, u32[]{:S(2)}) collective-permute-start(bf16[688,256]{1,0:T(8,128)(2,1)S(1)} %pack.1.refs_2_), channel_id=1, source_target_pairs={{16,17},{17,16},{18,19},{19,18},{20,21},{21,20},{22,23},{23,22},{2... | collective-permute-start | bytes 1056776 | tf_op jit(solution)/shard_map/ppermute | solution.py:352
  4.0 4.4 %collective-permute-start.8 = (bf16[688,256]{1,0:T(8,128)(2,1)S(1)}, bf16[688,256]{1,0:T(8,128)(2,1)}, u32[]{:S(2)}, u32[]{:S(2)}) collective-permute-start(bf16[688,256]{1,0:T(8,128)(2,1)S(1)} %pack.1.refs_2_), channel_id=1, source_target_pairs={{16,18},{17,19},{18,16},{19,17},{20,22},{21,23},{22,20},{23,21},{2... | collective-permute-start | bytes 1056776 | tf_op jit(solution)/shard_map/ppermute | solution.py:352
  5.4 3.0 %collective-permute-start.9 = (bf16[688,256]{1,0:T(8,128)(2,1)S(1)}, bf16[688,256]{1,0:T(8,128)(2,1)}, u32[]{:S(2)}, u32[]{:S(2)}) collective-permute-start(bf16[688,256]{1,0:T(8,128)(2,1)S(1)} %pack.1.refs_2_), channel_id=1, source_target_pairs={{16,19},{17,18},{18,17},{19,16},{20,23},{21,22},{22,21},{23,20},{2... | collective-permute-start | bytes 1056776 | tf_op jit(solution)/shard_map/ppermute | solution.py:352
  8.4 67.8 %collective-permute-start.10 = (bf16[2064,256]{1,0:T(8,128)(2,1)}, bf16[2064,256]{1,0:T(8,128)(2,1)}, u32[]{:S(2)}, u32[]{:S(2)}) collective-permute-start(bf16[2064,256]{1,0:T(8,128)(2,1)} %stack.3), channel_id=1, source_target_pairs={{16,17},{17,16},{18,19},{19,18},{20,21},{21,20},{22,23},{23,22},{2... | collective-permute-start | bytes 3170312 | tf_op jit(solution)/shard_map/ppermute | solution.py:352
  10.1 66.1 %collective-permute-start.11 = (bf16[2064,256]{1,0:T(8,128)(2,1)}, bf16[2064,256]{1,0:T(8,128)(2,1)}, u32[]{:S(2)}, u32[]{:S(2)}) collective-permute-start(bf16[2064,256]{1,0:T(8,128)(2,1)} %stack.3), channel_id=1, source_target_pairs={{16,18},{17,19},{18,16},{19,17},{20,22},{21,23},{22,20},{23,21},{2... | collective-permute-start | bytes 3170312 | tf_op jit(solution)/shard_map/ppermute | solution.py:352
  11.7 64.5 %collective-permute-start.12 = (bf16[2064,256]{1,0:T(8,128)(2,1)}, bf16[2064,256]{1,0:T(8,128)(2,1)}, u32[]{:S(2)}, u32[]{:S(2)}) collective-permute-start(bf16[2064,256]{1,0:T(8,128)(2,1)} %stack.3), channel_id=1, source_target_pairs={{16,19},{17,18},{18,17},{19,16},{20,23},{21,22},{22,21},{23,20},{2... | collective-permute-start | bytes 3170312 | tf_op jit(solution)/shard_map/ppermute | solution.py:352
  15.7 60.5 %copy-start.7 = (f32[1,1,1024]{2,1,0:T(1,128)S(1)}, f32[1,1,1024]{2,1,0:T(1,128)}, u32[]{:S(2)}) copy-start(f32[1,1,1024]{2,1,0:T(1,128)} %param.21) | copy-start | bytes 12292
  76.4 16.4 %collective-permute-start.13 = (bf16[1024,768]{1,0:T(8,128)(2,1)}, bf16[1024,768]{1,0:T(8,128)(2,1)S(1)}, u32[]{:S(2)}, u32[]{:S(2)}) collective-permute-start(bf16[1024,768]{1,0:T(8,128)(2,1)} %get-tuple-element.132), channel_id=1, source_target_pairs={{0,16},{1,17},{2,18},{3,19},{4,20},{5,21},{6,22},{7,23},{8,24},{9,... | collective-permute-start | bytes 4718600 | tf_op jit(solution)/shard_map/ppermute | solution.py:407
  77.8 12.8 %collective-permute-start.14 = (bf16[688,256]{1,0:T(8,128)(2,1)S(1)}, bf16[688,256]{1,0:T(8,128)(2,1)S(1)}, u32[]{:S(2)}, u32[]{:S(2)}) collective-permute-start(bf16[688,256]{1,0:T(8,128)(2,1)S(1)} %pack.1.refs_2_), channel_id=1, source_target_pairs={{0,4},{1,5},{2,6},{3,7},{4,8},{5,9},{6,10},{7,11},{8,12},{9,13},{1... | collective-permute-start | bytes 1056776 | tf_op jit(solution)/shard_map/ppermute | solution.py:352
  79.8 17.7 %collective-permute-start.15 = (bf16[688,256]{1,0:T(8,128)(2,1)S(1)}, bf16[688,256]{1,0:T(8,128)(2,1)}, u32[]{:S(2)}, u32[]{:S(2)}) collective-permute-start(bf16[688,256]{1,0:T(8,128)(2,1)S(1)} %pack.1.refs_2_), channel_id=1, source_target_pairs={{0,8},{1,9},{2,10},{3,11},{4,12},{5,13},{6,14},{7,15},{8,0},{9,1},... | collective-permute-start | bytes 1056776 | tf_op jit(solution)/shard_map/ppermute | solution.py:352
  84.8 14.8 %collective-permute-start.16 = (bf16[688,256]{1,0:T(8,128)(2,1)S(1)}, bf16[688,256]{1,0:T(8,128)(2,1)}, u32[]{:S(2)}, u32[]{:S(2)}) collective-permute-start(bf16[688,256]{1,0:T(8,128)(2,1)S(1)} %pack.1.refs_2_), channel_id=1, source_target_pairs={{0,12},{1,13},{2,14},{3,15},{4,0},{5,1},{6,2},{7,3},{8,4},{9,5},{1... | collective-permute-start | bytes 1056776 | tf_op jit(solution)/shard_map/ppermute | solution.py:352
  87.1 12.6 %collective-permute-start.17 = (bf16[688,256]{1,0:T(8,128)(2,1)S(1)}, bf16[688,256]{1,0:T(8,128)(2,1)}, u32[]{:S(2)}, u32[]{:S(2)}) collective-permute-start(bf16[688,256]{1,0:T(8,128)(2,1)S(1)} %pack.1.refs_2_), channel_id=1, source_target_pairs={{0,1},{1,0},{2,3},{3,2},{4,5},{5,4},{6,7},{7,6},{8,9},{9,8},{10,11... | collective-permute-start | bytes 1056776 | tf_op jit(solution)/shard_map/ppermute | solution.py:352
  90.6 14.6 %collective-permute-start.18 = (bf16[688,256]{1,0:T(8,128)(2,1)S(1)}, bf16[688,256]{1,0:T(8,128)(2,1)}, u32[]{:S(2)}, u32[]{:S(2)}) collective-permute-start(bf16[688,256]{1,0:T(8,128)(2,1)S(1)} %pack.1.refs_2_), channel_id=1, source_target_pairs={{0,2},{1,3},{2,0},{3,1},{4,6},{5,7},{6,4},{7,5},{8,10},{9,11},{10,... | collective-permute-start | bytes 1056776 | tf_op jit(solution)/shard_map/ppermute | solution.py:352
  92.9 12.4 %collective-permute-start.19 = (bf16[688,256]{1,0:T(8,128)(2,1)S(1)}, bf16[688,256]{1,0:T(8,128)(2,1)}, u32[]{:S(2)}, u32[]{:S(2)}) collective-permute-start(bf16[688,256]{1,0:T(8,128)(2,1)S(1)} %pack.1.refs_2_), channel_id=1, source_target_pairs={{0,3},{1,2},{2,1},{3,0},{4,7},{5,6},{6,5},{7,4},{8,11},{9,10},{10,... | collective-permute-start | bytes 1056776 | tf_op jit(solution)/shard_map/ppermute | solution.py:352
  105.2 52.2 %collective-permute-start.20 = (bf16[1024,768]{1,0:T(8,128)(2,1)}, bf16[1024,768]{1,0:T(8,128)(2,1)}, u32[]{:S(2)}, u32[]{:S(2)}) collective-permute-start(bf16[1024,768]{1,0:T(8,128)(2,1)} %get-tuple-element.133), channel_id=1, source_target_pairs={{16,0},{17,1},{18,2},{19,3},{20,4},{21,5},{22,6},{23,7},{24,8},{25... | collective-permute-start | bytes 4718600 | tf_op jit(solution)/shard_map/ppermute | solution.py:416
  106.7 53.2 %collective-permute-start.21 = (bf16[1024,768]{1,0:T(8,128)(2,1)}, bf16[1024,768]{1,0:T(8,128)(2,1)}, u32[]{:S(2)}, u32[]{:S(2)}) collective-permute-start(bf16[1024,768]{1,0:T(8,128)(2,1)} %bitcast.7), channel_id=1, source_target_pairs={{16,0},{17,1},{18,2},{19,3},{20,4},{21,5},{22,6},{23,7},{24,8},{25... | collective-permute-start | bytes 4718600 | tf_op jit(solution)/shard_map/ppermute | solution.py:414
  110.0 19.5 %collective-permute-start = (bf16[2064,256]{1,0:T(8,128)(2,1)}, bf16[2064,256]{1,0:T(8,128)(2,1)}, u32[]{:S(2)}, u32[]{:S(2)}) collective-permute-start(bf16[2064,256]{1,0:T(8,128)(2,1)} %stack.2), channel_id=1, source_target_pairs={{0,1},{1,0},{2,3},{3,2},{4,5},{5,4},{6,7},{7,6},{8,9},{9,8},{10,11... | collective-permute-start | bytes 3170312 | tf_op jit(solution)/shard_map/cond/branch_1_fun/ppermute | solution.py:352
  112.0 37.1 %collective-permute-start.1 = (bf16[2064,256]{1,0:T(8,128)(2,1)}, bf16[2064,256]{1,0:T(8,128)(2,1)}, u32[]{:S(2)}, u32[]{:S(2)}) collective-permute-start(bf16[2064,256]{1,0:T(8,128)(2,1)} %stack.2), channel_id=1, source_target_pairs={{0,2},{1,3},{2,0},{3,1},{4,6},{5,7},{6,4},{7,5},{8,10},{9,11},{10,... | collective-permute-start | bytes 3170312 | tf_op jit(solution)/shard_map/cond/branch_1_fun/ppermute | solution.py:352
  113.9 35.1 %collective-permute-start.2 = (bf16[2064,256]{1,0:T(8,128)(2,1)}, bf16[2064,256]{1,0:T(8,128)(2,1)}, u32[]{:S(2)}, u32[]{:S(2)}) collective-permute-start(bf16[2064,256]{1,0:T(8,128)(2,1)} %stack.2), channel_id=1, source_target_pairs={{0,3},{1,2},{2,1},{3,0},{4,7},{5,6},{6,5},{7,4},{8,11},{9,10},{10,... | collective-permute-start | bytes 3170312 | tf_op jit(solution)/shard_map/cond/branch_1_fun/ppermute | solution.py:352
  (7 other events, 16.4 us)

commit v4 on v3

--- a/solution.py
+++ b/solution.py
@@ -110,20 +110,20 @@
         matrix[...] = jnp.where(at == to, wide, 0.0).astype(BF)
 
     for q in range(4):
-        part = jnp.concatenate([x[:, 4 * c + q, :, :].reshape(256, 128) for c in range(2)], axis=1)
-        y[:, 16 * q : 16 * q + 16, :] = dot_nn(matrix[...], part).astype(BF).reshape(16, 16, 256)
+        part = jnp.concatenate([x[:, 4 * c + q, :, :].reshape(256, 128) for c in range(3)], axis=1)
+        y[:, 16 * q : 16 * q + 16, :] = dot_nn(matrix[...], part).astype(BF).reshape(16, 16, 384)
 
 
 def mix(x):
     return pl.pallas_call(
         mix_kernel,
-        grid=(3,),
+        grid=(2,),
         out_shape=jax.ShapeDtypeStruct((SHARDS, 64, 768), BF),
         in_specs=[
             pl.BlockSpec((SHARDS, 1, 16, 128), lambda i: (0, GROUPS - 1, 0, 0)),
-            pl.BlockSpec((SHARDS, 8, 16, 128), lambda i: (0, i, 0, 0)),
+            pl.BlockSpec((SHARDS, 12, 16, 128), lambda i: (0, i, 0, 0)),
         ],
-        out_specs=pl.BlockSpec((SHARDS, 64, 256), lambda i: (0, 0, i)),
+        out_specs=pl.BlockSpec((SHARDS, 64, 384), lambda i: (0, 0, i)),
         scratch_shapes=[pltpu.VMEM((256, 256), BF)],
         name="mix",
         cost_estimate=LIGHT,
@@ -190,7 +190,8 @@
 def forward_work(pieces, n_refs, *refs):
     x, twiddle, weights, refs = refs[0], refs[1], refs[2 : 2 + n_refs], refs[2 + n_refs :]
     active, slope, turning, gathered, scratch, rows_in, act, slo, right, sem_w, sem, sem_out = refs
-    loads = [pltpu.make_async_copy(x.at[0, pl.ds(512 * t, 512)], rows_in.at[pl.ds(512 * t, 512)], sem.at[t]) for t in range(2)]
+    tiles = [slice(256 * t, 256 * t + 256) for t in range(4)]
+    loads = [pltpu.make_async_copy(x.at[0, rows], rows_in.at[rows], sem.at[t]) for t, rows in enumerate(tiles)]
     copies = weight_copies(pieces, weights, scratch, sem_w, 0, ROWS)
     for c in loads[:1] + copies + loads[1:]:
         c.start()
@@ -203,9 +204,11 @@
         stores[-1].start()
 
     store(scratch.at[:, pl.ds(OUT, ROWS - OUT), :], gathered)
-    for t in range(2):
+    for t, rows in enumerate(tiles):
         loads[t].wait()
-        rows = slice(512 * t, 512 * t + 512)
+        part = scratch[:, RIGHT + 64 * t : RIGHT + 64 * t + 64, :].reshape(1024, 256)
+        right[rows, :] = (part.T.astype(F32) * twiddle[...]).astype(BF)
+        store(right.at[rows], turning.at[rows])
         for e in range(3):
             lanes = slice(256 * e, 256 * e + 256)
             value = scratch[:, VALUE + 48 * e : VALUE + 48 * e + 48, :].reshape(768, 256)
@@ -216,14 +219,8 @@
             on = gates * sigma
             act[rows, lanes] = on.astype(BF)
             slo[rows, lanes] = ((sigma + on * (1.0 - sigma)) * values).astype(BF)
-            step = 3 * t + e
-            if step in (0, 1, 3, 4):
-                g = (0, 1, 0, 2, 3)[step]
-                part = scratch[:, RIGHT + 64 * g : RIGHT + 64 * g + 64, :].reshape(1024, 256)
-                right[256 * g : 256 * g + 256, :] = (part.T.astype(F32) * twiddle[...]).astype(BF)
         store(act.at[rows], active.at[rows])
         store(slo.at[rows], slope.at[rows])
-        store(right.at[rows], turning.at[rows])
     for c in stores:
         c.wait()
 
@@ -245,7 +242,7 @@
         in_specs=[ANY, VMEM] + [ANY] * len(weights),
         out_specs=(ANY,) * 4,
         scratch_shapes=[pltpu.VMEM((SHARDS, ROWS, 256), BF), big, big, big, pltpu.VMEM((1024, 1024), BF)]
-        + [pltpu.SemaphoreType.DMA((SHARDS,)), pltpu.SemaphoreType.DMA((2,)), pltpu.SemaphoreType.DMA((7,))],
+        + [pltpu.SemaphoreType.DMA((SHARDS,)), pltpu.SemaphoreType.DMA((4,)), pltpu.SemaphoreType.DMA((13,))],
         compiler_params=PARAMS,
         name="forward",
         cost_estimate=LIGHT,

time: 173 us -> 172 us (level)
  transfers between devices with their start and end apart: 22 -> 22, of which waited for: 7 -> 9; matrix products, arithmetic and copies ran while one was open for 0% -> 0% of each run, Pallas kernels for 11% -> 10%
where the time goes in v4:
time: 172 us; the launch traced here: 169 us
  blocking collectives  56.4 us (33%)
  starting transfers between devices  42.8 us (25%)
  waiting for transfers between devices  40.7 us (24%)
  Pallas kernels  27.5 us (16%)
    all_to_all x2, blocking collectives, exchanged(): return lax.all_to_all(x, 'seq', split_axis=0, concat_axis=0, tiled=True)  56.4 us
    ppermute x18, starting transfers between devices, sent(): return lax.ppermute(x, ('pipe', 'seq'), pairs)  37.9 us
    ppermute x18, waiting for transfers between devices, sent(): return lax.ppermute(x, ('pipe', 'seq'), pairs)  36.5 us
    pallas_call x2, Pallas kernels, layer(): pl.pallas_call(lambda *refs: layer_kernel(section, last, *refs), out_shap...  10.9 us
    pallas_call x2, Pallas kernels, forward(): pl.pallas_call(lambda *refs: forward_kernel(section, pieces, len(weights)...  7.99 us
  transfers between devices with their start and end apart: 22, of which 9 were waited for; matrix products, arithmetic and copies ran while one was open for 0% of the time, Pallas kernels for 10%

profile of v4, /device:TPU:12, one launch (start us, length us, event | category | flops | bytes accessed | tf_op | source)
XLA Modules:
  0.0 169.4 jit_solution(4758623232225462875)
XLA Ops:
  13.4 2.3 %rows.1 = bf16[16,25,16,128]{3,2,1,0:T(8,128)(2,1)S(1)} custom-call(bf16[16,4,16,768]{3,2,1,0:T(8,128)(2,1)} %bitcast.6, bf16[1,1,16]{2,1,0:T(2,128)(2,1)} %copy-done.8), custom_call_target="tpu_custom_call" | custom-call | flops 1 | bytes 1 | tf_op jit(solution)/shard_map/rows/pallas_call | solution.py:89
  15.7 59.6 %conditional.3 = (bf16[1024,768]{1,0:T(8,128)(2,1)}) conditional(s32[]{:T(128)} %convert_element_type.8, () %tuple.30, bf16[16,25,16,128]{3,2,1,0:T(8,128)(2,1)S(1)} %rows.1), branch_computations={%region_0.0_spmd, %region_1.0_spmd} | conditional | flops 1 | bytes 6422537 | solution.py:385
  15.7 28.8 %all_to_all.16.left.x = bf16[16,25,16,128]{3,2,1,0:T(8,128)(2,1)} all-to-all(bf16[16,25,16,128]{3,2,1,0:T(8,128)(2,1)S(1)} %param.1), channel_id=1, replica_groups=mesh['pipe'=2,'seq'=16] {'seq'}, dimensions={0} | all-to-all | bytes 3276800 | tf_op jit(solution)/shard_map/cond/branch_1_fun/all_to_all | solution.py:361
  44.5 3.2 %mix.2 = bf16[16,64,768]{2,1,0:T(8,128)(2,1)} custom-call(bf16[16,25,16,128]{3,2,1,0:T(8,128)(2,1)} %all_to_all.16.left.x, bf16[16,25,16,128]{3,2,1,0:T(8,128)(2,1)} %all_to_all.16.left.x), custom_call_target="tpu_custom_call" | custom-call | flops 1 | bytes 1 | tf_op jit(solution)/shard_map/cond/branch_1_fun/mix/pallas_call | solution.py:118
  47.7 27.6 %all_to_all.17 = bf16[16,64,768]{2,1,0:T(8,128)(2,1)} all-to-all(bf16[16,64,768]{2,1,0:T(8,128)(2,1)} %mix.2), channel_id=1, replica_groups=mesh['pipe'=2,'seq'=16] {'seq'}, dimensions={0} | all-to-all | bytes 3145728 | tf_op jit(solution)/shard_map/cond/branch_1_fun/all_to_all | solution.py:361
  75.7 2.2 %collective-permute-start.13 = (bf16[1024,768]{1,0:T(8,128)(2,1)}, bf16[1024,768]{1,0:T(8,128)(2,1)S(1)}, u32[]{:S(2)}, u32[]{:S(2)}) collective-permute-start(bf16[1024,768]{1,0:T(8,128)(2,1)} %get-tuple-element.132), channel_id=1, source_target_pairs={{0,16},{1,17},{2,18},{3,19},{4,20},{5,21},{6,22},{7,23},{8,24},{9,... | collective-permute-start | bytes 4718600 | tf_op jit(solution)/shard_map/ppermute | solution.py:404
  79.8 5.1 %collective-permute-start.15 = (bf16[688,256]{1,0:T(8,128)(2,1)S(1)}, bf16[688,256]{1,0:T(8,128)(2,1)}, u32[]{:S(2)}, u32[]{:S(2)}) collective-permute-start(bf16[688,256]{1,0:T(8,128)(2,1)S(1)} %pack.1.refs_2_), channel_id=1, source_target_pairs={{0,8},{1,9},{2,10},{3,11},{4,12},{5,13},{6,14},{7,15},{8,0},{9,1},... | collective-permute-start | bytes 1056776 | tf_op jit(solution)/shard_map/ppermute | solution.py:349
  84.9 1.9 %collective-permute-start.16 = (bf16[688,256]{1,0:T(8,128)(2,1)S(1)}, bf16[688,256]{1,0:T(8,128)(2,1)}, u32[]{:S(2)}, u32[]{:S(2)}) collective-permute-start(bf16[688,256]{1,0:T(8,128)(2,1)S(1)} %pack.1.refs_2_), channel_id=1, source_target_pairs={{0,12},{1,13},{2,14},{3,15},{4,0},{5,1},{6,2},{7,3},{8,4},{9,5},{1... | collective-permute-start | bytes 1056776 | tf_op jit(solution)/shard_map/ppermute | solution.py:349
  86.8 3.7 %collective-permute-start.17 = (bf16[688,256]{1,0:T(8,128)(2,1)S(1)}, bf16[688,256]{1,0:T(8,128)(2,1)}, u32[]{:S(2)}, u32[]{:S(2)}) collective-permute-start(bf16[688,256]{1,0:T(8,128)(2,1)S(1)} %pack.1.refs_2_), channel_id=1, source_target_pairs={{0,1},{1,0},{2,3},{3,2},{4,5},{5,4},{6,7},{7,6},{8,9},{9,8},{10,11... | collective-permute-start | bytes 1056776 | tf_op jit(solution)/shard_map/ppermute | solution.py:349
  90.6 2.1 %collective-permute-start.18 = (bf16[688,256]{1,0:T(8,128)(2,1)S(1)}, bf16[688,256]{1,0:T(8,128)(2,1)}, u32[]{:S(2)}, u32[]{:S(2)}) collective-permute-start(bf16[688,256]{1,0:T(8,128)(2,1)S(1)} %pack.1.refs_2_), channel_id=1, source_target_pairs={{0,2},{1,3},{2,0},{3,1},{4,6},{5,7},{6,4},{7,5},{8,10},{9,11},{10,... | collective-permute-start | bytes 1056776 | tf_op jit(solution)/shard_map/ppermute | solution.py:349
  92.8 3.4 %collective-permute-start.19 = (bf16[688,256]{1,0:T(8,128)(2,1)S(1)}, bf16[688,256]{1,0:T(8,128)(2,1)}, u32[]{:S(2)}, u32[]{:S(2)}) collective-permute-start(bf16[688,256]{1,0:T(8,128)(2,1)S(1)} %pack.1.refs_2_), channel_id=1, source_target_pairs={{0,3},{1,2},{2,1},{3,0},{4,7},{5,6},{6,5},{7,4},{8,11},{9,10},{10,... | collective-permute-start | bytes 1056776 | tf_op jit(solution)/shard_map/ppermute | solution.py:349
  97.3 2.5 %collective-permute-done.16 = bf16[688,256]{1,0:T(8,128)(2,1)} collective-permute-done((bf16[688,256]{1,0:T(8,128)(2,1)S(1)}, bf16[688,256]{1,0:T(8,128)(2,1)}, u32[]{:S(2)}, u32[]{:S(2)}) %collective-permute-start.16) | collective-permute-done | bytes 352288 | tf_op jit(solution)/shard_map/ppermute | solution.py:349
  99.8 4.5 %collective-permute-done.18 = bf16[688,256]{1,0:T(8,128)(2,1)} collective-permute-done((bf16[688,256]{1,0:T(8,128)(2,1)S(1)}, bf16[688,256]{1,0:T(8,128)(2,1)}, u32[]{:S(2)}, u32[]{:S(2)}) %collective-permute-start.18) | collective-permute-done | bytes 352288 | tf_op jit(solution)/shard_map/ppermute | solution.py:349
  107.0 48.4 %conditional.5 = ((bf16[1024,768]{1,0:T(8,128)(2,1)}, bf16[1024,768]{1,0:T(8,128)(2,1)}, bf16[1024,1024]{1,0:T(8,128)(2,1)}, bf16[16,432,256]{2,1,0:T(8,128)(2,1)})) conditional(s32[]{:T(128)} %convert_element_type.8, () %tuple.37, (bf16[688,256]{1,0:T(8,128)(2,1)}, bf16[688,256]{1,0:T(8,128)(2,1)}, bf16[688,256]{1,0:T(8,128)(2,1)}, ...), branch_computations={%region_4.0_spmd, %region_5.0_spmd} | conditional | flops 2 | bytes 12681346 | solution.py:385
  107.0 2.0 %stack.2 = bf16[2064,256]{1,0:T(8,128)(2,1)} custom-call(bf16[688,256]{1,0:T(8,128)(2,1)} %get-tuple-element.34.refs_0_.refs_3_, bf16[688,256]{1,0:T(8,128)(2,1)} %get-tuple-element.35.refs_1_.refs_4_, bf16[688,256]{1,0:T(8,128)(2,1)} %get-tuple-element.36.refs_2_.refs_5_), custom_call_target="tpu_custom_call" | custom-call | flops 1 | bytes 1 | tf_op jit(solution)/shard_map/cond/branch_1_fun/stack/pallas_call | solution.py:154
  109.0 1.9 %collective-permute-start = (bf16[2064,256]{1,0:T(8,128)(2,1)}, bf16[2064,256]{1,0:T(8,128)(2,1)}, u32[]{:S(2)}, u32[]{:S(2)}) collective-permute-start(bf16[2064,256]{1,0:T(8,128)(2,1)} %stack.2), channel_id=1, source_target_pairs={{0,1},{1,0},{2,3},{3,2},{4,5},{5,4},{6,7},{7,6},{8,9},{9,8},{10,11... | collective-permute-start | bytes 3170312 | tf_op jit(solution)/shard_map/cond/branch_1_fun/ppermute | solution.py:349
  111.0 2.7 %collective-permute-start.1 = (bf16[2064,256]{1,0:T(8,128)(2,1)}, bf16[2064,256]{1,0:T(8,128)(2,1)}, u32[]{:S(2)}, u32[]{:S(2)}) collective-permute-start(bf16[2064,256]{1,0:T(8,128)(2,1)} %stack.2), channel_id=1, source_target_pairs={{0,2},{1,3},{2,0},{3,1},{4,6},{5,7},{6,4},{7,5},{8,10},{9,11},{10,... | collective-permute-start | bytes 3170312 | tf_op jit(solution)/shard_map/cond/branch_1_fun/ppermute | solution.py:349
  113.6 4.6 %collective-permute-start.2 = (bf16[2064,256]{1,0:T(8,128)(2,1)}, bf16[2064,256]{1,0:T(8,128)(2,1)}, u32[]{:S(2)}, u32[]{:S(2)}) collective-permute-start(bf16[2064,256]{1,0:T(8,128)(2,1)} %stack.2), channel_id=1, source_target_pairs={{0,3},{1,2},{2,1},{3,0},{4,7},{5,6},{6,5},{7,4},{8,11},{9,10},{10,... | collective-permute-start | bytes 3170312 | tf_op jit(solution)/shard_map/cond/branch_1_fun/ppermute | solution.py:349
  118.3 10.9 %collective-permute-done.refs_9_ = bf16[2064,256]{1,0:T(8,128)(2,1)} collective-permute-done((bf16[2064,256]{1,0:T(8,128)(2,1)}, bf16[2064,256]{1,0:T(8,128)(2,1)}, u32[]{:S(2)}, u32[]{:S(2)}) %collective-permute-start) | collective-permute-done | bytes 1056800 | tf_op jit(solution)/shard_map/cond/branch_1_fun/ppermute | solution.py:349
  129.2 11.6 %collective-permute-done.1.refs_10_ = bf16[2064,256]{1,0:T(8,128)(2,1)} collective-permute-done((bf16[2064,256]{1,0:T(8,128)(2,1)}, bf16[2064,256]{1,0:T(8,128)(2,1)}, u32[]{:S(2)}, u32[]{:S(2)}) %collective-permute-start.1) | collective-permute-done | bytes 1056800 | tf_op jit(solution)/shard_map/cond/branch_1_fun/ppermute | solution.py:349
  140.8 6.9 %collective-permute-done.2.refs_11_ = bf16[2064,256]{1,0:T(8,128)(2,1)} collective-permute-done((bf16[2064,256]{1,0:T(8,128)(2,1)}, bf16[2064,256]{1,0:T(8,128)(2,1)}, u32[]{:S(2)}, u32[]{:S(2)}) %collective-permute-start.2) | collective-permute-done | bytes 1056800 | tf_op jit(solution)/shard_map/cond/branch_1_fun/ppermute | solution.py:349
  147.7 7.7 %forward.2 = (bf16[1024,768]{1,0:T(8,128)(2,1)}, bf16[1024,768]{1,0:T(8,128)(2,1)}, bf16[1024,1024]{1,0:T(8,128)(2,1)}, bf16[16,432,256]{2,1,0:T(8,128)(2,1)}) custom-call(bf16[1,1024,768]{2,1,0:T(8,128)(2,1)S(1)} %get-tuple-element.31.refs_0_, f32[1,1024]{1,0:T(1,128)S(1)} %get-tuple-element.32.refs_1_, bf16[688,256]{1,0:T(8,128)(2,1)S(1)} %get-tuple-element.33.refs_2_, ...), custom_call_target="tpu_custom_call" | custom-call | flops 1 | bytes 1 | tf_op jit(solution)/shard_map/cond/branch_1_fun/forward/pallas_call | solution.py:239
  156.9 2.5 %collective-permute-done.21.refs_5_ = bf16[1024,768]{1,0:T(8,128)(2,1)} collective-permute-done((bf16[1024,768]{1,0:T(8,128)(2,1)}, bf16[1024,768]{1,0:T(8,128)(2,1)}, u32[]{:S(2)}, u32[]{:S(2)}) %collective-permute-start.21) | collective-permute-done | bytes 1572896 | tf_op jit(solution)/shard_map/ppermute | solution.py:411
  159.3 9.9 %layer.3 = bf16[16,4,16,768]{3,2,1,0:T(8,128)(2,1)} custom-call(bf16[1024,768]{1,0:T(8,128)(2,1)} %collective-permute-done.20.refs_0_, bf16[1024,768]{1,0:T(8,128)(2,1)} %get-tuple-element.119.refs_1_, bf16[1024,768]{1,0:T(8,128)(2,1)} %get-tuple-element.120.refs_2_, bf16[1024,1024]{1,0:T(8,128)(2,1)} %get-tuple-element.121.refs_3_, ...), custom_call_target="tpu_custom_call" | custom-call | flops 1 | bytes 1 | tf_op jit(solution)/shard_map/layer/pallas_call | solution.py:332
  (53 shorter events, 20.9 us)
Async XLA Ops:
  0.0 1.3 collective-permute-start.3
  1.3 12.1 %copy-start.8 = (bf16[1,1,16]{2,1,0:T(2,128)(2,1)}, bf16[1,1,16]{2,1,0:T(2,128)(2,1)S(1)}, u32[]{:S(2)}) copy-start(bf16[1,1,16]{2,1,0:T(2,128)(2,1)S(1)} %collective-permute-done.3.refs_1_.refs_6_) | copy-start | bytes 100
  1.3 4.2 %collective-permute-start.4 = (bf16[688,256]{1,0:T(8,128)(2,1)S(1)}, bf16[688,256]{1,0:T(8,128)(2,1)S(1)}, u32[]{:S(2)}, u32[]{:S(2)}) collective-permute-start(bf16[688,256]{1,0:T(8,128)(2,1)S(1)} %pack.1.refs_2_), channel_id=1, source_target_pairs={{16,20},{17,21},{18,22},{19,23},{20,24},{21,25},{22,26},{23,27},{2... | collective-permute-start | bytes 1056776 | tf_op jit(solution)/shard_map/ppermute | solution.py:349
  1.9 4.9 %collective-permute-start.5 = (bf16[688,256]{1,0:T(8,128)(2,1)S(1)}, bf16[688,256]{1,0:T(8,128)(2,1)S(1)}, u32[]{:S(2)}, u32[]{:S(2)}) collective-permute-start(bf16[688,256]{1,0:T(8,128)(2,1)S(1)} %pack.1.refs_2_), channel_id=1, source_target_pairs={{16,24},{17,25},{18,26},{19,27},{20,28},{21,29},{22,30},{23,31},{2... | collective-permute-start | bytes 1056776 | tf_op jit(solution)/shard_map/ppermute | solution.py:349
  2.6 4.2 %collective-permute-start.6 = (bf16[688,256]{1,0:T(8,128)(2,1)S(1)}, bf16[688,256]{1,0:T(8,128)(2,1)S(1)}, u32[]{:S(2)}, u32[]{:S(2)}) collective-permute-start(bf16[688,256]{1,0:T(8,128)(2,1)S(1)} %pack.1.refs_2_), channel_id=1, source_target_pairs={{16,28},{17,29},{18,30},{19,31},{20,16},{21,17},{22,18},{23,19},{2... | collective-permute-start | bytes 1056776 | tf_op jit(solution)/shard_map/ppermute | solution.py:349
  3.3 5.0 %collective-permute-start.7 = (bf16[688,256]{1,0:T(8,128)(2,1)S(1)}, bf16[688,256]{1,0:T(8,128)(2,1)S(1)}, u32[]{:S(2)}, u32[]{:S(2)}) collective-permute-start(bf16[688,256]{1,0:T(8,128)(2,1)S(1)} %pack.1.refs_2_), channel_id=1, source_target_pairs={{16,17},{17,16},{18,19},{19,18},{20,21},{21,20},{22,23},{23,22},{2... | collective-permute-start | bytes 1056776 | tf_op jit(solution)/shard_map/ppermute | solution.py:349
  4.0 4.4 %collective-permute-start.8 = (bf16[688,256]{1,0:T(8,128)(2,1)S(1)}, bf16[688,256]{1,0:T(8,128)(2,1)}, u32[]{:S(2)}, u32[]{:S(2)}) collective-permute-start(bf16[688,256]{1,0:T(8,128)(2,1)S(1)} %pack.1.refs_2_), channel_id=1, source_target_pairs={{16,18},{17,19},{18,16},{19,17},{20,22},{21,23},{22,20},{23,21},{2... | collective-permute-start | bytes 1056776 | tf_op jit(solution)/shard_map/ppermute | solution.py:349
  5.4 3.0 %collective-permute-start.9 = (bf16[688,256]{1,0:T(8,128)(2,1)S(1)}, bf16[688,256]{1,0:T(8,128)(2,1)}, u32[]{:S(2)}, u32[]{:S(2)}) collective-permute-start(bf16[688,256]{1,0:T(8,128)(2,1)S(1)} %pack.1.refs_2_), channel_id=1, source_target_pairs={{16,19},{17,18},{18,17},{19,16},{20,23},{21,22},{22,21},{23,20},{2... | collective-permute-start | bytes 1056776 | tf_op jit(solution)/shard_map/ppermute | solution.py:349
  8.4 66.9 %collective-permute-start.10 = (bf16[2064,256]{1,0:T(8,128)(2,1)}, bf16[2064,256]{1,0:T(8,128)(2,1)}, u32[]{:S(2)}, u32[]{:S(2)}) collective-permute-start(bf16[2064,256]{1,0:T(8,128)(2,1)} %stack.3), channel_id=1, source_target_pairs={{16,17},{17,16},{18,19},{19,18},{20,21},{21,20},{22,23},{23,22},{2... | collective-permute-start | bytes 3170312 | tf_op jit(solution)/shard_map/ppermute | solution.py:349
  10.1 65.3 %collective-permute-start.11 = (bf16[2064,256]{1,0:T(8,128)(2,1)}, bf16[2064,256]{1,0:T(8,128)(2,1)}, u32[]{:S(2)}, u32[]{:S(2)}) collective-permute-start(bf16[2064,256]{1,0:T(8,128)(2,1)} %stack.3), channel_id=1, source_target_pairs={{16,18},{17,19},{18,16},{19,17},{20,22},{21,23},{22,20},{23,21},{2... | collective-permute-start | bytes 3170312 | tf_op jit(solution)/shard_map/ppermute | solution.py:349
  11.7 63.6 %collective-permute-start.12 = (bf16[2064,256]{1,0:T(8,128)(2,1)}, bf16[2064,256]{1,0:T(8,128)(2,1)}, u32[]{:S(2)}, u32[]{:S(2)}) collective-permute-start(bf16[2064,256]{1,0:T(8,128)(2,1)} %stack.3), channel_id=1, source_target_pairs={{16,19},{17,18},{18,17},{19,16},{20,23},{21,22},{22,21},{23,20},{2... | collective-permute-start | bytes 3170312 | tf_op jit(solution)/shard_map/ppermute | solution.py:349
  15.7 59.6 %copy-start.7 = (f32[1,1,1024]{2,1,0:T(1,128)S(1)}, f32[1,1,1024]{2,1,0:T(1,128)}, u32[]{:S(2)}) copy-start(f32[1,1,1024]{2,1,0:T(1,128)} %param.21) | copy-start | bytes 12292
  75.7 17.1 %collective-permute-start.13 = (bf16[1024,768]{1,0:T(8,128)(2,1)}, bf16[1024,768]{1,0:T(8,128)(2,1)S(1)}, u32[]{:S(2)}, u32[]{:S(2)}) collective-permute-start(bf16[1024,768]{1,0:T(8,128)(2,1)} %get-tuple-element.132), channel_id=1, source_target_pairs={{0,16},{1,17},{2,18},{3,19},{4,20},{5,21},{6,22},{7,23},{8,24},{9,... | collective-permute-start | bytes 4718600 | tf_op jit(solution)/shard_map/ppermute | solution.py:404
  77.8 12.7 %collective-permute-start.14 = (bf16[688,256]{1,0:T(8,128)(2,1)S(1)}, bf16[688,256]{1,0:T(8,128)(2,1)S(1)}, u32[]{:S(2)}, u32[]{:S(2)}) collective-permute-start(bf16[688,256]{1,0:T(8,128)(2,1)S(1)} %pack.1.refs_2_), channel_id=1, source_target_pairs={{0,4},{1,5},{2,6},{3,7},{4,8},{5,9},{6,10},{7,11},{8,12},{9,13},{1... | collective-permute-start | bytes 1056776 | tf_op jit(solution)/shard_map/ppermute | solution.py:349
  79.8 17.5 %collective-permute-start.15 = (bf16[688,256]{1,0:T(8,128)(2,1)S(1)}, bf16[688,256]{1,0:T(8,128)(2,1)}, u32[]{:S(2)}, u32[]{:S(2)}) collective-permute-start(bf16[688,256]{1,0:T(8,128)(2,1)S(1)} %pack.1.refs_2_), channel_id=1, source_target_pairs={{0,8},{1,9},{2,10},{3,11},{4,12},{5,13},{6,14},{7,15},{8,0},{9,1},... | collective-permute-start | bytes 1056776 | tf_op jit(solution)/shard_map/ppermute | solution.py:349
  84.9 14.8 %collective-permute-start.16 = (bf16[688,256]{1,0:T(8,128)(2,1)S(1)}, bf16[688,256]{1,0:T(8,128)(2,1)}, u32[]{:S(2)}, u32[]{:S(2)}) collective-permute-start(bf16[688,256]{1,0:T(8,128)(2,1)S(1)} %pack.1.refs_2_), channel_id=1, source_target_pairs={{0,12},{1,13},{2,14},{3,15},{4,0},{5,1},{6,2},{7,3},{8,4},{9,5},{1... | collective-permute-start | bytes 1056776 | tf_op jit(solution)/shard_map/ppermute | solution.py:349
  86.8 12.9 %collective-permute-start.17 = (bf16[688,256]{1,0:T(8,128)(2,1)S(1)}, bf16[688,256]{1,0:T(8,128)(2,1)}, u32[]{:S(2)}, u32[]{:S(2)}) collective-permute-start(bf16[688,256]{1,0:T(8,128)(2,1)S(1)} %pack.1.refs_2_), channel_id=1, source_target_pairs={{0,1},{1,0},{2,3},{3,2},{4,5},{5,4},{6,7},{7,6},{8,9},{9,8},{10,11... | collective-permute-start | bytes 1056776 | tf_op jit(solution)/shard_map/ppermute | solution.py:349
  90.6 13.7 %collective-permute-start.18 = (bf16[688,256]{1,0:T(8,128)(2,1)S(1)}, bf16[688,256]{1,0:T(8,128)(2,1)}, u32[]{:S(2)}, u32[]{:S(2)}) collective-permute-start(bf16[688,256]{1,0:T(8,128)(2,1)S(1)} %pack.1.refs_2_), channel_id=1, source_target_pairs={{0,2},{1,3},{2,0},{3,1},{4,6},{5,7},{6,4},{7,5},{8,10},{9,11},{10,... | collective-permute-start | bytes 1056776 | tf_op jit(solution)/shard_map/ppermute | solution.py:349
  92.8 11.5 %collective-permute-start.19 = (bf16[688,256]{1,0:T(8,128)(2,1)S(1)}, bf16[688,256]{1,0:T(8,128)(2,1)}, u32[]{:S(2)}, u32[]{:S(2)}) collective-permute-start(bf16[688,256]{1,0:T(8,128)(2,1)S(1)} %pack.1.refs_2_), channel_id=1, source_target_pairs={{0,3},{1,2},{2,1},{3,0},{4,7},{5,6},{6,5},{7,4},{8,11},{9,10},{10,... | collective-permute-start | bytes 1056776 | tf_op jit(solution)/shard_map/ppermute | solution.py:349
  104.3 52.6 %collective-permute-start.20 = (bf16[1024,768]{1,0:T(8,128)(2,1)}, bf16[1024,768]{1,0:T(8,128)(2,1)}, u32[]{:S(2)}, u32[]{:S(2)}) collective-permute-start(bf16[1024,768]{1,0:T(8,128)(2,1)} %get-tuple-element.133), channel_id=1, source_target_pairs={{16,0},{17,1},{18,2},{19,3},{20,4},{21,5},{22,6},{23,7},{24,8},{25... | collective-permute-start | bytes 4718600 | tf_op jit(solution)/shard_map/ppermute | solution.py:413
  105.7 53.6 %collective-permute-start.21 = (bf16[1024,768]{1,0:T(8,128)(2,1)}, bf16[1024,768]{1,0:T(8,128)(2,1)}, u32[]{:S(2)}, u32[]{:S(2)}) collective-permute-start(bf16[1024,768]{1,0:T(8,128)(2,1)} %bitcast.7), channel_id=1, source_target_pairs={{16,0},{17,1},{18,2},{19,3},{20,4},{21,5},{22,6},{23,7},{24,8},{25... | collective-permute-start | bytes 4718600 | tf_op jit(solution)/shard_map/ppermute | solution.py:411
  109.0 20.2 %collective-permute-start = (bf16[2064,256]{1,0:T(8,128)(2,1)}, bf16[2064,256]{1,0:T(8,128)(2,1)}, u32[]{:S(2)}, u32[]{:S(2)}) collective-permute-start(bf16[2064,256]{1,0:T(8,128)(2,1)} %stack.2), channel_id=1, source_target_pairs={{0,1},{1,0},{2,3},{3,2},{4,5},{5,4},{6,7},{7,6},{8,9},{9,8},{10,11... | collective-permute-start | bytes 3170312 | tf_op jit(solution)/shard_map/cond/branch_1_fun/ppermute | solution.py:349
  111.0 29.8 %collective-permute-start.1 = (bf16[2064,256]{1,0:T(8,128)(2,1)}, bf16[2064,256]{1,0:T(8,128)(2,1)}, u32[]{:S(2)}, u32[]{:S(2)}) collective-permute-start(bf16[2064,256]{1,0:T(8,128)(2,1)} %stack.2), channel_id=1, source_target_pairs={{0,2},{1,3},{2,0},{3,1},{4,6},{5,7},{6,4},{7,5},{8,10},{9,11},{10,... | collective-permute-start | bytes 3170312 | tf_op jit(solution)/shard_map/cond/branch_1_fun/ppermute | solution.py:349
  113.6 34.1 %collective-permute-start.2 = (bf16[2064,256]{1,0:T(8,128)(2,1)}, bf16[2064,256]{1,0:T(8,128)(2,1)}, u32[]{:S(2)}, u32[]{:S(2)}) collective-permute-start(bf16[2064,256]{1,0:T(8,128)(2,1)} %stack.2), channel_id=1, source_target_pairs={{0,3},{1,2},{2,1},{3,0},{4,7},{5,6},{6,5},{7,4},{8,11},{9,10},{10,... | collective-permute-start | bytes 3170312 | tf_op jit(solution)/shard_map/cond/branch_1_fun/ppermute | solution.py:349
  (7 other events, 16.2 us)

commit v5 on v4

--- a/solution.py
+++ b/solution.py
@@ -368,8 +368,8 @@
 PIECES = (
     [(0, (0,), 0, 0)]
     + [(0, (k,), 0, 0) for k in (1, 2, 3)]
-    + [(0, (0,), d, 0) for d in (1, 2, 3)]
-    + [(0, (1, 2, 3), d, 0) for d in (1, 2, 3)]
+    + [(0, (0,), d, 0) for d in (3, 1, 2)]
+    + [(0, (1, 2, 3), d, 0) for d in (3, 1, 2)]
 )
 
 
@@ -394,16 +394,16 @@
     blob, got_left = tied(pack(right_factor, out_weight, value_weight, gate_weight), got_left)
 
     along = [along_z(blob, 1, k) for k in (1, 2, 3)]
-    own = [in_plane(blob, 1, d) for d in (1, 2, 3)]
+    own = [in_plane(blob, 1, d) for d in (3, 1, 2)]
     rest, *own = tied(stacked(1, *along), *own)
-    plane = [in_plane(rest, 1, d) for d in (1, 2, 3)]
+    plane = [in_plane(rest, 1, d) for d in (3, 1, 2)]
     left = only_on(0, mixed, rows_to_send(1, grad_out, got_left))
     left, *plane = tied(left, *plane)
     gated = forward(1, inputs_saved, twiddle[0], PIECES, [blob, *along, *own, *plane])
     left, later_blob, *gated = tied(left, blob, *gated)
     got = lax.ppermute(left, "pipe", [(0, 1)])
     along = [along_z(later_blob, 0, k) for k in (1, 2, 3)]
-    own = [in_plane(later_blob, 0, d) for d in (1, 2, 3)]
+    own = [in_plane(later_blob, 0, d) for d in (3, 1, 2)]
     grad, rows = layer(1, got, gated, grad_out, got_left, False)
     grad, rows, *moved = tied(grad, rows, *along, *own)
     along, own = moved[:3], moved[3:]
@@ -414,7 +414,7 @@
 
     def gathered(x, twiddle, blob, *moved):
         rest = stacked(0, *moved[:3])
-        plane = [in_plane(rest, 0, d) for d in (1, 2, 3)]
+        plane = [in_plane(rest, 0, d) for d in (3, 1, 2)]
         return forward(0, x, twiddle, PIECES, [blob, *moved, *plane])
 
     gated = only_on(0, gathered, inputs_saved, twiddle[0], later_blob, *moved)

time: 172 us -> 171 us (level)
  no operation moved by 1% of the time
where the time goes in v5:
time: 171 us; the launch traced here: 168 us
  blocking collectives  56.4 us (33%)
  starting transfers between devices  42.2 us (25%)
  waiting for transfers between devices  39.8 us (23%)
  Pallas kernels  27.5 us (16%)
    all_to_all x2, blocking collectives, exchanged(): return lax.all_to_all(x, 'seq', split_axis=0, concat_axis=0, tiled=True)  56.4 us
    ppermute x18, starting transfers between devices, sent(): return lax.ppermute(x, ('pipe', 'seq'), pairs)  38.1 us
    ppermute x18, waiting for transfers between devices, sent(): return lax.ppermute(x, ('pipe', 'seq'), pairs)  35.5 us
    pallas_call x2, Pallas kernels, layer(): pl.pallas_call(lambda *refs: layer_kernel(section, last, *refs), out_shap...  10.9 us
    pallas_call x2, Pallas kernels, forward(): pl.pallas_call(lambda *refs: forward_kernel(section, pieces, len(weights)...  7.99 us
  transfers between devices with their start and end apart: 22, of which 9 were waited for; matrix products, arithmetic and copies ran while one was open for 0% of the time, Pallas kernels for 10%

profile of v5, /device:TPU:12, one launch (start us, length us, event | category | flops | bytes accessed | tf_op | source)
XLA Modules:
  0.0 168.0 jit_solution(2986281387508810692)
XLA Ops:
  8.4 1.7 collective-permute-start.10
  13.4 2.3 %rows.1 = bf16[16,25,16,128]{3,2,1,0:T(8,128)(2,1)S(1)} custom-call(bf16[16,4,16,768]{3,2,1,0:T(8,128)(2,1)} %bitcast.6, bf16[1,1,16]{2,1,0:T(2,128)(2,1)} %copy-done.8), custom_call_target="tpu_custom_call" | custom-call | flops 1 | bytes 1 | tf_op jit(solution)/shard_map/rows/pallas_call | solution.py:89
  15.7 59.7 %conditional.3 = (bf16[1024,768]{1,0:T(8,128)(2,1)}) conditional(s32[]{:T(128)} %convert_element_type.8, () %tuple.30, bf16[16,25,16,128]{3,2,1,0:T(8,128)(2,1)S(1)} %rows.1), branch_computations={%region_0.0_spmd, %region_1.0_spmd} | conditional | flops 1 | bytes 6422537 | solution.py:385
  15.7 28.8 %all_to_all.16.left.x = bf16[16,25,16,128]{3,2,1,0:T(8,128)(2,1)} all-to-all(bf16[16,25,16,128]{3,2,1,0:T(8,128)(2,1)S(1)} %param.1), channel_id=1, replica_groups=mesh['pipe'=2,'seq'=16] {'seq'}, dimensions={0} | all-to-all | bytes 3276800 | tf_op jit(solution)/shard_map/cond/branch_1_fun/all_to_all | solution.py:361
  44.5 3.2 %mix.2 = bf16[16,64,768]{2,1,0:T(8,128)(2,1)} custom-call(bf16[16,25,16,128]{3,2,1,0:T(8,128)(2,1)} %all_to_all.16.left.x, bf16[16,25,16,128]{3,2,1,0:T(8,128)(2,1)} %all_to_all.16.left.x), custom_call_target="tpu_custom_call" | custom-call | flops 1 | bytes 1 | tf_op jit(solution)/shard_map/cond/branch_1_fun/mix/pallas_call | solution.py:118
  47.7 27.7 %all_to_all.17 = bf16[16,64,768]{2,1,0:T(8,128)(2,1)} all-to-all(bf16[16,64,768]{2,1,0:T(8,128)(2,1)} %mix.2), channel_id=1, replica_groups=mesh['pipe'=2,'seq'=16] {'seq'}, dimensions={0} | all-to-all | bytes 3145728 | tf_op jit(solution)/shard_map/cond/branch_1_fun/all_to_all | solution.py:361
  77.1 1.9 %collective-permute-start.14 = (bf16[688,256]{1,0:T(8,128)(2,1)S(1)}, bf16[688,256]{1,0:T(8,128)(2,1)S(1)}, u32[]{:S(2)}, u32[]{:S(2)}) collective-permute-start(bf16[688,256]{1,0:T(8,128)(2,1)S(1)} %pack.1.refs_2_), channel_id=1, source_target_pairs={{0,4},{1,5},{2,6},{3,7},{4,8},{5,9},{6,10},{7,11},{8,12},{9,13},{1... | collective-permute-start | bytes 1056776 | tf_op jit(solution)/shard_map/ppermute | solution.py:349
  79.0 5.0 %collective-permute-start.15 = (bf16[688,256]{1,0:T(8,128)(2,1)S(1)}, bf16[688,256]{1,0:T(8,128)(2,1)}, u32[]{:S(2)}, u32[]{:S(2)}) collective-permute-start(bf16[688,256]{1,0:T(8,128)(2,1)S(1)} %pack.1.refs_2_), channel_id=1, source_target_pairs={{0,8},{1,9},{2,10},{3,11},{4,12},{5,13},{6,14},{7,15},{8,0},{9,1},... | collective-permute-start | bytes 1056776 | tf_op jit(solution)/shard_map/ppermute | solution.py:349
  84.1 2.3 %collective-permute-start.16 = (bf16[688,256]{1,0:T(8,128)(2,1)S(1)}, bf16[688,256]{1,0:T(8,128)(2,1)}, u32[]{:S(2)}, u32[]{:S(2)}) collective-permute-start(bf16[688,256]{1,0:T(8,128)(2,1)S(1)} %pack.1.refs_2_), channel_id=1, source_target_pairs={{0,12},{1,13},{2,14},{3,15},{4,0},{5,1},{6,2},{7,3},{8,4},{9,5},{1... | collective-permute-start | bytes 1056776 | tf_op jit(solution)/shard_map/ppermute | solution.py:349
  86.4 2.7 %collective-permute-start.17 = (bf16[688,256]{1,0:T(8,128)(2,1)S(1)}, bf16[688,256]{1,0:T(8,128)(2,1)}, u32[]{:S(2)}, u32[]{:S(2)}) collective-permute-start(bf16[688,256]{1,0:T(8,128)(2,1)S(1)} %pack.1.refs_2_), channel_id=1, source_target_pairs={{0,3},{1,2},{2,1},{3,0},{4,7},{5,6},{6,5},{7,4},{8,11},{9,10},{10,... | collective-permute-start | bytes 1056776 | tf_op jit(solution)/shard_map/ppermute | solution.py:349
  89.1 3.4 %collective-permute-start.18 = (bf16[688,256]{1,0:T(8,128)(2,1)S(1)}, bf16[688,256]{1,0:T(8,128)(2,1)}, u32[]{:S(2)}, u32[]{:S(2)}) collective-permute-start(bf16[688,256]{1,0:T(8,128)(2,1)S(1)} %pack.1.refs_2_), channel_id=1, source_target_pairs={{0,1},{1,0},{2,3},{3,2},{4,5},{5,4},{6,7},{7,6},{8,9},{9,8},{10,11... | collective-permute-start | bytes 1056776 | tf_op jit(solution)/shard_map/ppermute | solution.py:349
  92.5 3.2 %collective-permute-start.19 = (bf16[688,256]{1,0:T(8,128)(2,1)S(1)}, bf16[688,256]{1,0:T(8,128)(2,1)}, u32[]{:S(2)}, u32[]{:S(2)}) collective-permute-start(bf16[688,256]{1,0:T(8,128)(2,1)S(1)} %pack.1.refs_2_), channel_id=1, source_target_pairs={{0,2},{1,3},{2,0},{3,1},{4,6},{5,7},{6,4},{7,5},{8,10},{9,11},{10,... | collective-permute-start | bytes 1056776 | tf_op jit(solution)/shard_map/ppermute | solution.py:349
  96.7 2.2 %collective-permute-done.16 = bf16[688,256]{1,0:T(8,128)(2,1)} collective-permute-done((bf16[688,256]{1,0:T(8,128)(2,1)S(1)}, bf16[688,256]{1,0:T(8,128)(2,1)}, u32[]{:S(2)}, u32[]{:S(2)}) %collective-permute-start.16) | collective-permute-done | bytes 352288 | tf_op jit(solution)/shard_map/ppermute | solution.py:349
  99.7 2.1 %collective-permute-done.19 = bf16[688,256]{1,0:T(8,128)(2,1)} collective-permute-done((bf16[688,256]{1,0:T(8,128)(2,1)S(1)}, bf16[688,256]{1,0:T(8,128)(2,1)}, u32[]{:S(2)}, u32[]{:S(2)}) %collective-permute-start.19) | collective-permute-done | bytes 352288 | tf_op jit(solution)/shard_map/ppermute | solution.py:349
  104.6 49.4 %conditional.5 = ((bf16[1024,768]{1,0:T(8,128)(2,1)}, bf16[1024,768]{1,0:T(8,128)(2,1)}, bf16[1024,1024]{1,0:T(8,128)(2,1)}, bf16[16,432,256]{2,1,0:T(8,128)(2,1)})) conditional(s32[]{:T(128)} %convert_element_type.8, () %tuple.37, (bf16[688,256]{1,0:T(8,128)(2,1)}, bf16[688,256]{1,0:T(8,128)(2,1)}, bf16[688,256]{1,0:T(8,128)(2,1)}, ...), branch_computations={%region_4.0_spmd, %region_5.0_spmd} | conditional | flops 2 | bytes 12681346 | solution.py:385
  104.6 2.0 %stack.2 = bf16[2064,256]{1,0:T(8,128)(2,1)} custom-call(bf16[688,256]{1,0:T(8,128)(2,1)} %get-tuple-element.34.refs_0_.refs_3_, bf16[688,256]{1,0:T(8,128)(2,1)} %get-tuple-element.35.refs_1_.refs_4_, bf16[688,256]{1,0:T(8,128)(2,1)} %get-tuple-element.36.refs_2_.refs_5_), custom_call_target="tpu_custom_call" | custom-call | flops 1 | bytes 1 | tf_op jit(solution)/shard_map/cond/branch_1_fun/stack/pallas_call | solution.py:154
  106.6 3.2 %collective-permute-start = (bf16[2064,256]{1,0:T(8,128)(2,1)}, bf16[2064,256]{1,0:T(8,128)(2,1)}, u32[]{:S(2)}, u32[]{:S(2)}) collective-permute-start(bf16[2064,256]{1,0:T(8,128)(2,1)} %stack.2), channel_id=1, source_target_pairs={{0,3},{1,2},{2,1},{3,0},{4,7},{5,6},{6,5},{7,4},{8,11},{9,10},{10,... | collective-permute-start | bytes 3170312 | tf_op jit(solution)/shard_map/cond/branch_1_fun/ppermute | solution.py:349
  109.8 3.4 %collective-permute-start.1 = (bf16[2064,256]{1,0:T(8,128)(2,1)}, bf16[2064,256]{1,0:T(8,128)(2,1)}, u32[]{:S(2)}, u32[]{:S(2)}) collective-permute-start(bf16[2064,256]{1,0:T(8,128)(2,1)} %stack.2), channel_id=1, source_target_pairs={{0,1},{1,0},{2,3},{3,2},{4,5},{5,4},{6,7},{7,6},{8,9},{9,8},{10,11... | collective-permute-start | bytes 3170312 | tf_op jit(solution)/shard_map/cond/branch_1_fun/ppermute | solution.py:349
  113.1 2.7 %collective-permute-start.2 = (bf16[2064,256]{1,0:T(8,128)(2,1)}, bf16[2064,256]{1,0:T(8,128)(2,1)}, u32[]{:S(2)}, u32[]{:S(2)}) collective-permute-start(bf16[2064,256]{1,0:T(8,128)(2,1)} %stack.2), channel_id=1, source_target_pairs={{0,2},{1,3},{2,0},{3,1},{4,6},{5,7},{6,4},{7,5},{8,10},{9,11},{10,... | collective-permute-start | bytes 3170312 | tf_op jit(solution)/shard_map/cond/branch_1_fun/ppermute | solution.py:349
  115.8 12.5 %collective-permute-done.refs_9_ = bf16[2064,256]{1,0:T(8,128)(2,1)} collective-permute-done((bf16[2064,256]{1,0:T(8,128)(2,1)}, bf16[2064,256]{1,0:T(8,128)(2,1)}, u32[]{:S(2)}, u32[]{:S(2)}) %collective-permute-start) | collective-permute-done | bytes 1056800 | tf_op jit(solution)/shard_map/cond/branch_1_fun/ppermute | solution.py:349
  128.3 17.3 %collective-permute-done.1.refs_10_ = bf16[2064,256]{1,0:T(8,128)(2,1)} collective-permute-done((bf16[2064,256]{1,0:T(8,128)(2,1)}, bf16[2064,256]{1,0:T(8,128)(2,1)}, u32[]{:S(2)}, u32[]{:S(2)}) %collective-permute-start.1) | collective-permute-done | bytes 1056800 | tf_op jit(solution)/shard_map/cond/branch_1_fun/ppermute | solution.py:349
  146.2 7.7 %forward.2 = (bf16[1024,768]{1,0:T(8,128)(2,1)}, bf16[1024,768]{1,0:T(8,128)(2,1)}, bf16[1024,1024]{1,0:T(8,128)(2,1)}, bf16[16,432,256]{2,1,0:T(8,128)(2,1)}) custom-call(bf16[1,1024,768]{2,1,0:T(8,128)(2,1)S(1)} %get-tuple-element.31.refs_0_, f32[1,1024]{1,0:T(1,128)S(1)} %get-tuple-element.32.refs_1_, bf16[688,256]{1,0:T(8,128)(2,1)S(1)} %get-tuple-element.33.refs_2_, ...), custom_call_target="tpu_custom_call" | custom-call | flops 1 | bytes 1 | tf_op jit(solution)/shard_map/cond/branch_1_fun/forward/pallas_call | solution.py:239
  155.6 2.5 %collective-permute-done.21.refs_5_ = bf16[1024,768]{1,0:T(8,128)(2,1)} collective-permute-done((bf16[1024,768]{1,0:T(8,128)(2,1)}, bf16[1024,768]{1,0:T(8,128)(2,1)}, u32[]{:S(2)}, u32[]{:S(2)}) %collective-permute-start.21) | collective-permute-done | bytes 1572896 | tf_op jit(solution)/shard_map/ppermute | solution.py:411
  158.0 9.9 %layer.3 = bf16[16,4,16,768]{3,2,1,0:T(8,128)(2,1)} custom-call(bf16[1024,768]{1,0:T(8,128)(2,1)} %collective-permute-done.20.refs_0_, bf16[1024,768]{1,0:T(8,128)(2,1)} %get-tuple-element.119.refs_1_, bf16[1024,768]{1,0:T(8,128)(2,1)} %get-tuple-element.120.refs_2_, bf16[1024,1024]{1,0:T(8,128)(2,1)} %get-tuple-element.121.refs_3_, ...), custom_call_target="tpu_custom_call" | custom-call | flops 1 | bytes 1 | tf_op jit(solution)/shard_map/layer/pallas_call | solution.py:332
  (53 shorter events, 20.1 us)
Async XLA Ops:
  0.0 1.3 collective-permute-start.3
  1.3 12.1 %copy-start.8 = (bf16[1,1,16]{2,1,0:T(2,128)(2,1)}, bf16[1,1,16]{2,1,0:T(2,128)(2,1)S(1)}, u32[]{:S(2)}) copy-start(bf16[1,1,16]{2,1,0:T(2,128)(2,1)S(1)} %collective-permute-done.3.refs_1_.refs_6_) | copy-start | bytes 100
  1.3 4.2 %collective-permute-start.4 = (bf16[688,256]{1,0:T(8,128)(2,1)S(1)}, bf16[688,256]{1,0:T(8,128)(2,1)S(1)}, u32[]{:S(2)}, u32[]{:S(2)}) collective-permute-start(bf16[688,256]{1,0:T(8,128)(2,1)S(1)} %pack.1.refs_2_), channel_id=1, source_target_pairs={{16,20},{17,21},{18,22},{19,23},{20,24},{21,25},{22,26},{23,27},{2... | collective-permute-start | bytes 1056776 | tf_op jit(solution)/shard_map/ppermute | solution.py:349
  1.9 4.9 %collective-permute-start.5 = (bf16[688,256]{1,0:T(8,128)(2,1)S(1)}, bf16[688,256]{1,0:T(8,128)(2,1)S(1)}, u32[]{:S(2)}, u32[]{:S(2)}) collective-permute-start(bf16[688,256]{1,0:T(8,128)(2,1)S(1)} %pack.1.refs_2_), channel_id=1, source_target_pairs={{16,24},{17,25},{18,26},{19,27},{20,28},{21,29},{22,30},{23,31},{2... | collective-permute-start | bytes 1056776 | tf_op jit(solution)/shard_map/ppermute | solution.py:349
  2.6 4.2 %collective-permute-start.6 = (bf16[688,256]{1,0:T(8,128)(2,1)S(1)}, bf16[688,256]{1,0:T(8,128)(2,1)S(1)}, u32[]{:S(2)}, u32[]{:S(2)}) collective-permute-start(bf16[688,256]{1,0:T(8,128)(2,1)S(1)} %pack.1.refs_2_), channel_id=1, source_target_pairs={{16,28},{17,29},{18,30},{19,31},{20,16},{21,17},{22,18},{23,19},{2... | collective-permute-start | bytes 1056776 | tf_op jit(solution)/shard_map/ppermute | solution.py:349
  3.3 5.0 %collective-permute-start.7 = (bf16[688,256]{1,0:T(8,128)(2,1)S(1)}, bf16[688,256]{1,0:T(8,128)(2,1)S(1)}, u32[]{:S(2)}, u32[]{:S(2)}) collective-permute-start(bf16[688,256]{1,0:T(8,128)(2,1)S(1)} %pack.1.refs_2_), channel_id=1, source_target_pairs={{16,19},{17,18},{18,17},{19,16},{20,23},{21,22},{22,21},{23,20},{2... | collective-permute-start | bytes 1056776 | tf_op jit(solution)/shard_map/ppermute | solution.py:349
  4.0 4.4 %collective-permute-start.8 = (bf16[688,256]{1,0:T(8,128)(2,1)S(1)}, bf16[688,256]{1,0:T(8,128)(2,1)}, u32[]{:S(2)}, u32[]{:S(2)}) collective-permute-start(bf16[688,256]{1,0:T(8,128)(2,1)S(1)} %pack.1.refs_2_), channel_id=1, source_target_pairs={{16,17},{17,16},{18,19},{19,18},{20,21},{21,20},{22,23},{23,22},{2... | collective-permute-start | bytes 1056776 | tf_op jit(solution)/shard_map/ppermute | solution.py:349
  5.4 3.0 %collective-permute-start.9 = (bf16[688,256]{1,0:T(8,128)(2,1)S(1)}, bf16[688,256]{1,0:T(8,128)(2,1)}, u32[]{:S(2)}, u32[]{:S(2)}) collective-permute-start(bf16[688,256]{1,0:T(8,128)(2,1)S(1)} %pack.1.refs_2_), channel_id=1, source_target_pairs={{16,18},{17,19},{18,16},{19,17},{20,22},{21,23},{22,20},{23,21},{2... | collective-permute-start | bytes 1056776 | tf_op jit(solution)/shard_map/ppermute | solution.py:349
  8.4 67.0 %collective-permute-start.10 = (bf16[2064,256]{1,0:T(8,128)(2,1)}, bf16[2064,256]{1,0:T(8,128)(2,1)}, u32[]{:S(2)}, u32[]{:S(2)}) collective-permute-start(bf16[2064,256]{1,0:T(8,128)(2,1)} %stack.3), channel_id=1, source_target_pairs={{16,19},{17,18},{18,17},{19,16},{20,23},{21,22},{22,21},{23,20},{2... | collective-permute-start | bytes 3170312 | tf_op jit(solution)/shard_map/ppermute | solution.py:349
  10.1 65.3 %collective-permute-start.11 = (bf16[2064,256]{1,0:T(8,128)(2,1)}, bf16[2064,256]{1,0:T(8,128)(2,1)}, u32[]{:S(2)}, u32[]{:S(2)}) collective-permute-start(bf16[2064,256]{1,0:T(8,128)(2,1)} %stack.3), channel_id=1, source_target_pairs={{16,17},{17,16},{18,19},{19,18},{20,21},{21,20},{22,23},{23,22},{2... | collective-permute-start | bytes 3170312 | tf_op jit(solution)/shard_map/ppermute | solution.py:349
  11.7 63.7 %collective-permute-start.12 = (bf16[2064,256]{1,0:T(8,128)(2,1)}, bf16[2064,256]{1,0:T(8,128)(2,1)}, u32[]{:S(2)}, u32[]{:S(2)}) collective-permute-start(bf16[2064,256]{1,0:T(8,128)(2,1)} %stack.3), channel_id=1, source_target_pairs={{16,18},{17,19},{18,16},{19,17},{20,22},{21,23},{22,20},{23,21},{2... | collective-permute-start | bytes 3170312 | tf_op jit(solution)/shard_map/ppermute | solution.py:349
  15.7 59.7 %copy-start.7 = (f32[1,1,1024]{2,1,0:T(1,128)S(1)}, f32[1,1,1024]{2,1,0:T(1,128)}, u32[]{:S(2)}) copy-start(f32[1,1,1024]{2,1,0:T(1,128)} %param.21) | copy-start | bytes 12292
  75.7 16.7 %collective-permute-start.13 = (bf16[1024,768]{1,0:T(8,128)(2,1)}, bf16[1024,768]{1,0:T(8,128)(2,1)S(1)}, u32[]{:S(2)}, u32[]{:S(2)}) collective-permute-start(bf16[1024,768]{1,0:T(8,128)(2,1)} %get-tuple-element.132), channel_id=1, source_target_pairs={{0,16},{1,17},{2,18},{3,19},{4,20},{5,21},{6,22},{7,23},{8,24},{9,... | collective-permute-start | bytes 4718600 | tf_op jit(solution)/shard_map/ppermute | solution.py:404
  77.1 11.9 %collective-permute-start.14 = (bf16[688,256]{1,0:T(8,128)(2,1)S(1)}, bf16[688,256]{1,0:T(8,128)(2,1)S(1)}, u32[]{:S(2)}, u32[]{:S(2)}) collective-permute-start(bf16[688,256]{1,0:T(8,128)(2,1)S(1)} %pack.1.refs_2_), channel_id=1, source_target_pairs={{0,4},{1,5},{2,6},{3,7},{4,8},{5,9},{6,10},{7,11},{8,12},{9,13},{1... | collective-permute-start | bytes 1056776 | tf_op jit(solution)/shard_map/ppermute | solution.py:349
  79.0 17.7 %collective-permute-start.15 = (bf16[688,256]{1,0:T(8,128)(2,1)S(1)}, bf16[688,256]{1,0:T(8,128)(2,1)}, u32[]{:S(2)}, u32[]{:S(2)}) collective-permute-start(bf16[688,256]{1,0:T(8,128)(2,1)S(1)} %pack.1.refs_2_), channel_id=1, source_target_pairs={{0,8},{1,9},{2,10},{3,11},{4,12},{5,13},{6,14},{7,15},{8,0},{9,1},... | collective-permute-start | bytes 1056776 | tf_op jit(solution)/shard_map/ppermute | solution.py:349
  84.1 14.8 %collective-permute-start.16 = (bf16[688,256]{1,0:T(8,128)(2,1)S(1)}, bf16[688,256]{1,0:T(8,128)(2,1)}, u32[]{:S(2)}, u32[]{:S(2)}) collective-permute-start(bf16[688,256]{1,0:T(8,128)(2,1)S(1)} %pack.1.refs_2_), channel_id=1, source_target_pairs={{0,12},{1,13},{2,14},{3,15},{4,0},{5,1},{6,2},{7,3},{8,4},{9,5},{1... | collective-permute-start | bytes 1056776 | tf_op jit(solution)/shard_map/ppermute | solution.py:349
  86.4 12.6 %collective-permute-start.17 = (bf16[688,256]{1,0:T(8,128)(2,1)S(1)}, bf16[688,256]{1,0:T(8,128)(2,1)}, u32[]{:S(2)}, u32[]{:S(2)}) collective-permute-start(bf16[688,256]{1,0:T(8,128)(2,1)S(1)} %pack.1.refs_2_), channel_id=1, source_target_pairs={{0,3},{1,2},{2,1},{3,0},{4,7},{5,6},{6,5},{7,4},{8,11},{9,10},{10,... | collective-permute-start | bytes 1056776 | tf_op jit(solution)/shard_map/ppermute | solution.py:349
  89.1 10.6 %collective-permute-start.18 = (bf16[688,256]{1,0:T(8,128)(2,1)S(1)}, bf16[688,256]{1,0:T(8,128)(2,1)}, u32[]{:S(2)}, u32[]{:S(2)}) collective-permute-start(bf16[688,256]{1,0:T(8,128)(2,1)S(1)} %pack.1.refs_2_), channel_id=1, source_target_pairs={{0,1},{1,0},{2,3},{3,2},{4,5},{5,4},{6,7},{7,6},{8,9},{9,8},{10,11... | collective-permute-start | bytes 1056776 | tf_op jit(solution)/shard_map/ppermute | solution.py:349
  92.5 9.3 %collective-permute-start.19 = (bf16[688,256]{1,0:T(8,128)(2,1)S(1)}, bf16[688,256]{1,0:T(8,128)(2,1)}, u32[]{:S(2)}, u32[]{:S(2)}) collective-permute-start(bf16[688,256]{1,0:T(8,128)(2,1)S(1)} %pack.1.refs_2_), channel_id=1, source_target_pairs={{0,2},{1,3},{2,0},{3,1},{4,6},{5,7},{6,4},{7,5},{8,10},{9,11},{10,... | collective-permute-start | bytes 1056776 | tf_op jit(solution)/shard_map/ppermute | solution.py:349
  101.8 53.7 %collective-permute-start.20 = (bf16[1024,768]{1,0:T(8,128)(2,1)}, bf16[1024,768]{1,0:T(8,128)(2,1)}, u32[]{:S(2)}, u32[]{:S(2)}) collective-permute-start(bf16[1024,768]{1,0:T(8,128)(2,1)} %get-tuple-element.133), channel_id=1, source_target_pairs={{16,0},{17,1},{18,2},{19,3},{20,4},{21,5},{22,6},{23,7},{24,8},{25... | collective-permute-start | bytes 4718600 | tf_op jit(solution)/shard_map/ppermute | solution.py:413
  103.2 54.8 %collective-permute-start.21 = (bf16[1024,768]{1,0:T(8,128)(2,1)}, bf16[1024,768]{1,0:T(8,128)(2,1)}, u32[]{:S(2)}, u32[]{:S(2)}) collective-permute-start(bf16[1024,768]{1,0:T(8,128)(2,1)} %bitcast.7), channel_id=1, source_target_pairs={{16,0},{17,1},{18,2},{19,3},{20,4},{21,5},{22,6},{23,7},{24,8},{25... | collective-permute-start | bytes 4718600 | tf_op jit(solution)/shard_map/ppermute | solution.py:411
  106.6 21.7 %collective-permute-start = (bf16[2064,256]{1,0:T(8,128)(2,1)}, bf16[2064,256]{1,0:T(8,128)(2,1)}, u32[]{:S(2)}, u32[]{:S(2)}) collective-permute-start(bf16[2064,256]{1,0:T(8,128)(2,1)} %stack.2), channel_id=1, source_target_pairs={{0,3},{1,2},{2,1},{3,0},{4,7},{5,6},{6,5},{7,4},{8,11},{9,10},{10,... | collective-permute-start | bytes 3170312 | tf_op jit(solution)/shard_map/cond/branch_1_fun/ppermute | solution.py:349
  109.8 35.8 %collective-permute-start.1 = (bf16[2064,256]{1,0:T(8,128)(2,1)}, bf16[2064,256]{1,0:T(8,128)(2,1)}, u32[]{:S(2)}, u32[]{:S(2)}) collective-permute-start(bf16[2064,256]{1,0:T(8,128)(2,1)} %stack.2), channel_id=1, source_target_pairs={{0,1},{1,0},{2,3},{3,2},{4,5},{5,4},{6,7},{7,6},{8,9},{9,8},{10,11... | collective-permute-start | bytes 3170312 | tf_op jit(solution)/shard_map/cond/branch_1_fun/ppermute | solution.py:349
  113.1 33.1 %collective-permute-start.2 = (bf16[2064,256]{1,0:T(8,128)(2,1)}, bf16[2064,256]{1,0:T(8,128)(2,1)}, u32[]{:S(2)}, u32[]{:S(2)}) collective-permute-start(bf16[2064,256]{1,0:T(8,128)(2,1)} %stack.2), channel_id=1, source_target_pairs={{0,2},{1,3},{2,0},{3,1},{4,6},{5,7},{6,4},{7,5},{8,10},{9,11},{10,... | collective-permute-start | bytes 3170312 | tf_op jit(solution)/shard_map/cond/branch_1_fun/ppermute | solution.py:349
  (7 other events, 17.2 us)

commit v6 on v5

--- a/solution.py
+++ b/solution.py
@@ -266,15 +266,14 @@
 
     part = load(given, left)
     rights = [load(turning.at[h], right.at[h]) for h in halves]
-    part.wait()
-    rights[0].wait()
     projections = load(gathered, weights)
-    inner[halves[0], :] = dot_nn(right[halves[0], :], left[...]).astype(BF)
     gates = []
     for h in halves:
         gates += [load(active.at[h], act.at[h]), load(slope.at[h], slo.at[h]), load(incoming.at[h], base.at[h])]
-    rights[1].wait()
-    inner[halves[1], :] = dot_nn(right[halves[1], :], left[...]).astype(BF)
+    part.wait()
+    for c, h in zip(rights, halves):
+        c.wait()
+        inner[h, :] = dot_nn(right[h, :], left[...]).astype(BF)
     projections.wait()
     stores = [] if last else [factor_group(factor, tail[0], out, sem_out.at[4])]
     for c in stores:

time: 171 us -> 171 us (level)
  no operation moved by 1% of the time
where the time goes in v6:
time: 171 us; the launch traced here: 168 us
  blocking collectives  56.4 us (33%)
  starting transfers between devices  42.2 us (25%)
  waiting for transfers between devices  39.8 us (23%)
  Pallas kernels  27.5 us (16%)
    all_to_all x2, blocking collectives, exchanged(): return lax.all_to_all(x, 'seq', split_axis=0, concat_axis=0, tiled=True)  56.4 us
    ppermute x18, starting transfers between devices, sent(): return lax.ppermute(x, ('pipe', 'seq'), pairs)  38.1 us
    ppermute x18, waiting for transfers between devices, sent(): return lax.ppermute(x, ('pipe', 'seq'), pairs)  35.5 us
    pallas_call x2, Pallas kernels, layer(): pl.pallas_call(lambda *refs: layer_kernel(section, last, *refs), out_shap...  10.9 us
    pallas_call x2, Pallas kernels, forward(): pl.pallas_call(lambda *refs: forward_kernel(section, pieces, len(weights)...  7.99 us
  transfers between devices with their start and end apart: 22, of which 9 were waited for; matrix products, arithmetic and copies ran while one was open for 0% of the time, Pallas kernels for 10%

profile of v6, /device:TPU:12, one launch (start us, length us, event | category | flops | bytes accessed | tf_op | source)
XLA Modules:
  0.0 168.0 jit_solution(2750124385479311491)
XLA Ops:
  8.4 1.7 collective-permute-start.10
  13.4 2.3 %rows.1 = bf16[16,25,16,128]{3,2,1,0:T(8,128)(2,1)S(1)} custom-call(bf16[16,4,16,768]{3,2,1,0:T(8,128)(2,1)} %bitcast.6, bf16[1,1,16]{2,1,0:T(2,128)(2,1)} %copy-done.8), custom_call_target="tpu_custom_call" | custom-call | flops 1 | bytes 1 | tf_op jit(solution)/shard_map/rows/pallas_call | solution.py:89
  15.7 59.7 %conditional.3 = (bf16[1024,768]{1,0:T(8,128)(2,1)}) conditional(s32[]{:T(128)} %convert_element_type.8, () %tuple.30, bf16[16,25,16,128]{3,2,1,0:T(8,128)(2,1)S(1)} %rows.1), branch_computations={%region_0.0_spmd, %region_1.0_spmd} | conditional | flops 1 | bytes 6422537 | solution.py:384
  15.7 28.8 %all_to_all.16.left.x = bf16[16,25,16,128]{3,2,1,0:T(8,128)(2,1)} all-to-all(bf16[16,25,16,128]{3,2,1,0:T(8,128)(2,1)S(1)} %param.1), channel_id=1, replica_groups=mesh['pipe'=2,'seq'=16] {'seq'}, dimensions={0} | all-to-all | bytes 3276800 | tf_op jit(solution)/shard_map/cond/branch_1_fun/all_to_all | solution.py:360
  44.5 3.2 %mix.2 = bf16[16,64,768]{2,1,0:T(8,128)(2,1)} custom-call(bf16[16,25,16,128]{3,2,1,0:T(8,128)(2,1)} %all_to_all.16.left.x, bf16[16,25,16,128]{3,2,1,0:T(8,128)(2,1)} %all_to_all.16.left.x), custom_call_target="tpu_custom_call" | custom-call | flops 1 | bytes 1 | tf_op jit(solution)/shard_map/cond/branch_1_fun/mix/pallas_call | solution.py:118
  47.7 27.7 %all_to_all.17 = bf16[16,64,768]{2,1,0:T(8,128)(2,1)} all-to-all(bf16[16,64,768]{2,1,0:T(8,128)(2,1)} %mix.2), channel_id=1, replica_groups=mesh['pipe'=2,'seq'=16] {'seq'}, dimensions={0} | all-to-all | bytes 3145728 | tf_op jit(solution)/shard_map/cond/branch_1_fun/all_to_all | solution.py:360
  77.1 1.9 %collective-permute-start.14 = (bf16[688,256]{1,0:T(8,128)(2,1)S(1)}, bf16[688,256]{1,0:T(8,128)(2,1)S(1)}, u32[]{:S(2)}, u32[]{:S(2)}) collective-permute-start(bf16[688,256]{1,0:T(8,128)(2,1)S(1)} %pack.1.refs_2_), channel_id=1, source_target_pairs={{0,4},{1,5},{2,6},{3,7},{4,8},{5,9},{6,10},{7,11},{8,12},{9,13},{1... | collective-permute-start | bytes 1056776 | tf_op jit(solution)/shard_map/ppermute | solution.py:348
  79.0 5.0 %collective-permute-start.15 = (bf16[688,256]{1,0:T(8,128)(2,1)S(1)}, bf16[688,256]{1,0:T(8,128)(2,1)}, u32[]{:S(2)}, u32[]{:S(2)}) collective-permute-start(bf16[688,256]{1,0:T(8,128)(2,1)S(1)} %pack.1.refs_2_), channel_id=1, source_target_pairs={{0,8},{1,9},{2,10},{3,11},{4,12},{5,13},{6,14},{7,15},{8,0},{9,1},... | collective-permute-start | bytes 1056776 | tf_op jit(solution)/shard_map/ppermute | solution.py:348
  84.1 2.3 %collective-permute-start.16 = (bf16[688,256]{1,0:T(8,128)(2,1)S(1)}, bf16[688,256]{1,0:T(8,128)(2,1)}, u32[]{:S(2)}, u32[]{:S(2)}) collective-permute-start(bf16[688,256]{1,0:T(8,128)(2,1)S(1)} %pack.1.refs_2_), channel_id=1, source_target_pairs={{0,12},{1,13},{2,14},{3,15},{4,0},{5,1},{6,2},{7,3},{8,4},{9,5},{1... | collective-permute-start | bytes 1056776 | tf_op jit(solution)/shard_map/ppermute | solution.py:348
  86.4 2.7 %collective-permute-start.17 = (bf16[688,256]{1,0:T(8,128)(2,1)S(1)}, bf16[688,256]{1,0:T(8,128)(2,1)}, u32[]{:S(2)}, u32[]{:S(2)}) collective-permute-start(bf16[688,256]{1,0:T(8,128)(2,1)S(1)} %pack.1.refs_2_), channel_id=1, source_target_pairs={{0,3},{1,2},{2,1},{3,0},{4,7},{5,6},{6,5},{7,4},{8,11},{9,10},{10,... | collective-permute-start | bytes 1056776 | tf_op jit(solution)/shard_map/ppermute | solution.py:348
  89.1 3.4 %collective-permute-start.18 = (bf16[688,256]{1,0:T(8,128)(2,1)S(1)}, bf16[688,256]{1,0:T(8,128)(2,1)}, u32[]{:S(2)}, u32[]{:S(2)}) collective-permute-start(bf16[688,256]{1,0:T(8,128)(2,1)S(1)} %pack.1.refs_2_), channel_id=1, source_target_pairs={{0,1},{1,0},{2,3},{3,2},{4,5},{5,4},{6,7},{7,6},{8,9},{9,8},{10,11... | collective-permute-start | bytes 1056776 | tf_op jit(solution)/shard_map/ppermute | solution.py:348
  92.5 3.2 %collective-permute-start.19 = (bf16[688,256]{1,0:T(8,128)(2,1)S(1)}, bf16[688,256]{1,0:T(8,128)(2,1)}, u32[]{:S(2)}, u32[]{:S(2)}) collective-permute-start(bf16[688,256]{1,0:T(8,128)(2,1)S(1)} %pack.1.refs_2_), channel_id=1, source_target_pairs={{0,2},{1,3},{2,0},{3,1},{4,6},{5,7},{6,4},{7,5},{8,10},{9,11},{10,... | collective-permute-start | bytes 1056776 | tf_op jit(solution)/shard_map/ppermute | solution.py:348
  96.7 2.2 %collective-permute-done.16 = bf16[688,256]{1,0:T(8,128)(2,1)} collective-permute-done((bf16[688,256]{1,0:T(8,128)(2,1)S(1)}, bf16[688,256]{1,0:T(8,128)(2,1)}, u32[]{:S(2)}, u32[]{:S(2)}) %collective-permute-start.16) | collective-permute-done | bytes 352288 | tf_op jit(solution)/shard_map/ppermute | solution.py:348
  99.7 2.1 %collective-permute-done.19 = bf16[688,256]{1,0:T(8,128)(2,1)} collective-permute-done((bf16[688,256]{1,0:T(8,128)(2,1)S(1)}, bf16[688,256]{1,0:T(8,128)(2,1)}, u32[]{:S(2)}, u32[]{:S(2)}) %collective-permute-start.19) | collective-permute-done | bytes 352288 | tf_op jit(solution)/shard_map/ppermute | solution.py:348
  104.6 49.4 %conditional.5 = ((bf16[1024,768]{1,0:T(8,128)(2,1)}, bf16[1024,768]{1,0:T(8,128)(2,1)}, bf16[1024,1024]{1,0:T(8,128)(2,1)}, bf16[16,432,256]{2,1,0:T(8,128)(2,1)})) conditional(s32[]{:T(128)} %convert_element_type.8, () %tuple.37, (bf16[688,256]{1,0:T(8,128)(2,1)}, bf16[688,256]{1,0:T(8,128)(2,1)}, bf16[688,256]{1,0:T(8,128)(2,1)}, ...), branch_computations={%region_4.0_spmd, %region_5.0_spmd} | conditional | flops 2 | bytes 12681346 | solution.py:384
  104.6 2.0 %stack.2 = bf16[2064,256]{1,0:T(8,128)(2,1)} custom-call(bf16[688,256]{1,0:T(8,128)(2,1)} %get-tuple-element.34.refs_0_.refs_3_, bf16[688,256]{1,0:T(8,128)(2,1)} %get-tuple-element.35.refs_1_.refs_4_, bf16[688,256]{1,0:T(8,128)(2,1)} %get-tuple-element.36.refs_2_.refs_5_), custom_call_target="tpu_custom_call" | custom-call | flops 1 | bytes 1 | tf_op jit(solution)/shard_map/cond/branch_1_fun/stack/pallas_call | solution.py:154
  106.6 3.2 %collective-permute-start = (bf16[2064,256]{1,0:T(8,128)(2,1)}, bf16[2064,256]{1,0:T(8,128)(2,1)}, u32[]{:S(2)}, u32[]{:S(2)}) collective-permute-start(bf16[2064,256]{1,0:T(8,128)(2,1)} %stack.2), channel_id=1, source_target_pairs={{0,3},{1,2},{2,1},{3,0},{4,7},{5,6},{6,5},{7,4},{8,11},{9,10},{10,... | collective-permute-start | bytes 3170312 | tf_op jit(solution)/shard_map/cond/branch_1_fun/ppermute | solution.py:348
  109.8 3.4 %collective-permute-start.1 = (bf16[2064,256]{1,0:T(8,128)(2,1)}, bf16[2064,256]{1,0:T(8,128)(2,1)}, u32[]{:S(2)}, u32[]{:S(2)}) collective-permute-start(bf16[2064,256]{1,0:T(8,128)(2,1)} %stack.2), channel_id=1, source_target_pairs={{0,1},{1,0},{2,3},{3,2},{4,5},{5,4},{6,7},{7,6},{8,9},{9,8},{10,11... | collective-permute-start | bytes 3170312 | tf_op jit(solution)/shard_map/cond/branch_1_fun/ppermute | solution.py:348
  113.1 2.7 %collective-permute-start.2 = (bf16[2064,256]{1,0:T(8,128)(2,1)}, bf16[2064,256]{1,0:T(8,128)(2,1)}, u32[]{:S(2)}, u32[]{:S(2)}) collective-permute-start(bf16[2064,256]{1,0:T(8,128)(2,1)} %stack.2), channel_id=1, source_target_pairs={{0,2},{1,3},{2,0},{3,1},{4,6},{5,7},{6,4},{7,5},{8,10},{9,11},{10,... | collective-permute-start | bytes 3170312 | tf_op jit(solution)/shard_map/cond/branch_1_fun/ppermute | solution.py:348
  115.8 12.5 %collective-permute-done.refs_9_ = bf16[2064,256]{1,0:T(8,128)(2,1)} collective-permute-done((bf16[2064,256]{1,0:T(8,128)(2,1)}, bf16[2064,256]{1,0:T(8,128)(2,1)}, u32[]{:S(2)}, u32[]{:S(2)}) %collective-permute-start) | collective-permute-done | bytes 1056800 | tf_op jit(solution)/shard_map/cond/branch_1_fun/ppermute | solution.py:348
  128.3 17.3 %collective-permute-done.1.refs_10_ = bf16[2064,256]{1,0:T(8,128)(2,1)} collective-permute-done((bf16[2064,256]{1,0:T(8,128)(2,1)}, bf16[2064,256]{1,0:T(8,128)(2,1)}, u32[]{:S(2)}, u32[]{:S(2)}) %collective-permute-start.1) | collective-permute-done | bytes 1056800 | tf_op jit(solution)/shard_map/cond/branch_1_fun/ppermute | solution.py:348
  146.2 7.7 %forward.2 = (bf16[1024,768]{1,0:T(8,128)(2,1)}, bf16[1024,768]{1,0:T(8,128)(2,1)}, bf16[1024,1024]{1,0:T(8,128)(2,1)}, bf16[16,432,256]{2,1,0:T(8,128)(2,1)}) custom-call(bf16[1,1024,768]{2,1,0:T(8,128)(2,1)S(1)} %get-tuple-element.31.refs_0_, f32[1,1024]{1,0:T(1,128)S(1)} %get-tuple-element.32.refs_1_, bf16[688,256]{1,0:T(8,128)(2,1)S(1)} %get-tuple-element.33.refs_2_, ...), custom_call_target="tpu_custom_call" | custom-call | flops 1 | bytes 1 | tf_op jit(solution)/shard_map/cond/branch_1_fun/forward/pallas_call | solution.py:239
  155.6 2.5 %collective-permute-done.21.refs_5_ = bf16[1024,768]{1,0:T(8,128)(2,1)} collective-permute-done((bf16[1024,768]{1,0:T(8,128)(2,1)}, bf16[1024,768]{1,0:T(8,128)(2,1)}, u32[]{:S(2)}, u32[]{:S(2)}) %collective-permute-start.21) | collective-permute-done | bytes 1572896 | tf_op jit(solution)/shard_map/ppermute | solution.py:410
  158.0 9.9 %layer.3 = bf16[16,4,16,768]{3,2,1,0:T(8,128)(2,1)} custom-call(bf16[1024,768]{1,0:T(8,128)(2,1)} %collective-permute-done.20.refs_0_, bf16[1024,768]{1,0:T(8,128)(2,1)} %get-tuple-element.119.refs_1_, bf16[1024,768]{1,0:T(8,128)(2,1)} %get-tuple-element.120.refs_2_, bf16[1024,1024]{1,0:T(8,128)(2,1)} %get-tuple-element.121.refs_3_, ...), custom_call_target="tpu_custom_call" | custom-call | flops 1 | bytes 1 | tf_op jit(solution)/shard_map/layer/pallas_call | solution.py:331
  (53 shorter events, 20.1 us)
Async XLA Ops:
  0.0 1.3 collective-permute-start.3
  1.3 12.1 %copy-start.8 = (bf16[1,1,16]{2,1,0:T(2,128)(2,1)}, bf16[1,1,16]{2,1,0:T(2,128)(2,1)S(1)}, u32[]{:S(2)}) copy-start(bf16[1,1,16]{2,1,0:T(2,128)(2,1)S(1)} %collective-permute-done.3.refs_1_.refs_6_) | copy-start | bytes 100
  1.3 4.2 %collective-permute-start.4 = (bf16[688,256]{1,0:T(8,128)(2,1)S(1)}, bf16[688,256]{1,0:T(8,128)(2,1)S(1)}, u32[]{:S(2)}, u32[]{:S(2)}) collective-permute-start(bf16[688,256]{1,0:T(8,128)(2,1)S(1)} %pack.1.refs_2_), channel_id=1, source_target_pairs={{16,20},{17,21},{18,22},{19,23},{20,24},{21,25},{22,26},{23,27},{2... | collective-permute-start | bytes 1056776 | tf_op jit(solution)/shard_map/ppermute | solution.py:348
  1.9 4.9 %collective-permute-start.5 = (bf16[688,256]{1,0:T(8,128)(2,1)S(1)}, bf16[688,256]{1,0:T(8,128)(2,1)S(1)}, u32[]{:S(2)}, u32[]{:S(2)}) collective-permute-start(bf16[688,256]{1,0:T(8,128)(2,1)S(1)} %pack.1.refs_2_), channel_id=1, source_target_pairs={{16,24},{17,25},{18,26},{19,27},{20,28},{21,29},{22,30},{23,31},{2... | collective-permute-start | bytes 1056776 | tf_op jit(solution)/shard_map/ppermute | solution.py:348
  2.6 4.2 %collective-permute-start.6 = (bf16[688,256]{1,0:T(8,128)(2,1)S(1)}, bf16[688,256]{1,0:T(8,128)(2,1)S(1)}, u32[]{:S(2)}, u32[]{:S(2)}) collective-permute-start(bf16[688,256]{1,0:T(8,128)(2,1)S(1)} %pack.1.refs_2_), channel_id=1, source_target_pairs={{16,28},{17,29},{18,30},{19,31},{20,16},{21,17},{22,18},{23,19},{2... | collective-permute-start | bytes 1056776 | tf_op jit(solution)/shard_map/ppermute | solution.py:348
  3.3 5.0 %collective-permute-start.7 = (bf16[688,256]{1,0:T(8,128)(2,1)S(1)}, bf16[688,256]{1,0:T(8,128)(2,1)S(1)}, u32[]{:S(2)}, u32[]{:S(2)}) collective-permute-start(bf16[688,256]{1,0:T(8,128)(2,1)S(1)} %pack.1.refs_2_), channel_id=1, source_target_pairs={{16,19},{17,18},{18,17},{19,16},{20,23},{21,22},{22,21},{23,20},{2... | collective-permute-start | bytes 1056776 | tf_op jit(solution)/shard_map/ppermute | solution.py:348
  4.0 4.4 %collective-permute-start.8 = (bf16[688,256]{1,0:T(8,128)(2,1)S(1)}, bf16[688,256]{1,0:T(8,128)(2,1)}, u32[]{:S(2)}, u32[]{:S(2)}) collective-permute-start(bf16[688,256]{1,0:T(8,128)(2,1)S(1)} %pack.1.refs_2_), channel_id=1, source_target_pairs={{16,17},{17,16},{18,19},{19,18},{20,21},{21,20},{22,23},{23,22},{2... | collective-permute-start | bytes 1056776 | tf_op jit(solution)/shard_map/ppermute | solution.py:348
  5.4 3.0 %collective-permute-start.9 = (bf16[688,256]{1,0:T(8,128)(2,1)S(1)}, bf16[688,256]{1,0:T(8,128)(2,1)}, u32[]{:S(2)}, u32[]{:S(2)}) collective-permute-start(bf16[688,256]{1,0:T(8,128)(2,1)S(1)} %pack.1.refs_2_), channel_id=1, source_target_pairs={{16,18},{17,19},{18,16},{19,17},{20,22},{21,23},{22,20},{23,21},{2... | collective-permute-start | bytes 1056776 | tf_op jit(solution)/shard_map/ppermute | solution.py:348
  8.4 67.0 %collective-permute-start.10 = (bf16[2064,256]{1,0:T(8,128)(2,1)}, bf16[2064,256]{1,0:T(8,128)(2,1)}, u32[]{:S(2)}, u32[]{:S(2)}) collective-permute-start(bf16[2064,256]{1,0:T(8,128)(2,1)} %stack.3), channel_id=1, source_target_pairs={{16,19},{17,18},{18,17},{19,16},{20,23},{21,22},{22,21},{23,20},{2... | collective-permute-start | bytes 3170312 | tf_op jit(solution)/shard_map/ppermute | solution.py:348
  10.1 65.3 %collective-permute-start.11 = (bf16[2064,256]{1,0:T(8,128)(2,1)}, bf16[2064,256]{1,0:T(8,128)(2,1)}, u32[]{:S(2)}, u32[]{:S(2)}) collective-permute-start(bf16[2064,256]{1,0:T(8,128)(2,1)} %stack.3), channel_id=1, source_target_pairs={{16,17},{17,16},{18,19},{19,18},{20,21},{21,20},{22,23},{23,22},{2... | collective-permute-start | bytes 3170312 | tf_op jit(solution)/shard_map/ppermute | solution.py:348
  11.7 63.7 %collective-permute-start.12 = (bf16[2064,256]{1,0:T(8,128)(2,1)}, bf16[2064,256]{1,0:T(8,128)(2,1)}, u32[]{:S(2)}, u32[]{:S(2)}) collective-permute-start(bf16[2064,256]{1,0:T(8,128)(2,1)} %stack.3), channel_id=1, source_target_pairs={{16,18},{17,19},{18,16},{19,17},{20,22},{21,23},{22,20},{23,21},{2... | collective-permute-start | bytes 3170312 | tf_op jit(solution)/shard_map/ppermute | solution.py:348
  15.7 59.7 %copy-start.7 = (f32[1,1,1024]{2,1,0:T(1,128)S(1)}, f32[1,1,1024]{2,1,0:T(1,128)}, u32[]{:S(2)}) copy-start(f32[1,1,1024]{2,1,0:T(1,128)} %param.21) | copy-start | bytes 12292
  75.7 16.7 %collective-permute-start.13 = (bf16[1024,768]{1,0:T(8,128)(2,1)}, bf16[1024,768]{1,0:T(8,128)(2,1)S(1)}, u32[]{:S(2)}, u32[]{:S(2)}) collective-permute-start(bf16[1024,768]{1,0:T(8,128)(2,1)} %get-tuple-element.132), channel_id=1, source_target_pairs={{0,16},{1,17},{2,18},{3,19},{4,20},{5,21},{6,22},{7,23},{8,24},{9,... | collective-permute-start | bytes 4718600 | tf_op jit(solution)/shard_map/ppermute | solution.py:403
  77.1 11.9 %collective-permute-start.14 = (bf16[688,256]{1,0:T(8,128)(2,1)S(1)}, bf16[688,256]{1,0:T(8,128)(2,1)S(1)}, u32[]{:S(2)}, u32[]{:S(2)}) collective-permute-start(bf16[688,256]{1,0:T(8,128)(2,1)S(1)} %pack.1.refs_2_), channel_id=1, source_target_pairs={{0,4},{1,5},{2,6},{3,7},{4,8},{5,9},{6,10},{7,11},{8,12},{9,13},{1... | collective-permute-start | bytes 1056776 | tf_op jit(solution)/shard_map/ppermute | solution.py:348
  79.0 17.7 %collective-permute-start.15 = (bf16[688,256]{1,0:T(8,128)(2,1)S(1)}, bf16[688,256]{1,0:T(8,128)(2,1)}, u32[]{:S(2)}, u32[]{:S(2)}) collective-permute-start(bf16[688,256]{1,0:T(8,128)(2,1)S(1)} %pack.1.refs_2_), channel_id=1, source_target_pairs={{0,8},{1,9},{2,10},{3,11},{4,12},{5,13},{6,14},{7,15},{8,0},{9,1},... | collective-permute-start | bytes 1056776 | tf_op jit(solution)/shard_map/ppermute | solution.py:348
  84.1 14.8 %collective-permute-start.16 = (bf16[688,256]{1,0:T(8,128)(2,1)S(1)}, bf16[688,256]{1,0:T(8,128)(2,1)}, u32[]{:S(2)}, u32[]{:S(2)}) collective-permute-start(bf16[688,256]{1,0:T(8,128)(2,1)S(1)} %pack.1.refs_2_), channel_id=1, source_target_pairs={{0,12},{1,13},{2,14},{3,15},{4,0},{5,1},{6,2},{7,3},{8,4},{9,5},{1... | collective-permute-start | bytes 1056776 | tf_op jit(solution)/shard_map/ppermute | solution.py:348
  86.4 12.6 %collective-permute-start.17 = (bf16[688,256]{1,0:T(8,128)(2,1)S(1)}, bf16[688,256]{1,0:T(8,128)(2,1)}, u32[]{:S(2)}, u32[]{:S(2)}) collective-permute-start(bf16[688,256]{1,0:T(8,128)(2,1)S(1)} %pack.1.refs_2_), channel_id=1, source_target_pairs={{0,3},{1,2},{2,1},{3,0},{4,7},{5,6},{6,5},{7,4},{8,11},{9,10},{10,... | collective-permute-start | bytes 1056776 | tf_op jit(solution)/shard_map/ppermute | solution.py:348
  89.1 10.6 %collective-permute-start.18 = (bf16[688,256]{1,0:T(8,128)(2,1)S(1)}, bf16[688,256]{1,0:T(8,128)(2,1)}, u32[]{:S(2)}, u32[]{:S(2)}) collective-permute-start(bf16[688,256]{1,0:T(8,128)(2,1)S(1)} %pack.1.refs_2_), channel_id=1, source_target_pairs={{0,1},{1,0},{2,3},{3,2},{4,5},{5,4},{6,7},{7,6},{8,9},{9,8},{10,11... | collective-permute-start | bytes 1056776 | tf_op jit(solution)/shard_map/ppermute | solution.py:348
  92.5 9.3 %collective-permute-start.19 = (bf16[688,256]{1,0:T(8,128)(2,1)S(1)}, bf16[688,256]{1,0:T(8,128)(2,1)}, u32[]{:S(2)}, u32[]{:S(2)}) collective-permute-start(bf16[688,256]{1,0:T(8,128)(2,1)S(1)} %pack.1.refs_2_), channel_id=1, source_target_pairs={{0,2},{1,3},{2,0},{3,1},{4,6},{5,7},{6,4},{7,5},{8,10},{9,11},{10,... | collective-permute-start | bytes 1056776 | tf_op jit(solution)/shard_map/ppermute | solution.py:348
  101.8 53.7 %collective-permute-start.20 = (bf16[1024,768]{1,0:T(8,128)(2,1)}, bf16[1024,768]{1,0:T(8,128)(2,1)}, u32[]{:S(2)}, u32[]{:S(2)}) collective-permute-start(bf16[1024,768]{1,0:T(8,128)(2,1)} %get-tuple-element.133), channel_id=1, source_target_pairs={{16,0},{17,1},{18,2},{19,3},{20,4},{21,5},{22,6},{23,7},{24,8},{25... | collective-permute-start | bytes 4718600 | tf_op jit(solution)/shard_map/ppermute | solution.py:412
  103.2 54.8 %collective-permute-start.21 = (bf16[1024,768]{1,0:T(8,128)(2,1)}, bf16[1024,768]{1,0:T(8,128)(2,1)}, u32[]{:S(2)}, u32[]{:S(2)}) collective-permute-start(bf16[1024,768]{1,0:T(8,128)(2,1)} %bitcast.7), channel_id=1, source_target_pairs={{16,0},{17,1},{18,2},{19,3},{20,4},{21,5},{22,6},{23,7},{24,8},{25... | collective-permute-start | bytes 4718600 | tf_op jit(solution)/shard_map/ppermute | solution.py:410
  106.6 21.7 %collective-permute-start = (bf16[2064,256]{1,0:T(8,128)(2,1)}, bf16[2064,256]{1,0:T(8,128)(2,1)}, u32[]{:S(2)}, u32[]{:S(2)}) collective-permute-start(bf16[2064,256]{1,0:T(8,128)(2,1)} %stack.2), channel_id=1, source_target_pairs={{0,3},{1,2},{2,1},{3,0},{4,7},{5,6},{6,5},{7,4},{8,11},{9,10},{10,... | collective-permute-start | bytes 3170312 | tf_op jit(solution)/shard_map/cond/branch_1_fun/ppermute | solution.py:348
  109.8 35.8 %collective-permute-start.1 = (bf16[2064,256]{1,0:T(8,128)(2,1)}, bf16[2064,256]{1,0:T(8,128)(2,1)}, u32[]{:S(2)}, u32[]{:S(2)}) collective-permute-start(bf16[2064,256]{1,0:T(8,128)(2,1)} %stack.2), channel_id=1, source_target_pairs={{0,1},{1,0},{2,3},{3,2},{4,5},{5,4},{6,7},{7,6},{8,9},{9,8},{10,11... | collective-permute-start | bytes 3170312 | tf_op jit(solution)/shard_map/cond/branch_1_fun/ppermute | solution.py:348
  113.1 33.1 %collective-permute-start.2 = (bf16[2064,256]{1,0:T(8,128)(2,1)}, bf16[2064,256]{1,0:T(8,128)(2,1)}, u32[]{:S(2)}, u32[]{:S(2)}) collective-permute-start(bf16[2064,256]{1,0:T(8,128)(2,1)} %stack.2), channel_id=1, source_target_pairs={{0,2},{1,3},{2,0},{3,1},{4,6},{5,7},{6,4},{7,5},{8,10},{9,11},{10,... | collective-permute-start | bytes 3170312 | tf_op jit(solution)/shard_map/cond/branch_1_fun/ppermute | solution.py:348
  (7 other events, 17.2 us)
